TPU v7x, 32 devices: a whole 2x2x4 slice. The times are simulated.
32 devices in a mesh: dp: 4 (over y, x), ctx: 8 (over z, core).
Axes of the slice: x: 2, y: 2, z: 4, core: 2. Of those that a mesh axis runs over, the one named last changes fastest.
Arguments:
- layer_input: bfloat16 [2, 4, 1024, 2048], P(None, 'dp', 'ctx'), may hold values from -6 to 6
- out_grad: bfloat16 [2, 4, 1024, 2048], P(None, 'dp', 'ctx'), may hold values from -6 to 6
- prefix_len: int32 [2, 4], P(None, 'dp'), may hold values from 102 to 512
- qkv_weight: bfloat16 [2048, 6144], P(('dp', 'ctx')), may hold values from -0.125 to 0.125
- qkv_bias: bfloat16 [6144], P(('dp', 'ctx')), may hold values from -3 to 3
- dense_weight: bfloat16 [2048, 2048], P(('dp', 'ctx')), may hold values from -1.5 to 1.5
- dense_bias: bfloat16 [2048], P(('dp', 'ctx')), may hold values from -3 to 3
- expand_weight: bfloat16 [2048, 8192], P(('dp', 'ctx')), may hold values from -0.125 to 0.125
- expand_bias: bfloat16 [8192], P(('dp', 'ctx')), may hold values from -3 to 3
- shrink_weight: bfloat16 [8192, 2048], P(('dp', 'ctx')), may hold values from -0.0625 to 0.0625
- shrink_bias: bfloat16 [2048], P(('dp', 'ctx')), may hold values from -3 to 3
- attn_gain: bfloat16 [2048], P(('dp', 'ctx')), may hold values from 0.099609375 to 1.8984375
- attn_shift: bfloat16 [2048], P(('dp', 'ctx')), may hold values from -2 to 2
- mlp_gain: bfloat16 [2048], P(('dp', 'ctx')), may hold values from 0.099609375 to 1.8984375
- mlp_shift: bfloat16 [2048], P(('dp', 'ctx')), may hold values from -2 to 2
Outputs:
- layer_output: bfloat16 [2, 4, 1024, 2048], P(None, 'dp', 'ctx')
- input_grad: bfloat16 [2, 4, 1024, 2048], P(None, 'dp', 'ctx')
- qkv_weight_grad: float32 [2048, 6144], P(('dp', 'ctx'))
- qkv_bias_grad: float32 [4096], P(('dp', 'ctx'))
- value_bias_grad: float32 [2048], P(('dp', 'ctx'))
- dense_weight_grad: float32 [2048, 2048], P(('dp', 'ctx'))
- dense_bias_grad: float32 [2048], P(('dp', 'ctx'))
- expand_weight_grad: float32 [2048, 8192], P(('dp', 'ctx'))
- expand_bias_grad: float32 [8192], P(('dp', 'ctx'))
- shrink_weight_grad: float32 [8192, 2048], P(('dp', 'ctx'))
- shrink_bias_grad: float32 [2048], P(('dp', 'ctx'))
- attn_gain_grad: float32 [2048], P(('dp', 'ctx'))
- attn_shift_grad: float32 [2048], P(('dp', 'ctx'))
- mlp_gain_grad: float32 [2048], P(('dp', 'ctx'))
- mlp_shift_grad: float32 [2048], P(('dp', 'ctx'))
All inputs are finite; a program needn't handle non-finite values.
Results may differ from a plain program's by a relative error of at most 0.011.
Values may be sent and summed in bfloat16 or wider, within the bound.
A program may use at most 704 MiB of HBM per device.

v0:
```python
import math

import jax
import jax.numpy as jnp
from jax import lax
from jax.sharding import PartitionSpec as P

HEADS = 8
HEAD = 256
ROT = 64
SEQ = 1024


def norm_rows(inputs, norm_gain, norm_bias):
    row_mean = jnp.mean(inputs, axis=-1, keepdims=True)
    centered = inputs - row_mean
    variance = jnp.mean(centered * centered, axis=-1, keepdims=True)
    return centered * lax.rsqrt(variance + 1e-05) * norm_gain + norm_bias


def gelu_exact(values):
    return jax.nn.gelu(values, approximate=False)


def rope_tables(positions):
    freqs = jnp.exp(jnp.arange(ROT // 2, dtype=jnp.float32) * (-2.0 * math.log(10000.0) / ROT))
    angles = positions[:, None] * freqs[None, :]
    return (jnp.cos(angles), jnp.sin(angles))


def rotate(heads, cos_table, sin_table):
    half_rot = ROT // 2
    lower = heads[..., :half_rot]
    upper = heads[..., half_rot:ROT]
    cos_wide = cos_table[:, None, :]
    sin_wide = sin_table[:, None, :]
    return jnp.concatenate(
        [
            lower * cos_wide - upper * sin_wide,
            upper * cos_wide + lower * sin_wide,
            heads[..., ROT:],
        ],
        axis=-1,
    )


def unpack_small(packed, lengths, devices):
    table_rows = packed.reshape(devices, -1)
    members = []
    offset = 0
    for length in lengths:
        members.append(table_rows[:, offset : offset + length].reshape(-1).astype(jnp.float32))
        offset = offset + length
    return members


def contract_rows(left_mat, right_mat):
    return lax.dot_general(
        left_mat, right_mat, (((0,), (0,)), ((), ())), preferred_element_type=jnp.float32
    )


def contract_cols(left_mat, right_mat):
    return lax.dot_general(
        left_mat, right_mat, (((1,), (1,)), ((), ())), preferred_element_type=jnp.float32
    )


def shards(
    layer_input,
    out_grad,
    prefix_len,
    qkv_weight,
    qkv_bias,
    dense_weight,
    dense_bias,
    expand_weight,
    expand_bias,
    shrink_weight,
    shrink_bias,
    attn_gain,
    attn_shift,
    mlp_gain,
    mlp_shift,
):
    devices = lax.axis_size("dp") * lax.axis_size("ctx")
    ctx_index = lax.axis_index("ctx")
    micro, seq_count, span, width = layer_input.shape
    sequences = micro * seq_count
    rows = sequences * span
    heads_shape = (sequences, span, HEADS, HEAD)
    scale = 1.0 / math.sqrt(HEAD)
    attn_lengths = (attn_gain.shape[0], attn_shift.shape[0], qkv_bias.shape[0], dense_bias.shape[0])
    mlp_lengths = (
        mlp_gain.shape[0],
        mlp_shift.shape[0],
        expand_bias.shape[0],
        shrink_bias.shape[0],
    )
    attn_packed = jnp.concatenate([attn_gain, attn_shift, qkv_bias, dense_bias])
    mlp_packed = jnp.concatenate([mlp_gain, mlp_shift, expand_bias, shrink_bias])

    def fetch_attn():
        return (
            lax.all_gather(qkv_weight, ("dp", "ctx"), axis=0, tiled=True),
            lax.all_gather(dense_weight, ("dp", "ctx"), axis=0, tiled=True),
            lax.all_gather(attn_packed, ("dp", "ctx"), axis=0, tiled=True),
        )

    def fetch_mlp():
        return (
            lax.all_gather(expand_weight, ("dp", "ctx"), axis=0, tiled=True),
            lax.all_gather(shrink_weight, ("dp", "ctx"), axis=0, tiled=True),
            lax.all_gather(mlp_packed, ("dp", "ctx"), axis=0, tiled=True),
        )

    local_pos = ctx_index * span + jnp.arange(span, dtype=jnp.int32)
    cos_table, sin_table = rope_tables(local_pos.astype(jnp.float32))
    key_pos = jnp.arange(SEQ, dtype=jnp.int32)
    causal = key_pos[None, :] <= local_pos[:, None]
    inputs = layer_input.astype(jnp.float32).reshape(rows, width)
    cot_rows = out_grad.reshape(rows, width)
    cot_float = cot_rows.astype(jnp.float32)
    prefix = prefix_len.reshape(sequences)
    allowed = (causal[None] | (key_pos[None, None, :] < prefix[:, None, None]))[:, None]
    attn_set = fetch_attn()
    qkv_full, dense_full, attn_small = attn_set
    gain_attn, shift_attn, joined_shift, dense_shift = unpack_small(
        attn_small, attn_lengths, devices
    )
    hidden_attn = norm_rows(inputs, gain_attn, shift_attn).astype(jnp.bfloat16)
    joined = jnp.dot(hidden_attn, qkv_full, preferred_element_type=jnp.float32) + joined_shift
    queries = rotate(joined[:, :width].reshape(heads_shape), cos_table, sin_table).astype(
        jnp.bfloat16
    )
    key_rows = rotate(
        joined[:, width : 2 * width].reshape(heads_shape), cos_table, sin_table
    ).astype(jnp.bfloat16)
    value_rows = joined[:, 2 * width :].reshape(heads_shape).astype(jnp.bfloat16)
    all_keys, all_values = (
        lax.all_gather(key_rows, "ctx", axis=1, tiled=True),
        lax.all_gather(value_rows, "ctx", axis=1, tiled=True),
    )
    scores = (
        jnp.einsum("sqhe,skhe->shqk", queries, all_keys, preferred_element_type=jnp.float32) * scale
    )
    scores = jnp.where(allowed, scores, -1e30)
    row_max = jnp.max(scores, axis=-1, keepdims=True)
    expo = jnp.exp(scores - row_max)
    row_total = jnp.sum(expo, axis=-1, keepdims=True)
    log_total = row_max + jnp.log(row_total)
    probs_low = (expo / row_total).astype(jnp.bfloat16)
    mixed = jnp.einsum("shqk,skhe->sqhe", probs_low, all_values, preferred_element_type=jnp.float32)
    mixed = mixed.reshape(rows, width).astype(jnp.bfloat16)
    attn_out = jnp.dot(mixed, dense_full, preferred_element_type=jnp.float32) + dense_shift
    mlp_set = fetch_mlp()
    expand_full, shrink_full, mlp_small = mlp_set
    gain_mlp, shift_mlp, expand_shift, shrink_shift = unpack_small(mlp_small, mlp_lengths, devices)
    hidden_mlp = norm_rows(inputs, gain_mlp, shift_mlp).astype(jnp.bfloat16)
    expanded = jnp.dot(hidden_mlp, expand_full, preferred_element_type=jnp.float32) + expand_shift
    activated = gelu_exact(expanded).astype(jnp.bfloat16)
    mlp_out = jnp.dot(activated, shrink_full, preferred_element_type=jnp.float32) + shrink_shift
    layer_output = (
        (inputs + attn_out + mlp_out).astype(jnp.bfloat16).reshape(micro, seq_count, span, width)
    )
    attn_back_set = fetch_attn()
    qkv_back, dense_back, attn_small_back = attn_back_set
    gain_attn, shift_attn, joined_shift, dense_shift = unpack_small(
        attn_small_back, attn_lengths, devices
    )
    grad_out_shift = jnp.sum(cot_float, axis=0)
    grad_mixed = contract_cols(cot_rows, dense_back).astype(jnp.bfloat16).reshape(heads_shape)
    again = (
        jnp.einsum("sqhe,skhe->shqk", queries, all_keys, preferred_element_type=jnp.float32) * scale
    )
    again = jnp.where(allowed, again, -1e30)
    probs = jnp.exp(again - log_total)
    grad_probs = jnp.einsum(
        "sqhe,skhe->shqk", grad_mixed, all_values, preferred_element_type=jnp.float32
    )
    delta = jnp.sum(probs * grad_probs, axis=-1, keepdims=True)
    grad_scores = (probs * (grad_probs - delta)).astype(jnp.bfloat16)
    grad_queries = (
        jnp.einsum("shqk,skhe->sqhe", grad_scores, all_keys, preferred_element_type=jnp.float32)
        * scale
    )
    all_queries, all_grad_mixed = (
        lax.all_gather(queries, "ctx", axis=1, tiled=True),
        lax.all_gather(grad_mixed, "ctx", axis=1, tiled=True),
    )
    stat_lse = jnp.transpose(log_total[..., 0], (0, 2, 1))
    stat_delta = jnp.transpose(delta[..., 0], (0, 2, 1))
    lse_all, delta_all = (
        lax.all_gather(stat_lse, "ctx", axis=1, tiled=True),
        lax.all_gather(stat_delta, "ctx", axis=1, tiled=True),
    )
    lse_all = jnp.transpose(lse_all, (0, 2, 1))[..., None]
    delta_all = jnp.transpose(delta_all, (0, 2, 1))[..., None]
    key_allowed = (local_pos[None, :] <= key_pos[:, None])[None] | (
        local_pos[None, None, :] < prefix[:, None, None]
    )
    block_scores = (
        jnp.einsum("sqhe,skhe->shqk", all_queries, key_rows, preferred_element_type=jnp.float32)
        * scale
    )
    block_scores = jnp.where(key_allowed[:, None], block_scores, -1e30)
    block_probs = jnp.exp(block_scores - lse_all)
    block_grad_probs = jnp.einsum(
        "sqhe,skhe->shqk", all_grad_mixed, value_rows, preferred_element_type=jnp.float32
    )
    block_grad_scores = (block_probs * (block_grad_probs - delta_all)).astype(jnp.bfloat16)
    own_keys = (
        jnp.einsum(
            "shqk,sqhe->skhe", block_grad_scores, all_queries, preferred_element_type=jnp.float32
        )
        * scale
    )
    own_values = jnp.einsum(
        "shqk,sqhe->skhe",
        block_probs.astype(jnp.bfloat16),
        all_grad_mixed,
        preferred_element_type=jnp.float32,
    )
    grad_joined = jnp.concatenate(
        [
            rotate(grad_queries, cos_table, -sin_table).reshape(rows, width),
            rotate(own_keys, cos_table, -sin_table).reshape(rows, width),
            own_values.reshape(rows, width),
        ],
        axis=1,
    ).astype(jnp.bfloat16)
    grad_joined_shift = jnp.sum(grad_joined.astype(jnp.float32), axis=0)
    grad_hidden_attn = contract_cols(grad_joined, qkv_back)
    unused_attn, attn_back = jax.vjp(norm_rows, inputs, gain_attn, shift_attn)
    grad_in_attn, grad_gain_attn, grad_shift_attn = attn_back(grad_hidden_attn)
    attn_columns = jnp.concatenate(
        [
            grad_gain_attn[:, None],
            grad_shift_attn[:, None],
            grad_joined_shift[: 2 * width].reshape(width, 2),
            grad_joined_shift[2 * width :][:, None],
            grad_out_shift[:, None],
        ],
        axis=1,
    )
    hidden_part = hidden_attn
    small_part = attn_columns
    attn_grads = lax.psum_scatter(
        jnp.concatenate(
            [contract_rows(hidden_part, grad_joined), contract_rows(mixed, cot_rows), small_part],
            axis=1,
        ),
        ("dp", "ctx"),
        scatter_dimension=0,
        tiled=True,
    )
    qkv_grad = attn_grads[:, : 3 * width]
    dense_grad = attn_grads[:, 3 * width : 4 * width]
    attn_tail = attn_grads[:, 4 * width :]
    mlp_back_set = fetch_mlp()
    expand_back, shrink_back, mlp_small_back = mlp_back_set
    gain_mlp, shift_mlp, expand_shift, shrink_shift = unpack_small(
        mlp_small_back, mlp_lengths, devices
    )
    unused_gelu, gelu_back = jax.vjp(gelu_exact, expanded)
    grad_act = contract_cols(cot_rows, shrink_back)
    grad_expanded = gelu_back(grad_act)[0].astype(jnp.bfloat16)
    grad_expand_shift = jnp.sum(grad_expanded.astype(jnp.float32), axis=0)
    grad_hidden_mlp = contract_cols(grad_expanded, expand_back)
    unused_mlp, mlp_back = jax.vjp(norm_rows, inputs, gain_mlp, shift_mlp)
    grad_in_mlp, grad_gain_mlp, grad_shift_mlp = mlp_back(grad_hidden_mlp)
    ratio = expand_shift.shape[0] // width
    mlp_columns = jnp.concatenate(
        [
            grad_gain_mlp[:, None],
            grad_shift_mlp[:, None],
            grad_expand_shift.reshape(width, ratio),
            grad_out_shift[:, None],
        ],
        axis=1,
    )
    ff_width = expand_back.shape[1]
    hidden_part = hidden_mlp
    small_part = mlp_columns
    expand_grads = lax.psum_scatter(
        jnp.concatenate([contract_rows(hidden_part, grad_expanded), small_part], axis=1),
        ("dp", "ctx"),
        scatter_dimension=0,
        tiled=True,
    )
    shrink_grad = lax.psum_scatter(
        contract_rows(activated, cot_rows), ("dp", "ctx"), scatter_dimension=0, tiled=True
    )
    expand_grad = expand_grads[:, :ff_width]
    mlp_tail = expand_grads[:, ff_width:]
    input_grad = (
        (cot_float + grad_in_attn + grad_in_mlp)
        .astype(jnp.bfloat16)
        .reshape(micro, seq_count, span, width)
    )
    return (
        layer_output,
        input_grad,
        qkv_grad,
        attn_tail[:, 2:4].reshape(-1),
        attn_tail[:, 4],
        dense_grad,
        attn_tail[:, 5],
        expand_grad,
        mlp_tail[:, 2 : 2 + ratio].reshape(-1),
        shrink_grad,
        mlp_tail[:, 2 + ratio],
        attn_tail[:, 0],
        attn_tail[:, 1],
        mlp_tail[:, 0],
        mlp_tail[:, 1],
    )


def solution(mesh):
    placed = (
        P(None, "dp", "ctx", None),
        P(None, "dp", "ctx", None),
        P(None, "dp"),
        P(("dp", "ctx"), None),
        P(("dp", "ctx")),
        P(("dp", "ctx"), None),
        P(("dp", "ctx")),
        P(("dp", "ctx"), None),
        P(("dp", "ctx")),
        P(("dp", "ctx"), None),
        P(("dp", "ctx")),
        P(("dp", "ctx")),
        P(("dp", "ctx")),
        P(("dp", "ctx")),
        P(("dp", "ctx")),
    )
    return jax.shard_map(
        shards,
        mesh=mesh,
        in_specs=placed,
        out_specs=(
            P(None, "dp", "ctx", None),
            P(None, "dp", "ctx", None),
            P(("dp", "ctx"), None),
            P(("dp", "ctx")),
            P(("dp", "ctx")),
            P(("dp", "ctx"), None),
            P(("dp", "ctx")),
            P(("dp", "ctx"), None),
            P(("dp", "ctx")),
            P(("dp", "ctx"), None),
            P(("dp", "ctx")),
            P(("dp", "ctx")),
            P(("dp", "ctx")),
            P(("dp", "ctx")),
            P(("dp", "ctx")),
        ),
        check_vma=False,
    )
```

profile of v0, /device:TPU:9, one launch (start us, length us, event | category | flops | bytes accessed | tf_op | source)
XLA Modules:
  0.0 3269.6 jit_solution(3282374814490839247)
XLA Ops:
  9.8 41.9 %all-reduce = bf16[14336]{0:T(1024)(128)(2,1)S(1)} all-reduce(bf16[14336]{0:T(1024)(128)(2,1)S(1)} %dynamic-update-slice), channel_id=1, replica_groups=mesh['dp'=4,'ctx'=8] {'dp','ctx'}, use_global_device_ids=true, to_apply=%add | all-reduce | flops 14336 | bytes 57344
  53.3 38.4 %all-gather = bf16[32,1,384]{2,1,0:T(2,128)(2,1)S(1)} all-gather(bf16[1,1,384]{2,1,0:T(2,128)(2,1)S(1)} %reshape.467), channel_id=1, replica_groups=mesh['dp'=4,'ctx'=8] {'dp','ctx'}, dimensions={0}, use_global_device_ids=true | all-gather | bytes 25344 | tf_op jit(solution)/shard_map/all_gather | solution.py:107
  96.9 2.9 add_convert_fusion.2
  99.9 67.2 %all-gather.10.cloned.1.call-done = bf16[2048,6144]{1,0:T(8,128)(2,1)} async-done(((bf16[64,6144]{1,0:T(8,128)(2,1)}), bf16[2048,6144]{1,0:T(8,128)(2,1)}) %all-gather.10.cloned.1.call-update) | async-done | bytes 25165840 | tf_op jit(solution)/shard_map/all_gather | solution.py:105
  167.0 11.6 convolution_add_fusion.1
  186.4 11.9 all-gather.12.cloned.1.call-start
  201.3 2.7 copy.75
  204.6 3.1 pad_maximum_fusion
  207.8 39.5 %all-gather.16.cloned.1.call-done = bf16[2048,2048]{1,0:T(8,128)(2,1)} async-done(((bf16[64,2048]{1,0:T(8,128)(2,1)}), bf16[2048,2048]{1,0:T(8,128)(2,1)}) %all-gather.16.cloned.1.call-update) | async-done | bytes 8388624 | tf_op jit(solution)/shard_map/all_gather | solution.py:106
  247.4 5.8 convolution_convert_fusion
  259.8 67.7 %all-gather.14.cloned.1.call-done = bf16[2,1024,8,256]{3,1,2,0:T(8,128)(2,1)} async-done(((bf16[2,128,8,256]{3,1,2,0:T(8,128)(2,1)}), bf16[2,1024,8,256]{3,1,2,0:T(8,128)(2,1)}) %all-gather.14.cloned.1.call-update) | async-done | bytes 8388624 | tf_op jit(solution)/shard_map/all_gather | solution.py:141
  327.5 6.4 fusion.8
  334.0 3.3 copy-done
  340.1 70.2 %all-gather.12.cloned.1.call-done = bf16[2,1024,8,256]{1,3,2,0:T(8,128)(2,1)} async-done(((bf16[2,128,8,256]{1,3,2,0:T(8,128)(2,1)}), bf16[2,1024,8,256]{1,3,2,0:T(8,128)(2,1)}) %all-gather.12.cloned.1.call-update) | async-done | bytes 8388624 | tf_op jit(solution)/shard_map/all_gather | solution.py:142
  410.3 9.0 multiply_reduce_fusion
  419.4 6.0 multiply_bitcast_fusion.1
  426.7 17.3 all_gather.53
  444.1 16.1 all_gather.51
  460.2 33.7 %all-gather.22.cloned.1.call-done = bf16[2,1024,8,256]{3,1,2,0:T(8,128)(2,1)} async-done(((bf16[2,128,8,256]{3,1,2,0:T(8,128)(2,1)}), bf16[2,1024,8,256]{3,1,2,0:T(8,128)(2,1)}) %all-gather.22.cloned.1.call-update) | async-done | bytes 8388624 | tf_op jit(solution)/shard_map/all_gather | solution.py:188
  493.9 9.0 fusion.65
  503.0 73.0 %all-gather.24.cloned.1.call-done = bf16[2,1024,8,256]{3,1,2,0:T(8,128)(2,1)} async-done(((bf16[2,128,8,256]{3,1,2,0:T(8,128)(2,1)}), bf16[2,1024,8,256]{3,1,2,0:T(8,128)(2,1)}) %all-gather.24.cloned.1.call-update) | async-done | bytes 8388624 | tf_op jit(solution)/shard_map/all_gather | solution.py:189
  576.0 13.0 multiply_bitcast_fusion
  591.2 2.5 subtract_convert_fusion
  599.4 7.3 fusion.38
  611.4 10.5 fusion.41
  621.9 2.7 copy.82
  624.6 2.5 copy.122
  630.4 9.7 fusion.68
  640.1 20.9 fusion.67
  661.0 112.2 %all-gather.18.cloned.1.call-done = bf16[2048,8192]{1,0:T(8,128)(2,1)} async-done(((bf16[64,8192]{1,0:T(8,128)(2,1)}), bf16[2048,8192]{1,0:T(8,128)(2,1)}) %all-gather.18.cloned.1.call-update) | async-done | bytes 33554448 | tf_op jit(solution)/shard_map/all_gather | solution.py:112
  773.1 17.7 convolution_add_fusion
  790.8 178.3 %all-gather.20.cloned.1.call-done = bf16[8192,2048]{1,0:T(8,128)(2,1)} async-done(((bf16[256,2048]{1,0:T(8,128)(2,1)}), bf16[8192,2048]{1,0:T(8,128)(2,1)}) %all-gather.20.cloned.1.call-update) | async-done | bytes 33554448 | tf_op jit(solution)/shard_map/all_gather | solution.py:113
  969.1 33.7 %convert_reduce_fusion = (f32[8192]{0:T(1024)S(1)}, bf16[256,8192]{1,0:T(8,128)(2,1)}, f32[256,8192]{1,0:T(8,128)}) fusion(f32[256,8192]{1,0:T(8,128)} %convolution_add_fusion, bf16[256,2048]{1,0:T(8,128)(2,1)S(1)} %bitcast.132, bf16[8192,2048]{1,0:T(8,128)(2,1)} %all-gather.20.cloned.1.call-done), kind=kOutput, calls=%fused_computation.3 | convolution fusion | flops 8745115648 | bytes 55607296 | tf_op jit(solution)/shard_map/dot_general | solution.py:64
  1002.8 17.3 fusion.66
  1020.2 14.3 fusion.59
  1034.6 4.4 multiply_reduce_fusion.1
  1040.7 77.4 %concatenate.39 = f32[2048,8198]{1,0:T(8,128)} concatenate(f32[2048,6144]{1,0:T(8,128)} %fusion.67, f32[2048,2048]{1,0:T(8,128)} %fusion.68, f32[2048,1]{1,0:T(8,128)S(1)} %copy.96, f32[2048,1]{1,0:T(8,128)} %copy.97, f32[2048,2]{1,0:T(8,128)S(1)} %copy-done.18, f32[2048,1]{1,0:T(8,128)} %copy.98, f32[2048,1]{1,0:T(8,128)S(1)} %copy-done.10), dimensions={1} | concatenate | bytes 134316032 | tf_op jit(solution)/shard_map/concatenate | solution.py:249
  1122.0 25.9 fusion.69
  1147.9 79.3 %concatenate.40 = f32[2048,8199]{1,0:T(8,128)} concatenate(f32[2048,8192]{1,0:T(8,128)} %fusion.69, f32[2048,1]{1,0:T(8,128)S(1)} %copy.100, f32[2048,1]{1,0:T(8,128)} %copy.101, f32[2048,4]{1,0:T(8,128)} %reshape.455, f32[2048,1]{1,0:T(8,128)S(1)} %copy-done.10), dimensions={1} | concatenate | bytes 134332416 | tf_op jit(solution)/shard_map/concatenate | solution.py:286
  1227.4 7.4 multiply_convert_fusion.2
  1237.0 23.7 fusion.70
  1262.3 7.3 fusion.32
  1272.1 17.3 fusion.33
  1289.4 545.5 %reduce-scatter.4.cloned.1.call-done = f32[64,8198]{1,0:T(8,128)} async-done(((f32[2048,8198]{1,0:T(8,128)}), f32[64,8198]{1,0:T(8,128)}) %reduce-scatter.4.cloned.1.call-update) | async-done | bytes 2098704 | tf_op jit(solution)/shard_map/reduce_scatter | solution.py:248
  1836.4 2.7 slice.202
  1842.6 711.4 %reduce-scatter.6.cloned.1.call-done = f32[64,8199]{1,0:T(8,128)} async-done(((f32[2048,8199]{1,0:T(8,128)}), f32[64,8199]{1,0:T(8,128)}) %reduce-scatter.6.cloned.1.call-update) | async-done | bytes 2098960 | tf_op jit(solution)/shard_map/reduce_scatter | solution.py:285
  2555.5 3.1 slice.207
  2560.3 702.6 %reduce-scatter.8.cloned.1.call-done = f32[256,2048]{1,0:T(8,128)} async-done(((f32[8192,2048]{1,0:T(8,128)}), f32[256,2048]{1,0:T(8,128)}) %reduce-scatter.8.cloned.1.call-update) | async-done | bytes 2097168 | tf_op jit(solution)/shard_map/reduce_scatter | solution.py:291
  (208 shorter events, 67.5 us)
Async XLA Ops:
  7.2 159.9 %all-gather.10.cloned.1.call-start = ((), (), s32[]{:S(2)}) async-start(), calls=%async_computation.3 | async-start | bytes 25952256 | tf_op jit(solution)/shard_map/all_gather | solution.py:105
  7.9 239.5 %all-gather.16.cloned.1.call-start = ((), (), s32[]{:S(2)}) async-start(), calls=%async_computation.6 | async-start | bytes 8650752 | tf_op jit(solution)/shard_map/all_gather | solution.py:106
  8.7 318.9 %all-gather.14.cloned.1.call-start = ((), (), s32[]{:S(2)}) async-start(), calls=%async_computation.5 | async-start | bytes 9437184 | tf_op jit(solution)/shard_map/all_gather | solution.py:141
  52.5 126.1 %copy-start.22 = (f32[2048]{0:T(1024)}, f32[2048]{0:T(1024)S(1)}, u32[]{:S(2)}) copy-start(f32[2048]{0:T(1024)S(1)} %reshape.461) | copy-start | bytes 24580
  92.5 86.1 %copy-start.25 = (f32[2048]{0:T(1024)}, f32[2048]{0:T(1024)S(1)}, u32[]{:S(2)}) copy-start(f32[2048]{0:T(1024)S(1)} %reshape.457) | copy-start | bytes 24580
  94.4 84.3 %copy-start.34 = (f32[256]{0:T(256)}, f32[256]{0:T(256)S(1)}, u32[]{:S(2)}) copy-start(f32[256]{0:T(256)S(1)} %get-tuple-element.113) | copy-start | bytes 3076
  96.4 82.3 %copy-start.37 = (f32[256]{0:T(256)}, f32[256]{0:T(256)S(1)}, u32[]{:S(2)}) copy-start(f32[256]{0:T(256)S(1)} %bitcast_rsqrt_fusion) | copy-start | bytes 3076
  99.9 78.8 %copy-start.15 = (bf16[256,2048]{1,0:T(8,128)(2,1)}, bf16[256,2048]{1,0:T(8,128)(2,1)S(1)}, u32[]{:S(2)}) copy-start(bf16[256,2048]{1,0:T(8,128)(2,1)S(1)} %get-tuple-element.97) | copy-start | bytes 3145732
  186.4 61.0 %copy-start.7 = (bf16[2,1,128,2048]{3,2,1,0:T(8,128)(2,1)S(1)}, bf16[2,1,128,2048]{3,2,1,0:T(8,128)(2,1)}, u32[]{:S(2)}) copy-start(bf16[2,1,128,2048]{3,2,1,0:T(8,128)(2,1)} %param.16) | copy-start | bytes 3145732
  186.4 223.9 %all-gather.12.cloned.1.call-start = ((), (), s32[]{:S(2)}) async-start(), calls=%async_computation.4 | async-start | bytes 9437184 | tf_op jit(solution)/shard_map/all_gather | solution.py:142
  204.0 289.9 %all-gather.22.cloned.1.call-start = ((), (), s32[]{:S(2)}) async-start(), calls=%async_computation.9 | async-start | bytes 9437184 | tf_op jit(solution)/shard_map/all_gather | solution.py:188
  207.8 368.2 %all-gather.24.cloned.1.call-start = ((), (), s32[]{:S(2)}) async-start(), calls=%async_computation.10 | async-start | bytes 9437184 | tf_op jit(solution)/shard_map/all_gather | solution.py:189
  253.2 5.3 copy-start.48
  253.2 74.4 %copy-start.12 = (bf16[2,128,8,256]{3,1,2,0:T(8,128)(2,1)S(1)}, bf16[2,128,8,256]{3,1,2,0:T(8,128)(2,1)}, u32[]{:S(2)}) copy-start(bf16[2,128,8,256]{3,1,2,0:T(8,128)(2,1)} %pad_maximum_fusion) | copy-start | bytes 3145732
  254.7 518.4 %all-gather.18.cloned.1.call-start = ((), (), s32[]{:S(2)}) async-start(), calls=%async_computation.7 | async-start | bytes 34603008 | tf_op jit(solution)/shard_map/all_gather | solution.py:112
  255.5 713.6 %all-gather.20.cloned.1.call-start = ((), (), s32[]{:S(2)}) async-start(), calls=%async_computation.8 | async-start | bytes 34603008 | tf_op jit(solution)/shard_map/all_gather | solution.py:113
  256.2 1578.6 %reduce-scatter.4.cloned.1.call-start = ((), (), s32[]{:S(2)}) async-start(), calls=%async_computation.11 | async-start | bytes 70287360 | tf_op jit(solution)/shard_map/reduce_scatter | solution.py:248
  410.3 9.0 copy-start.1
  419.4 74.6 %copy-start.11 = (bf16[2,128,8,256]{3,1,2,0:T(8,128)(2,1)S(1)}, bf16[2,128,8,256]{3,1,2,0:T(8,128)(2,1)}, u32[]{:S(2)}) copy-start(bf16[2,128,8,256]{3,1,2,0:T(8,128)(2,1)} %pad_maximum_fusion.1) | copy-start | bytes 3145732
  588.9 4.8 copy-start.20
  591.2 8.2 slice-start
  593.7 5.7 copy-start.21
  593.7 5.7 copy-start.28
  610.9 29.2 copy-start.6
  640.1 133.0 %copy-start.31 = (f32[4,2,8,128]{3,1,2,0:T(2,128)S(1)}, f32[4,2,8,128]{3,1,2,0:T(2,128)}, u32[]{:S(2)}) copy-start(f32[4,2,8,128]{3,1,2,0:T(2,128)} %copy.123) | copy-start | bytes 98308
  773.1 196.0 %copy-start.8 = (bf16[2,1,128,2048]{3,2,1,0:T(8,128)(2,1)S(1)}, bf16[2,1,128,2048]{3,2,1,0:T(8,128)(2,1)}, u32[]{:S(2)}) copy-start(bf16[2,1,128,2048]{3,2,1,0:T(8,128)(2,1)} %param.16) | copy-start | bytes 3145732
  1002.8 17.3 copy-start.2
  1002.8 17.3 copy-start.23
  1002.8 17.3 copy-start.26
  1002.8 17.3 copy-start.35
  1020.1 14.4 copy-start.41
  1020.2 14.4 copy-start.38
  1020.2 20.6 copy-start.10
  1020.2 20.6 copy-start.18
  1118.2 1435.8 %reduce-scatter.6.cloned.1.call-start = ((), (), s32[]{:S(2)}) async-start(), calls=%async_computation.12 | async-start | bytes 70287360 | tf_op jit(solution)/shard_map/reduce_scatter | solution.py:285
  1227.2 2035.7 %reduce-scatter.8.cloned.1.call-start = ((), (), s32[]{:S(2)}) async-start(), calls=%async_computation.13 | async-start | bytes 69206016 | tf_op jit(solution)/shard_map/reduce_scatter | solution.py:291
  1227.4 9.5 copy-start.9
  1262.2 7.4 copy-start.47
  1262.2 7.4 copy-start.46
  1262.2 7.4 copy-start.13
  1262.3 7.4 copy-start.14
  1262.3 7.4 copy-start.24
  1262.3 7.4 copy-start.27
  1262.3 7.4 copy-start.36
  1262.3 7.4 copy-start.39
  1262.3 7.4 copy-start.43
  1262.3 7.4 copy-start.45
  1262.3 9.7 copy-start.5
  (14 other events, 35.7 us)
Sparse Core Ops, SparseCore 0:
  11.0 155.9 all-gather.9
  170.0 77.3 all-gather.15
  249.6 77.9 all-gather.13
  329.6 80.7 all-gather.11
  412.4 81.5 all-gather.21
  495.4 80.5 all-gather.23
  578.9 194.1 all-gather.17
  776.1 192.9 all-gather.19
  1118.3 716.5 reduce-scatter.3
  1837.2 716.7 reduce-scatter.5
  2556.9 705.9 reduce-scatter.7
where the time goes:
time: 3290 us; the launch traced here: 3270 us
  waiting for transfers between devices  2600 us (79%)
  matrix products  266 us (8%)
  local copies, waits for them, and re-layouts  218 us (7%)
  blocking collectives  114 us (3%)
  other arithmetic  39.6 us (1%)
    reduce_scatter x1, waiting for transfers between devices, shards(): lax.psum_scatter(jnp.concatenate([contract_rows(hidden_part, grad_expande...  711 us
    reduce_scatter x1, waiting for transfers between devices, shards(): lax.psum_scatter(contract_rows(activated, cot_rows), ('dp', 'ctx'), scatt...  703 us
    reduce_scatter x1, waiting for transfers between devices, shards(): lax.psum_scatter(jnp.concatenate([contract_rows(hidden_part, grad_joined)...  546 us
    all_gather x1, waiting for transfers between devices, fetch_mlp(): lax.all_gather(shrink_weight, ('dp', 'ctx'), axis=0, tiled=True)  178 us
    all_gather x1, waiting for transfers between devices, fetch_mlp(): lax.all_gather(expand_weight, ('dp', 'ctx'), axis=0, tiled=True)  112 us
    dot_general x4, matrix products, contract_rows(): lax.dot_general(left_mat, right_mat, (((0,), (0,)), ((), ())), preferred_...  80.1 us
    concatenate x1, local copies, waits for them, and re-layouts, shards(): jnp.concatenate([contract_rows(hidden_part, grad_expanded), small_part],...  79.3 us
    concatenate x1, local copies, waits for them, and re-layouts, shards(): jnp.concatenate([contract_rows(hidden_part, grad_joined), contract_rows(m...  77.4 us
  transfers between devices with their start and end apart: 11, of which 11 were waited for; matrix products, arithmetic and copies ran while one was open for 11% of the time, Pallas kernels for 0%

commit v1 on v0

--- a/solution.py
+++ b/solution.py
@@ -317,6 +317,218 @@
     )
 
 
+def low(values):
+    return values.astype(jnp.bfloat16)
+
+
+def small_params(packed_row):
+    return lax.all_gather(packed_row, ("dp", "ctx"), axis=0, tiled=True)
+
+
+def tensor_shards(
+    layer_input,
+    out_grad,
+    prefix_len,
+    qkv_weight,
+    qkv_bias,
+    dense_weight,
+    dense_bias,
+    expand_weight,
+    expand_bias,
+    shrink_weight,
+    shrink_bias,
+    attn_gain,
+    attn_shift,
+    mlp_gain,
+    mlp_shift,
+):
+    dp_size = lax.axis_size("dp")
+    ctx_size = lax.axis_size("ctx")
+    devices = dp_size * ctx_size
+    me = lax.axis_index("ctx")
+    group = lax.axis_index("dp")
+    micro, seq_count, span, width = layer_input.shape
+    sequences = micro * seq_count
+    tokens = sequences * SEQ
+    row_share = qkv_weight.shape[0]
+    scale = 1.0 / math.sqrt(HEAD)
+    ff = expand_weight.shape[1]
+    unit = shrink_weight.shape[0]
+    lengths = tuple(
+        member.shape[0]
+        for member in (attn_gain, attn_shift, mlp_gain, mlp_shift, qkv_bias, dense_bias, expand_bias, shrink_bias)
+    )
+    packed = jnp.concatenate(
+        [attn_gain, attn_shift, mlp_gain, mlp_shift, qkv_bias, dense_bias, expand_bias, shrink_bias]
+    )
+    own_x = layer_input.reshape(sequences, span, width)
+    own_g = out_grad.reshape(sequences, span, width)
+    x_all = lax.all_gather(own_x, "ctx", axis=1, tiled=True).reshape(tokens, width)
+    g_all = lax.all_gather(own_g, "ctx", axis=1, tiled=True).reshape(tokens, width)
+    columns = jnp.concatenate(
+        [
+            qkv_weight.reshape(row_share, 3, ctx_size, HEAD),
+            expand_weight.reshape(row_share, dp_size, ctx_size, unit),
+        ],
+        axis=1,
+    )
+    columns = jnp.transpose(columns, (2, 0, 1, 3)).reshape(ctx_size * row_share, -1)
+    columns = lax.all_to_all(columns, "ctx", split_axis=0, concat_axis=0, tiled=True)
+    columns = lax.all_gather(columns, "dp", axis=0, tiled=True)
+    qkv_part = columns[:, : 3 * HEAD]
+    expand_part = columns[:, 3 * HEAD :]
+    shrink_part = lax.all_gather(shrink_weight, "dp", axis=0, tiled=True)
+    dense_full = lax.all_gather(dense_weight, ("dp", "ctx"), axis=0, tiled=True)
+    dense_part = lax.dynamic_slice_in_dim(dense_full, me * HEAD, HEAD, 0)
+    small = unpack_small(small_params(packed), lengths, devices)
+    gain_attn, shift_attn, gain_mlp, shift_mlp, qkv_shift, dense_shift, expand_shift, shrink_shift = small
+    qkv_shift = lax.dynamic_slice_in_dim(qkv_shift.reshape(3, ctx_size, HEAD), me, 1, 1).reshape(-1)
+    expand_shift = lax.dynamic_slice_in_dim(
+        expand_shift.reshape(dp_size, ctx_size, unit), me, 1, 1
+    ).reshape(-1)
+
+    inputs = x_all.astype(jnp.float32)
+    row_mean = jnp.mean(inputs, axis=-1, keepdims=True)
+    centered = inputs - row_mean
+    spread = lax.rsqrt(jnp.mean(centered * centered, axis=-1, keepdims=True) + 1e-05)
+    normal = centered * spread
+    hidden_attn = low(normal * gain_attn + shift_attn)
+    hidden_mlp = low(normal * gain_mlp + shift_mlp)
+
+    cos_table, sin_table = rope_tables(jnp.arange(SEQ, dtype=jnp.float32))
+    joined = jnp.dot(hidden_attn, qkv_part, preferred_element_type=jnp.float32) + qkv_shift
+    joined = joined.reshape(sequences, SEQ, 3, HEAD)
+
+    def turn(heads, sin_values):
+        return rotate(heads[:, :, None, :], cos_table, sin_values)[:, :, 0]
+
+    queries = low(turn(joined[:, :, 0], sin_table))
+    key_rows = low(turn(joined[:, :, 1], sin_table))
+    value_rows = low(joined[:, :, 2])
+    positions = jnp.arange(SEQ, dtype=jnp.int32)
+    prefix = prefix_len.reshape(sequences)
+    allowed = (positions[None, :] <= positions[:, None])[None] | (
+        positions[None, None, :] < prefix[:, None, None]
+    )
+    scores = jnp.einsum("sqe,ske->sqk", queries, key_rows, preferred_element_type=jnp.float32) * scale
+    scores = jnp.where(allowed, scores, -1e30)
+    expo = jnp.exp(scores - jnp.max(scores, axis=-1, keepdims=True))
+    probs = expo / jnp.sum(expo, axis=-1, keepdims=True)
+    probs_low = low(probs)
+    mixed = low(
+        jnp.einsum("sqk,ske->sqe", probs_low, value_rows, preferred_element_type=jnp.float32)
+    ).reshape(tokens, HEAD)
+    expanded = jnp.dot(hidden_mlp, expand_part, preferred_element_type=jnp.float32) + expand_shift
+    activated = low(gelu_exact(expanded))
+    features = jnp.concatenate([mixed, activated], axis=1)
+    out_part = jnp.concatenate([dense_part, shrink_part], axis=0)
+    partial = low(jnp.dot(features, out_part, preferred_element_type=jnp.float32))
+    reduced = lax.psum_scatter(
+        partial.reshape(sequences, SEQ, width), "ctx", scatter_dimension=1, tiled=True
+    )
+    layer_output = low(
+        own_x.astype(jnp.float32) + reduced.astype(jnp.float32) + (dense_shift + shrink_shift)
+    ).reshape(layer_input.shape)
+
+    out_grads = low(contract_rows(features, g_all))
+    grad_features = contract_cols(g_all, out_part)
+    unused, gelu_back = jax.vjp(gelu_exact, expanded)
+    grad_expanded = low(gelu_back(grad_features[:, HEAD:])[0])
+    grad_mixed = low(grad_features[:, :HEAD]).reshape(sequences, SEQ, HEAD)
+    shrink_grad = lax.psum_scatter(out_grads[HEAD:], "dp", scatter_dimension=0, tiled=True)
+    dense_own = jnp.zeros((ctx_size, HEAD, width), jnp.bfloat16)
+    dense_own = lax.dynamic_update_slice(dense_own, out_grads[:HEAD][None], (me, 0, 0))
+    dense_grad = lax.psum_scatter(
+        dense_own.reshape(ctx_size * HEAD, width), ("dp", "ctx"), scatter_dimension=0, tiled=True
+    )
+    expand_grads = low(contract_rows(hidden_mlp, grad_expanded))
+    back_mlp = contract_cols(grad_expanded, expand_part)
+
+    grad_probs = jnp.einsum("sqe,ske->sqk", grad_mixed, value_rows, preferred_element_type=jnp.float32)
+    delta = jnp.sum(probs * grad_probs, axis=-1, keepdims=True)
+    grad_scores = low(probs * (grad_probs - delta))
+    grad_queries = (
+        jnp.einsum("sqk,ske->sqe", grad_scores, key_rows, preferred_element_type=jnp.float32) * scale
+    )
+    grad_keys = (
+        jnp.einsum("sqk,sqe->ske", grad_scores, queries, preferred_element_type=jnp.float32) * scale
+    )
+    grad_values = jnp.einsum("sqk,sqe->ske", probs_low, grad_mixed, preferred_element_type=jnp.float32)
+    grad_joined = low(
+        jnp.concatenate([turn(grad_queries, -sin_table), turn(grad_keys, -sin_table), grad_values], axis=-1)
+    ).reshape(tokens, 3 * HEAD)
+    qkv_grads = low(contract_rows(hidden_attn, grad_joined))
+    back_attn = contract_cols(grad_joined, qkv_part)
+    column_grads = jnp.concatenate([qkv_grads, expand_grads], axis=1)
+    column_grads = lax.psum_scatter(column_grads, "dp", scatter_dimension=0, tiled=True)
+    column_grads = lax.all_to_all(column_grads, "ctx", split_axis=0, concat_axis=0, tiled=True)
+    column_grads = column_grads.reshape(ctx_size, row_share, 3 + dp_size, HEAD)
+    column_grads = jnp.transpose(column_grads, (1, 2, 0, 3)).astype(jnp.float32)
+    qkv_grad = column_grads[:, :3].reshape(row_share, 3 * width)
+    expand_grad = column_grads[:, 3:].reshape(row_share, ff)
+
+    combined = low(back_attn * gain_attn + back_mlp * gain_mlp)
+    combined = lax.psum_scatter(
+        combined.reshape(sequences, SEQ, width), "ctx", scatter_dimension=1, tiled=True
+    ).astype(jnp.float32)
+    own = own_x.astype(jnp.float32)
+    own_center = own - jnp.mean(own, axis=-1, keepdims=True)
+    own_spread = lax.rsqrt(jnp.mean(own_center * own_center, axis=-1, keepdims=True) + 1e-05)
+    own_normal = own_center * own_spread
+    share = own_spread * (
+        combined
+        - jnp.mean(combined, axis=-1, keepdims=True)
+        - own_normal * jnp.mean(combined * own_normal, axis=-1, keepdims=True)
+    )
+    input_grad = low(own_g.astype(jnp.float32) + share).reshape(layer_input.shape)
+
+    def place(values, parts):
+        board = jnp.zeros((parts, ctx_size, values.shape[0] // parts), jnp.float32)
+        board = lax.dynamic_update_slice(board, values.reshape(parts, 1, -1), (0, me, 0))
+        return board.reshape(devices, -1)
+
+    joined_sum = jnp.sum(grad_joined.astype(jnp.float32), axis=0)
+    expand_sum = jnp.sum(grad_expanded.astype(jnp.float32), axis=0)
+    out_sum = jnp.sum(own_g.astype(jnp.float32), axis=(0, 1))
+    board = jnp.concatenate(
+        [
+            place(joined_sum[: 2 * HEAD], 2),
+            place(joined_sum[2 * HEAD :], 1),
+            out_sum.reshape(devices, -1),
+            place(expand_sum, dp_size),
+            jnp.sum(back_attn * normal, axis=0).reshape(devices, -1),
+            jnp.sum(back_attn, axis=0).reshape(devices, -1),
+            jnp.sum(back_mlp * normal, axis=0).reshape(devices, -1),
+            jnp.sum(back_mlp, axis=0).reshape(devices, -1),
+        ],
+        axis=1,
+    )
+    tail = lax.psum_scatter(board, ("dp", "ctx"), scatter_dimension=0, tiled=True).reshape(-1)
+    share_len = width // devices
+    at = 0
+    pieces = []
+    for length in (2 * share_len, share_len, share_len, ff // devices, share_len, share_len, share_len, share_len):
+        pieces.append(tail[at : at + length])
+        at += length
+    return (
+        layer_output,
+        input_grad,
+        qkv_grad,
+        pieces[0],
+        pieces[1],
+        dense_grad.astype(jnp.float32),
+        pieces[2],
+        expand_grad,
+        pieces[3],
+        shrink_grad.astype(jnp.float32),
+        pieces[2],
+        pieces[4],
+        pieces[5],
+        pieces[6],
+        pieces[7],
+    )
+
+
 def solution(mesh):
     placed = (
         P(None, "dp", "ctx", None),
@@ -336,7 +548,7 @@
         P(("dp", "ctx")),
     )
     return jax.shard_map(
-        shards,
+        tensor_shards if mesh.shape["ctx"] == HEADS else shards,
         mesh=mesh,
         in_specs=placed,
         out_specs=(

time: 3290 us -> 1160 us (0.35)
  waiting for transfers between devices: 2600 us -> 695 us
  local copies, waits for them, and re-layouts: 218 us -> 65.5 us
  matrix products: 266 us -> 174 us
    reduce_scatter x3 -> x5, waiting for transfers between devices: 1960 us -> 379 us  [the longest x1 142 us: tensor_shards(): lax.psum_scatter(dense_own.reshape(ctx_size * HEAD, width), ('dp', 'ctx')...]
    all_gather x8 -> x5, waiting for transfers between devices: 642 us -> 205 us  [the longest x1 81.3 us: tensor_shards(): lax.all_gather(own_g, 'ctx', axis=1, tiled=True).reshape(tokens, width)]
    concatenate x5 -> x2, local copies, waits for them, and re-layouts: 158 us -> 0.81 us  [the longest x1 0.72 us: tensor_shards(): jnp.concatenate([place(joined_sum[:2 * HEAD], 2), place(joined_sum[2 * HE...]
    unnamed x11 -> x12, waiting for transfers between devices: 2.88 us -> 111 us
    all_to_all x0 -> x1, blocking collectives: none -> 94.2 us  [tensor_shards(): lax.all_to_all(columns, 'ctx', split_axis=0, concat_axis=0, tiled=True)]
    all_gather x3 -> x0, blocking collectives: 71.8 us -> none  [the longest x1 38.4 us: fetch_attn(): lax.all_gather(attn_packed, ('dp', 'ctx'), axis=0, tiled=True)]
    dot_general x4 -> x3, matrix products: 80.1 us -> 36.6 us  [contract_rows(): lax.dot_general(left_mat, right_mat, (((0,), (0,)), ((), ())), preferred_...]
    dot_general x11 -> x8, matrix products: 115 us -> 75.3 us  [the longest x1 33.5 us: tensor_shards(): jnp.dot(hidden_mlp, expand_part, preferred_element_type=jnp.float32)]
  transfers between devices with their start and end apart: 11 -> 12, of which waited for: 11 -> 9; matrix products, arithmetic and copies ran while one was open for 11% -> 16% of each run, Pallas kernels for 0% -> 0%
where the time goes in v1:
time: 1160 us
  waiting for transfers between devices  695 us (60%)
  matrix products  174 us (15%)
  blocking collectives  138 us (12%)
  local copies, waits for them, and re-layouts  65.5 us (6%)
  other arithmetic  62.9 us (5%)
  between operations  15.1 us (1%)
    reduce_scatter x1, waiting for transfers between devices, tensor_shards(): lax.psum_scatter(dense_own.reshape(ctx_size * HEAD, width), ('dp', 'ctx')...  142 us
    unnamed x12, waiting for transfers between devices  111 us
    reduce_scatter x1, waiting for transfers between devices, tensor_shards(): lax.psum_scatter(combined.reshape(sequences, SEQ, width), 'ctx', scatter_...  96 us
    all_to_all x1, blocking collectives, tensor_shards(): lax.all_to_all(columns, 'ctx', split_axis=0, concat_axis=0, tiled=True)  94.2 us
    reduce_scatter x1, waiting for transfers between devices, tensor_shards(): lax.psum_scatter(partial.reshape(sequences, SEQ, width), 'ctx', scatter_d...  88.5 us
    all_gather x1, waiting for transfers between devices, tensor_shards(): lax.all_gather(own_g, 'ctx', axis=1, tiled=True).reshape(tokens, width)  81.3 us
    dot_general x3, matrix products, contract_cols(): lax.dot_general(left_mat, right_mat, (((1,), (1,)), ((), ())), preferred_...  53.2 us
    reduce_scatter x1, waiting for transfers between devices, tensor_shards(): lax.psum_scatter(out_grads[HEAD:], 'dp', scatter_dimension=0, tiled=True)  52.6 us
  transfers between devices with their start and end apart: 12, of which 9 were waited for; matrix products, arithmetic and copies ran while one was open for 16% of the time, Pallas kernels for 0%

profile of v1, /device:TPU:9, one launch (start us, length us, event | category | flops | bytes accessed | tf_op | source)
XLA Modules:
  0.0 1156.4 jit_solution(16134408234653374175)
XLA Ops:
  12.8 2.9 all_to_all.14
  15.7 94.2 %all_to_all.21 = bf16[8,64,1792]{2,1,0:T(8,128)(2,1)} all-to-all(bf16[8,64,1792]{2,1,0:T(8,128)(2,1)} %all_to_all.14), channel_id=1, replica_groups=mesh['dp'=4,'ctx'=8] {'ctx'}, dimensions={0} | all-to-all | bytes 3670016 | tf_op jit(solution)/shard_map/all_to_all | solution.py:376
  112.4 43.8 %all-reduce = bf16[26624]{0:T(1024)(128)(2,1)S(1)} all-reduce(bf16[26624]{0:T(1024)(128)(2,1)S(1)} %dynamic-update-slice), channel_id=1, replica_groups=mesh['dp'=4,'ctx'=8] {'dp','ctx'}, use_global_device_ids=true, to_apply=%add | all-reduce | flops 26624 | bytes 106496
  158.2 2.9 fusion.53
  161.1 4.7 convert_reduce_fusion
  166.9 2.3 fusion.2
  169.3 8.6 add_convert_fusion.2
  177.9 33.7 %all-gather.8.cloned.1.call-done = bf16[2048,1792]{1,0:T(8,128)(2,1)} async-done(((bf16[512,1792]{1,0:T(8,128)(2,1)}), bf16[2048,1792]{1,0:T(8,128)(2,1)}) %all-gather.8.cloned.1.call-update) | async-done | bytes 7340048 | tf_op jit(solution)/shard_map/all_gather | solution.py:377
  211.6 11.7 %broadcast_add_fusion = f32[2048,768]{1,0:T(8,128)} fusion(f32[768]{0:T(1024)S(1)} %add.126, bf16[2048,2048]{1,0:T(8,128)(2,1)} %get-tuple-element.29, bf16[2048,1792]{1,0:T(8,128)(2,1)} %all-gather.8.cloned.1.call-done), kind=kOutput, calls=%fused_computation.58 | convolution fusion | flops 6444023808 | bytes 17828864 | tf_op jit(solution)/shard_map/dot_general | solution.py:399
  223.2 11.3 reshape.415
  234.5 4.9 fusion.63
  239.4 2.3 fusion.64
  243.8 8.7 fusion.65
  252.5 39.8 %all-gather.10.cloned.1.call-done = bf16[2048,2048]{1,0:T(8,128)(2,1)} async-done(((bf16[64,2048]{1,0:T(8,128)(2,1)}), bf16[2048,2048]{1,0:T(8,128)(2,1)}) %all-gather.10.cloned.1.call-update) | async-done | bytes 8388624 | tf_op jit(solution)/shard_map/all_gather | solution.py:381
  292.3 2.3 constant_dynamic-slice_fusion
  294.6 50.3 %all-gather.12.cloned.1.call-done = bf16[1024,2048]{1,0:T(8,128)(2,1)} async-done(((bf16[256,2048]{1,0:T(8,128)(2,1)}), bf16[1024,2048]{1,0:T(8,128)(2,1)}) %all-gather.12.cloned.1.call-update) | async-done | bytes 4194320 | tf_op jit(solution)/shard_map/all_gather | solution.py:380
  344.9 81.3 %all-gather.16.cloned.1.call-done = bf16[2,1,1024,2048]{3,2,1,0:T(8,128)(2,1)} async-done(((bf16[2,1,128,2048]{3,2,1,0:T(8,128)(2,1)}), bf16[2,1,1024,2048]{3,2,1,0:T(8,128)(2,1)}) %all-gather.16.cloned.1.call-update) | async-done | bytes 8388624 | tf_op jit(solution)/shard_map/all_gather | solution.py:367
  426.2 16.8 %convolution_bitcast_fusion = f32[2048,1280]{1,0:T(8,128)} fusion(bf16[2048,2048]{1,0:T(8,128)(2,1)} %bitcast.216, bf16[1024,2048]{1,0:T(8,128)(2,1)} %all-gather.12.cloned.1.call-done, bf16[256,2048]{1,0:T(8,128)(2,1)} %constant_dynamic-slice_fusion), kind=kOutput, calls=%fused_computation.13 | convolution fusion | flops 10747904000 | bytes 24117248 | tf_op jit(solution)/shard_map/dot_general | solution.py:64
  444.6 2.2 fusion.42
  448.5 2.6 multiply_convert_fusion
  452.7 2.4 multiply_bitcast_fusion.1
  457.3 33.5 %convert_reduce_fusion.1 = (f32[1024]{0:T(1024)S(1)}, bf16[2048,1024]{1,0:T(8,128)(2,1)}, f32[2048,1024]{1,0:T(8,128)}, f32[2048,1024]{1,0:T(8,128)}) fusion(f32[2048,1280]{1,0:T(8,128)} %convolution_bitcast_fusion, f32[1024]{0:T(1024)S(1)} %bitcast.209, bf16[2048,2048]{1,0:T(8,128)(2,1)S(1)} %bitcast.186, bf16[2048,1792]{1,0:T(8,128)(2,1)} %all-gather.8.cloned.1.call-done), kind=kOutput, calls=%fused_computation.15 | convolution fusion | flops 8747219968 | bytes 41951232 | tf_op jit(solution)/shard_map/dot_general | solution.py:421
  490.8 12.7 %convolution_convert_fusion.2 = bf16[2048,1024]{0,1:T(8,128)(2,1)} fusion(bf16[2048,2048]{1,0:T(8,128)(2,1)S(1)} %bitcast.186, bf16[2048,1024]{1,0:T(8,128)(2,1)} %get-tuple-element.22), kind=kOutput, calls=%fused_computation.48 | convolution fusion | flops 8592031744 | bytes 16777216 | tf_op jit(solution)/shard_map/dot_general | solution.py:58
  505.4 7.7 convolution_convert_fusion.3
  513.1 6.5 pad_maximum_fusion
  519.9 6.4 fusion.39
  527.1 13.0 %fusion.19 = f32[2048,2048]{1,0:T(8,128)} fusion(bf16[2048,1792]{1,0:T(8,128)(2,1)} %all-gather.8.cloned.1.call-done, bf16[2048,256]{1,0:T(8,128)(2,1)} %bitcast.202, bf16[2048,256]{1,0:T(8,128)(2,1)S(1)} %bitcast.193, bf16[2048,256]{1,0:T(8,128)(2,1)S(1)} %bitcast.196), kind=kOutput, calls=%fused_computation.59 | convolution fusion | flops 6451888128 | bytes 23068672 | tf_op jit(solution)/shard_map/dot_general | solution.py:64
  540.1 23.4 %fusion.60 = (f32[2048]{0:T(1024)S(1)}, f32[2048]{0:T(1024)S(1)}, bf16[2048,2048]{1,0:T(8,128)(2,1)}, f32[2048]{0:T(1024)S(1)}, f32[2048]{0:T(1024)S(1)}) fusion(f32[2048]{0:T(1024)S(1)} %copy-done.25, f32[2048]{0:T(1024)S(1)} %copy-done.27, bf16[2,1,1024,2048]{3,2,1,0:T(8,128)(2,1)} %all-gather.14.cloned.1.call-done, f32[2048]{0:T(1024)S(1)} %copy-done.23, ...), kind=kOutput, calls=%fused_computation.147 | convolution fusion | flops 8644452352 | bytes 42008576 | tf_op jit(solution)/shard_map/dot_general | solution.py:64
  564.6 10.4 multiply_convert_fusion.1
  575.1 16.2 %convolution_convert_fusion.1 = bf16[1280,2048]{1,0:T(8,128)(2,1)S(1)} fusion(bf16[2048,2048]{1,0:T(8,128)(2,1)} %bitcast.217, bf16[2048,1024]{1,0:T(8,128)(2,1)} %multiply_convert_fusion.1, bf16[2048,256]{1,0:T(8,128)(2,1)S(1)} %bitcast.218), kind=kOutput, calls=%fused_computation.36 | convolution fusion | flops 10750525440 | bytes 18874368 | tf_op jit(solution)/shard_map/dot_general | solution.py:58
  591.3 2.4 copy-done.5
  593.7 2.2 slice.241
  596.0 4.3 broadcast_in_dim.24
  600.4 2.4 fusion.47
  604.0 16.1 %convolution_convert_fusion = bf16[2048,2048]{1,0:T(8,128)(2,1)} fusion(bf16[1024,2048]{1,0:T(8,128)(2,1)} %all-gather.12.cloned.1.call-done, bf16[256,2048]{1,0:T(8,128)(2,1)S(1)} %copy-done.10, bf16[2048,1024]{1,0:T(8,128)(2,1)} %multiply_convert_fusion.1, bf16[2048,256]{1,0:T(8,128)(2,1)S(1)} %bitcast.219), kind=kOutput, calls=%fused_computation.35 | convolution fusion | flops 10762584064 | bytes 18874368 | tf_op jit(solution)/shard_map/dot_general | solution.py:425
  620.1 3.9 copy.125
  624.0 5.5 all-to-all-start.1
  631.1 108.2 %all-reduce.4.cloned.1.call-done = f32[32,768]{1,0:T(8,128)} async-done(((f32[32,768]{1,0:T(8,128)}), f32[32,768]{1,0:T(8,128)}) %all-reduce.4.cloned.1.call-update) | async-done | bytes 98320
  743.3 52.6 %reduce-scatter.14.cloned.1.call-done = bf16[256,2048]{1,0:T(8,128)(2,1)} async-done(((bf16[1024,2048]{1,0:T(8,128)(2,1)}), bf16[256,2048]{1,0:T(8,128)(2,1)}) %reduce-scatter.14.cloned.1.call-update) | async-done | bytes 1048592 | tf_op jit(solution)/shard_map/reduce_scatter | solution.py:438
  795.8 2.8 convert_element_type.216
  798.6 141.8 %reduce-scatter.12.cloned.1.call-done = bf16[64,2048]{1,0:T(8,128)(2,1)} async-done(((bf16[2048,2048]{1,0:T(8,128)(2,1)}), bf16[64,2048]{1,0:T(8,128)(2,1)}) %reduce-scatter.12.cloned.1.call-update) | async-done | bytes 262160 | tf_op jit(solution)/shard_map/reduce_scatter | solution.py:441
  942.2 96.0 %reduce-scatter.8.cloned.1.call-done = bf16[2,128,2048]{2,1,0:T(8,128)(2,1)} async-done(((bf16[2,1024,2048]{2,1,0:T(8,128)(2,1)}), bf16[2,128,2048]{2,1,0:T(8,128)(2,1)}) %reduce-scatter.8.cloned.1.call-update) | async-done | bytes 1048592 | tf_op jit(solution)/shard_map/reduce_scatter | solution.py:471
  1040.1 88.5 %reduce-scatter.6.cloned.1.call-done = bf16[2,128,2048]{2,1,0:T(8,128)(2,1)} async-done(((bf16[2,1024,2048]{2,1,0:T(8,128)(2,1)}), bf16[2,128,2048]{2,1,0:T(8,128)(2,1)}) %reduce-scatter.6.cloned.1.call-update) | async-done | bytes 1048592 | tf_op jit(solution)/shard_map/reduce_scatter | solution.py:426
  1128.6 4.0 fusion.46
  1132.6 4.8 reshape.404
  1137.4 2.7 slice.240
  1140.1 2.5 slice.238
  1146.4 2.5 copy.143
  (182 shorter events, 38.7 us)
Async XLA Ops:
  7.2 154.0 %all-gather.14.cloned.1.call-start = ((), (), s32[]{:S(2)}) async-start(), calls=%async_computation.15 | async-start | bytes 9437184 | tf_op jit(solution)/shard_map/all_gather | solution.py:366
  7.9 203.6 %all-gather.8.cloned.1.call-start = ((), (), s32[]{:S(2)}) async-start(), calls=%async_computation.7 | async-start | bytes 9175040 | tf_op jit(solution)/shard_map/all_gather | solution.py:377
  11.6 100.4 %copy-start.28 = (bf16[64]{0:T(256)(128)(2,1)S(1)}, bf16[64]{0:T(256)(128)(2,1)}, u32[]{:S(2)}) copy-start(bf16[64]{0:T(256)(128)(2,1)} %param.26) | copy-start | bytes 388
  11.6 100.4 %copy-start.29 = (bf16[64]{0:T(256)(128)(2,1)S(1)}, bf16[64]{0:T(256)(128)(2,1)}, u32[]{:S(2)}) copy-start(bf16[64]{0:T(256)(128)(2,1)} %param.27) | copy-start | bytes 388
  11.6 100.4 %copy-start.30 = (bf16[64]{0:T(256)(128)(2,1)S(1)}, bf16[64]{0:T(256)(128)(2,1)}, u32[]{:S(2)}) copy-start(bf16[64]{0:T(256)(128)(2,1)} %param.28) | copy-start | bytes 388
  11.6 100.4 %copy-start.31 = (bf16[64]{0:T(256)(128)(2,1)S(1)}, bf16[64]{0:T(256)(128)(2,1)}, u32[]{:S(2)}) copy-start(bf16[64]{0:T(256)(128)(2,1)} %param.29) | copy-start | bytes 388
  11.6 100.4 %copy-start.32 = (bf16[192]{0:T(256)(128)(2,1)S(1)}, bf16[192]{0:T(256)(128)(2,1)}, u32[]{:S(2)}) copy-start(bf16[192]{0:T(256)(128)(2,1)} %param.19) | copy-start | bytes 1156
  11.6 100.4 %copy-start.33 = (bf16[64]{0:T(256)(128)(2,1)S(1)}, bf16[64]{0:T(256)(128)(2,1)}, u32[]{:S(2)}) copy-start(bf16[64]{0:T(256)(128)(2,1)} %param.21) | copy-start | bytes 388
  11.6 100.4 %copy-start.34 = (bf16[256]{0:T(256)(128)(2,1)S(1)}, bf16[256]{0:T(256)(128)(2,1)}, u32[]{:S(2)}) copy-start(bf16[256]{0:T(256)(128)(2,1)} %param.23) | copy-start | bytes 1540
  11.7 100.4 %copy-start.35 = (bf16[64]{0:T(256)(128)(2,1)S(1)}, bf16[64]{0:T(256)(128)(2,1)}, u32[]{:S(2)}) copy-start(bf16[64]{0:T(256)(128)(2,1)} %param.25) | copy-start | bytes 388
  11.7 146.5 %copy-start.36 = (s32[2,1]{0,1:T(1,128)S(1)}, s32[2,1]{0,1:T(1,128)}, u32[]{:S(2)}) copy-start(s32[2,1]{0,1:T(1,128)} %param.17) | copy-start | bytes 28
  110.0 182.3 %all-gather.10.cloned.1.call-start = ((), (), s32[]{:S(2)}) async-start(), calls=%async_computation.8 | async-start | bytes 8650752 | tf_op jit(solution)/shard_map/all_gather | solution.py:381
  110.7 234.2 %all-gather.12.cloned.1.call-start = ((), (), s32[]{:S(2)}) async-start(), calls=%async_computation.9 | async-start | bytes 5242880 | tf_op jit(solution)/shard_map/all_gather | solution.py:380
  111.3 314.9 %all-gather.16.cloned.1.call-start = ((), (), s32[]{:S(2)}) async-start(), calls=%async_computation.16 | async-start | bytes 9437184 | tf_op jit(solution)/shard_map/all_gather | solution.py:367
  111.9 508.2 %reduce-scatter.10.cloned.1.call-start = ((), (), s32[]{:S(2)}) async-start(), calls=%async_computation.12 | async-start | bytes 9175040 | tf_op jit(solution)/shard_map/reduce_scatter | solution.py:463
  156.3 12.9 %copy-start.19 = (bf16[32,832]{1,0:T(8,128)(2,1)}, bf16[32,832]{1,0:T(8,128)(2,1)S(1)}, u32[]{:S(2)}) copy-start(bf16[32,832]{1,0:T(8,128)(2,1)S(1)} %reshape.372) | copy-start | bytes 159748
  156.6 12.7 %copy-start.20 = (f32[2048]{0:T(1024)}, f32[2048]{0:T(1024)S(1)}, u32[]{:S(2)}) copy-start(f32[2048]{0:T(1024)S(1)} %reshape.398) | copy-start | bytes 24580
  156.7 12.6 %copy-start.22 = (f32[2048]{0:T(1024)}, f32[2048]{0:T(1024)S(1)}, u32[]{:S(2)}) copy-start(f32[2048]{0:T(1024)S(1)} %reshape.401) | copy-start | bytes 24580
  161.1 5.8 copy-start
  169.3 8.6 copy-start.24
  169.3 8.6 copy-start.26
  234.5 7.3 copy-start.6
  234.5 7.3 copy-start.9
  239.4 207.4 %copy-start.3 = (bf16[2,1024,3,256]{3,1,0,2:T(8,128)(2,1)}, bf16[2,1024,3,256]{3,1,0,2:T(8,128)(2,1)S(1)}, u32[]{:S(2)}) copy-start(bf16[2,1024,3,256]{3,1,0,2:T(8,128)(2,1)S(1)} %get-tuple-element.24) | copy-start | bytes 9437188
  426.2 18.5 %copy-start.4 = (f32[2,1024,1024]{1,2,0:T(8,128)S(1)}, f32[2,1024,1024]{1,2,0:T(8,128)}, u32[]{:S(2)}) copy-start(f32[2,1024,1024]{1,2,0:T(8,128)} %get-tuple-element.62) | copy-start | bytes 25165828
  448.5 2.7 copy-start.14
  448.5 2.7 copy-start.17
  452.7 3.2 copy-start.7
  452.7 3.2 copy-start.8
  452.7 4.0 slice-start.2
  455.9 49.5 %slice-start = ((s8[8388608]{0:T(1024)(128)(4,1)}), s8[4194304]{0:T(1024)(128)(4,1)S(1)}, s32[]{:S(2)}) async-start(s8[8388608]{0:T(1024)(128)(4,1)} %bitcast.183), calls=%async_computation.18 | async-start | bytes 8388608
  457.3 48.0 %slice-start.1 = ((s8[8388608]{0:T(1024)(128)(4,1)}), s8[4194304]{0:T(1024)(128)(4,1)S(1)}, s32[]{:S(2)}) async-start(s8[8388608]{0:T(1024)(128)(4,1)} %bitcast.183), calls=%async_computation.19 | async-start | bytes 8388608
  490.8 14.6 %copy-start.11 = (bf16[2,1024,256]{2,1,0:T(8,128)(2,1)S(1)}, bf16[2,1024,256]{2,1,0:T(8,128)(2,1)}, u32[]{:S(2)}) copy-start(bf16[2,1024,256]{2,1,0:T(8,128)(2,1)} %fusion.42) | copy-start | bytes 3145732
  513.1 6.5 copy-start.2
  519.6 219.7 %all-reduce.4.cloned.1.call-start = ((), (), s32[]{:S(2)}) async-start(), calls=%async_computation.17 | async-start | bytes 196608
  519.9 6.4 copy-start.12
  527.1 13.0 %copy-start.21 = (f32[2048]{0:T(1024)S(1)}, f32[2048]{0:T(1024)}, u32[]{:S(2)}) copy-start(f32[2048]{0:T(1024)} %copy-done.20) | copy-start | bytes 24580
  527.1 13.0 %copy-start.23 = (f32[2048]{0:T(1024)S(1)}, f32[2048]{0:T(1024)}, u32[]{:S(2)}) copy-start(f32[2048]{0:T(1024)} %copy-done.22) | copy-start | bytes 24580
  527.1 13.0 %copy-start.25 = (f32[2048]{0:T(1024)S(1)}, f32[2048]{0:T(1024)}, u32[]{:S(2)}) copy-start(f32[2048]{0:T(1024)} %copy-done.24) | copy-start | bytes 24580
  527.1 13.0 %copy-start.27 = (f32[2048]{0:T(1024)S(1)}, f32[2048]{0:T(1024)}, u32[]{:S(2)}) copy-start(f32[2048]{0:T(1024)} %copy-done.26) | copy-start | bytes 24580
  564.6 10.4 copy-start.38
  575.0 220.8 %reduce-scatter.14.cloned.1.call-start = ((), (), s32[]{:S(2)}) async-start(), calls=%async_computation.14 | async-start | bytes 5242880 | tf_op jit(solution)/shard_map/reduce_scatter | solution.py:438
  596.0 344.5 %reduce-scatter.12.cloned.1.call-start = ((), (), s32[]{:S(2)}) async-start(), calls=%async_computation.13 | async-start | bytes 8650752 | tf_op jit(solution)/shard_map/reduce_scatter | solution.py:441
  602.8 435.4 %reduce-scatter.8.cloned.1.call-start = ((), (), s32[]{:S(2)}) async-start(), calls=%async_computation.11 | async-start | bytes 9437184 | tf_op jit(solution)/shard_map/reduce_scatter | solution.py:471
  603.4 525.2 %reduce-scatter.6.cloned.1.call-start = ((), (), s32[]{:S(2)}) async-start(), calls=%async_computation.10 | async-start | bytes 9437184 | tf_op jit(solution)/shard_map/reduce_scatter | solution.py:426
  620.1 10.3 copy-start.1
  624.0 508.6 %all-to-all-start.1 = ((bf16[8,64,1792]{2,1,0:T(8,128)(2,1)}), bf16[8,64,1792]{2,1,0:T(8,128)(2,1)}, u32[]{:S(2)}, u32[]{:S(2)}) async-start(bf16[8,64,1792]{2,1,0:T(8,128)(2,1)} %bitcast.189), calls=%async_computation.4 | async-start | bytes 3670016 | tf_op jit(solution)/shard_map/all_to_all | solution.py:464
  740.7 408.2 %copy-start.37 = (f32[64]{0:T(128)}, f32[64]{0:T(128)S(1)}, u32[]{:S(2)}) copy-start(f32[64]{0:T(128)S(1)} %get-tuple-element.92) | copy-start | bytes 772
  (7 other events, 13.0 us)
Sparse Core Ops, SparseCore 0:
  9.6 117.1 all-gather.13
  128.6 82.8 all-gather.7
  214.5 77.7 all-gather.9
  294.0 50.8 all-gather.11
  346.3 79.7 all-gather.15
  519.7 79.7 reduce-scatter.9
  605.6 133.5 all-reduce.3
  742.2 53.5 reduce-scatter.13
  798.2 142.1 reduce-scatter.11
  942.7 95.4 reduce-scatter.7
  1040.6 87.9 reduce-scatter.5

commit v2 on v1

--- a/solution.py
+++ b/solution.py
@@ -1,8 +1,11 @@
+import functools
 import math
 
 import jax
 import jax.numpy as jnp
 from jax import lax
+from jax.experimental import pallas as pl
+from jax.experimental.pallas import tpu as pltpu
 from jax.sharding import PartitionSpec as P
 
 HEADS = 8
@@ -321,8 +324,408 @@
     return values.astype(jnp.bfloat16)
 
 
-def small_params(packed_row):
-    return lax.all_gather(packed_row, ("dp", "ctx"), axis=0, tiled=True)
+MESH_ID = pl.DeviceIdType.MESH
+
+
+def remote(src, dst, send_sem, recv_sem, dp, ctx):
+    return pltpu.make_async_remote_copy(
+        src_ref=src,
+        dst_ref=dst,
+        send_sem=send_sem,
+        recv_sem=recv_sem,
+        device_id=(dp, ctx),
+        device_id_type=MESH_ID,
+    )
+
+
+def greet_all(dp, ctx, dp_size, ctx_size):
+    barrier = pltpu.get_barrier_semaphore()
+    devices = dp_size * ctx_size
+    me = dp * ctx_size + ctx
+
+    def greet(step, carry):
+        other = lax.rem(me + step, devices)
+        pl.semaphore_signal(
+            barrier, inc=1, device_id=(other // ctx_size, lax.rem(other, ctx_size)), device_id_type=MESH_ID
+        )
+        return carry
+
+    lax.fori_loop(1, devices, greet, 0)
+    pl.semaphore_wait(barrier, devices - 1)
+
+
+def gather_kernel(
+    dp_size,
+    ctx_size,
+    x,
+    qkv,
+    expand,
+    dense,
+    shrink,
+    packed,
+    x_all,
+    panels,
+    out_w,
+    small,
+    local_sem,
+    small_sem,
+    block_send,
+    block_recv,
+    core_send,
+    core_recv,
+    panel_send,
+    panel_recv,
+    share_send,
+    share_recv,
+    pass_send,
+    pass_recv,
+):
+    d = lax.axis_index("dp")
+    c = lax.axis_index("ctx")
+    z = c // 2
+    sibling = c + 1 - 2 * lax.rem(c, 2)
+    x_mate = d + 1 - 2 * lax.rem(d, 2)
+    y_mate = lax.rem(d + 2, 4)
+    micro, span = x.shape[0], x.shape[1]
+    devices = dp_size * ctx_size
+    me = d * ctx_size + c
+    rows = qkv.shape[0]
+    unit = shrink.shape[0]
+    levels = ctx_size // 2
+    panel_rows = ctx_size * rows
+    n_panels = 3 + dp_size
+
+    greet_all(d, c, dp_size, ctx_size)
+
+    def column_block(panel, target):
+        if panel < 3:
+            start = panel * (qkv.shape[1] // 3) + target * HEAD
+            return qkv.at[:, pl.ds(pl.multiple_of(start, HEAD), HEAD)]
+        start = (panel - 3) * ctx_size * unit + target * unit
+        return expand.at[:, pl.ds(pl.multiple_of(start, HEAD), HEAD)]
+
+    own_rows = pl.ds(pl.multiple_of((d * ctx_size + c) * rows, rows), rows)
+
+    for panel in range(n_panels):
+        pltpu.make_async_copy(
+            column_block(panel, c), panels.at[panel, own_rows], local_sem.at[panel]
+        ).start()
+
+        def push(step, carry, panel=panel):
+            target = lax.rem(c + step, ctx_size)
+            remote(
+                column_block(panel, target),
+                panels.at[panel, own_rows],
+                panel_send.at[panel],
+                panel_recv.at[panel],
+                d,
+                target,
+            ).start()
+            return carry
+
+        lax.fori_loop(1, ctx_size, push, 0)
+
+    def shrink_rows(owner, offset, count):
+        return out_w.at[pl.ds(pl.multiple_of(HEAD + owner * unit + offset, 16), count)]
+
+    shrink_local = pltpu.make_async_copy(shrink, shrink_rows(d, 0, unit), local_sem.at[n_panels])
+    shrink_local.start()
+    for way, mate in ((0, x_mate), (1, y_mate)):
+        remote(
+            shrink, shrink_rows(d, 0, unit), share_send.at[n_panels, way], share_recv.at[n_panels, way], mate, c
+        ).start()
+
+    per_head = HEAD // rows
+    head_of = (d * ctx_size + c) // per_head
+    dense_rows = pl.ds(pl.multiple_of(lax.rem(c, per_head) * rows, rows), rows)
+    dense_out = remote(dense, out_w.at[dense_rows], panel_send.at[n_panels], panel_recv.at[n_panels], d, head_of)
+    dense_own = pltpu.make_async_copy(dense, out_w.at[dense_rows], local_sem.at[n_panels + 1])
+    stays = head_of == c
+
+    @pl.when(stays)
+    def _():
+        dense_own.start()
+
+    @pl.when(jnp.logical_not(stays))
+    def _():
+        dense_out.start()
+
+    def block(origin, m):
+        return x_all.at[m, pl.ds(pl.multiple_of(origin * span, span), span)]
+
+    x_local = []
+    for m in range(micro):
+        copy = pltpu.make_async_copy(x.at[m], block(c, m), local_sem.at[n_panels + 2 + m])
+        copy.start()
+        x_local.append(copy)
+
+    def chain(way, hop, m):
+        step = 2 if way == 0 else -2
+        origin = c - step * hop
+        src = x.at[m] if hop == 0 else block(origin, m)
+        exists = jnp.logical_and(z >= hop, z <= levels - 2) if way == 0 else jnp.logical_and(
+            z + hop <= levels - 1, z >= 1
+        )
+        copy = remote(src, block(origin, m), block_send.at[way, hop, m], block_recv.at[way, hop, m], d, c + step)
+        return exists, copy
+
+    def arrives(way, hop):
+        return z >= hop + 1 if way == 0 else z + hop + 1 <= levels - 1
+
+    def core_copy(slot, origin, m):
+        src = x.at[m] if slot == 0 else block(origin, m)
+        return remote(src, block(origin, m), core_send.at[slot, m], core_recv.at[slot, m], d, sibling)
+
+    for m in range(micro):
+        core_copy(0, c, m).start()
+        for way in range(2):
+            exists, copy = chain(way, 0, m)
+
+            @pl.when(exists)
+            def _(copy=copy):
+                copy.start()
+
+    small_copy = pltpu.make_async_copy(packed, small.at[me], local_sem.at[n_panels + 2 + micro])
+    small_copy.start()
+
+    def push_small(step, carry):
+        other = lax.rem(me + step, devices)
+        remote(
+            packed,
+            small.at[me],
+            small_sem.at[0],
+            small_sem.at[1],
+            other // ctx_size,
+            lax.rem(other, ctx_size),
+        ).start()
+        return carry
+
+    lax.fori_loop(1, devices, push_small, 0)
+
+    def slot_of(way, hop):
+        return 1 + way * (levels - 1) + hop
+
+    def hop_step(hop):
+        for m in range(micro):
+            for way in range(2):
+                step = 2 if way == 0 else -2
+
+                @pl.when(arrives(way, hop))
+                def _(way=way, m=m, step=step):
+                    origin = c - step * (hop + 1)
+                    remote(
+                        block(origin, m), block(origin, m), block_send.at[way, hop, m], block_recv.at[way, hop, m], d, c - step
+                    ).wait_recv()
+                    core_copy(slot_of(way, hop), origin, m).start()
+
+                if hop + 1 <= levels - 2:
+                    exists, copy = chain(way, hop + 1, m)
+
+                    @pl.when(exists)
+                    def _(copy=copy):
+                        copy.start()
+
+    def group_rows(owner, offset, count):
+        return pl.ds(pl.multiple_of(owner * panel_rows + offset, 16), count)
+
+    def panel_share(panel, way, mate):
+        view = panels.at[panel, group_rows(d, 0, panel_rows)]
+        return remote(view, view, share_send.at[panel, way], share_recv.at[panel, way], mate, c)
+
+    def panel_step(panel):
+        pltpu.make_async_copy(column_block(panel, c), panels.at[panel, own_rows], local_sem.at[panel]).wait()
+        whole = panels.at[panel, group_rows(d, 0, (ctx_size - 1) * rows)]
+        remote(whole, whole, panel_send.at[panel], panel_recv.at[panel], d, sibling).wait_recv()
+        panel_share(panel, 0, x_mate).start()
+        panel_share(panel, 1, y_mate).start()
+
+    half = panel_rows // 2
+
+    def panel_pass(panel, way):
+        owner, mate = ((x_mate, y_mate), (y_mate, x_mate))[way]
+        view = panels.at[panel, group_rows(owner, way * half, half)]
+        return remote(view, view, pass_send.at[panel, way], pass_recv.at[panel, way], mate, c)
+
+    def panel_forward(panel):
+        for way, owner in ((0, x_mate), (1, y_mate)):
+            view = panels.at[panel, group_rows(owner, 0, panel_rows)]
+            remote(view, view, share_send.at[panel, way], share_recv.at[panel, way], owner, c).wait_recv()
+            panel_pass(panel, way).start()
+
+    def shrink_share_wait(way, owner):
+        view = shrink_rows(owner, 0, unit)
+        remote(view, view, share_send.at[n_panels, way], share_recv.at[n_panels, way], owner, c).wait_recv()
+
+    def shrink_pass(way):
+        owner, mate = ((x_mate, y_mate), (y_mate, x_mate))[way]
+        view = shrink_rows(owner, way * (unit // 2), unit // 2)
+        return remote(view, view, pass_send.at[n_panels, way], pass_recv.at[n_panels, way], mate, c)
+
+    source = c // (ctx_size // dp_size)
+    at_source = d == source
+    from_x = x_mate == source
+    from_y = y_mate == source
+    head_rows = out_w.at[pl.ds(0, HEAD)]
+    half_head = HEAD // 2
+
+    def dense_share(way, mate):
+        return remote(head_rows, head_rows, share_send.at[n_panels + 1, way], share_recv.at[n_panels + 1, way], mate, c)
+
+    def dense_pass(way, mate):
+        view = out_w.at[pl.ds(way * half_head, half_head)]
+        return remote(view, view, pass_send.at[n_panels + 1, way], pass_recv.at[n_panels + 1, way], mate, c)
+
+    owns_share = jnp.logical_and(at_source, stays)
+
+    def dense_gather_step():
+        @pl.when(owns_share)
+        def _():
+            dense_own.wait()
+            view = out_w.at[pl.ds(0, (per_head - 1) * rows)]
+            remote(view, view, panel_send.at[n_panels], panel_recv.at[n_panels], d, sibling).wait_recv()
+
+        @pl.when(jnp.logical_and(at_source, jnp.logical_not(stays)))
+        def _():
+            remote(head_rows, head_rows, panel_send.at[n_panels], panel_recv.at[n_panels], d, sibling).wait_recv()
+
+        @pl.when(at_source)
+        def _():
+            dense_share(0, x_mate).start()
+            dense_share(1, y_mate).start()
+
+    def dense_forward_step():
+        @pl.when(from_x)
+        def _():
+            dense_share(0, x_mate).wait_recv()
+            dense_pass(0, y_mate).start()
+
+        @pl.when(from_y)
+        def _():
+            dense_share(1, y_mate).wait_recv()
+            dense_pass(1, x_mate).start()
+
+    across = jnp.logical_not(jnp.logical_or(at_source, jnp.logical_or(from_x, from_y)))
+
+    for panel in range(3):
+        panel_step(panel)
+    shrink_share_wait(0, x_mate)
+    shrink_pass(0).start()
+    shrink_share_wait(1, y_mate)
+    shrink_pass(1).start()
+    dense_gather_step()
+    hop_step(0)
+    for panel in range(3, n_panels):
+        panel_step(panel)
+        panel_forward(panel - 3)
+    hop_step(1)
+    dense_forward_step()
+    for panel in range(n_panels - 3, n_panels):
+        panel_forward(panel)
+    for hop in range(2, levels - 1):
+        hop_step(hop)
+
+    for panel in range(n_panels):
+        for way, mate in ((0, x_mate), (1, y_mate)):
+            panel_share(panel, way, mate).wait_send()
+            panel_pass(panel, way).wait_send()
+        for way in range(2):
+            diagonal = 3 - d
+            view = panels.at[panel, group_rows(diagonal, way * half, half)]
+            remote(view, view, pass_send.at[panel, way], pass_recv.at[panel, way], x_mate, c).wait_recv()
+        whole = panels.at[panel, group_rows(d, 0, (ctx_size - 1) * rows)]
+        remote(whole, whole, panel_send.at[panel], panel_recv.at[panel], x_mate, c).wait_send()
+    shrink_local.wait()
+    for way in range(2):
+        mate = (x_mate, y_mate)[way]
+        remote(
+            shrink, shrink_rows(d, 0, unit), share_send.at[n_panels, way], share_recv.at[n_panels, way], mate, c
+        ).wait_send()
+        shrink_pass(way).wait_send()
+        view = shrink_rows(3 - d, way * (unit // 2), unit // 2)
+        remote(view, view, pass_send.at[n_panels, way], pass_recv.at[n_panels, way], mate, c).wait_recv()
+
+    @pl.when(jnp.logical_not(stays))
+    def _():
+        dense_out.wait_send()
+
+    @pl.when(at_source)
+    def _():
+        dense_share(0, x_mate).wait_send()
+        dense_share(1, y_mate).wait_send()
+
+    @pl.when(from_x)
+    def _():
+        dense_pass(0, y_mate).wait_send()
+
+    @pl.when(from_y)
+    def _():
+        dense_pass(1, x_mate).wait_send()
+
+    @pl.when(across)
+    def _():
+        dense_pass(0, y_mate).wait_recv()
+        dense_pass(1, x_mate).wait_recv()
+
+    for m in range(micro):
+        x_local[m].wait()
+        core_copy(0, c, m).wait_send()
+        core_copy(0, sibling, m).wait_recv()
+        for way in range(2):
+            step = 2 if way == 0 else -2
+            for hop in range(levels - 1):
+                exists, copy = chain(way, hop, m)
+
+                @pl.when(exists)
+                def _(copy=copy):
+                    copy.wait_send()
+
+                @pl.when(arrives(way, hop))
+                def _(way=way, hop=hop, m=m, step=step):
+                    slot = slot_of(way, hop)
+                    core_copy(slot, c - step * (hop + 1), m).wait_send()
+                    core_copy(slot, sibling - step * (hop + 1), m).wait_recv()
+
+    small_copy.wait()
+    rest = small.at[pl.ds(0, devices - 1)]
+    remote(rest, rest, small_sem.at[0], small_sem.at[1], d, sibling).wait()
+
+
+def gather_call(dp_size, ctx_size, x, qkv, expand, dense, shrink, packed):
+    micro, span, width = x.shape
+    rows = qkv.shape[0]
+    n_panels = 3 + dp_size
+    levels = ctx_size // 2
+    devices = dp_size * ctx_size
+    dma = pltpu.SemaphoreType.DMA
+    out_shape = (
+        jax.ShapeDtypeStruct((micro, ctx_size * span, width), x.dtype),
+        jax.ShapeDtypeStruct((n_panels, devices * rows, HEAD), x.dtype),
+        jax.ShapeDtypeStruct((HEAD + dp_size * shrink.shape[0], width), x.dtype),
+        jax.ShapeDtypeStruct((devices,) + packed.shape, x.dtype),
+    )
+    anywhere = pl.BlockSpec(memory_space=pl.ANY)
+    return pl.pallas_call(
+        functools.partial(gather_kernel, dp_size, ctx_size),
+        out_shape=out_shape,
+        in_specs=[anywhere] * 6,
+        out_specs=(anywhere,) * 4,
+        scratch_shapes=[
+            dma((n_panels + 3 + micro,)),
+            dma((2,)),
+            dma((2, levels - 1, micro)),
+            dma((2, levels - 1, micro)),
+            dma((2 * levels - 1, micro)),
+            dma((2 * levels - 1, micro)),
+            dma((n_panels + 1,)),
+            dma((n_panels + 1,)),
+            dma((n_panels + 2, 2)),
+            dma((n_panels + 2, 2)),
+            dma((n_panels + 2, 2)),
+            dma((n_panels + 2, 2)),
+        ],
+        compiler_params=pltpu.CompilerParams(collective_id=1, has_side_effects=True),
+        name="gather_all",
+    )(x, qkv, expand, dense, shrink, packed)
 
 
 def tensor_shards(
@@ -363,24 +766,16 @@
     )
     own_x = layer_input.reshape(sequences, span, width)
     own_g = out_grad.reshape(sequences, span, width)
-    x_all = lax.all_gather(own_x, "ctx", axis=1, tiled=True).reshape(tokens, width)
     g_all = lax.all_gather(own_g, "ctx", axis=1, tiled=True).reshape(tokens, width)
-    columns = jnp.concatenate(
-        [
-            qkv_weight.reshape(row_share, 3, ctx_size, HEAD),
-            expand_weight.reshape(row_share, dp_size, ctx_size, unit),
-        ],
-        axis=1,
-    )
-    columns = jnp.transpose(columns, (2, 0, 1, 3)).reshape(ctx_size * row_share, -1)
-    columns = lax.all_to_all(columns, "ctx", split_axis=0, concat_axis=0, tiled=True)
-    columns = lax.all_gather(columns, "dp", axis=0, tiled=True)
-    qkv_part = columns[:, : 3 * HEAD]
-    expand_part = columns[:, 3 * HEAD :]
-    shrink_part = lax.all_gather(shrink_weight, "dp", axis=0, tiled=True)
-    dense_full = lax.all_gather(dense_weight, ("dp", "ctx"), axis=0, tiled=True)
-    dense_part = lax.dynamic_slice_in_dim(dense_full, me * HEAD, HEAD, 0)
-    small = unpack_small(small_params(packed), lengths, devices)
+    count = packed.shape[0]
+    packed = jnp.pad(packed, (0, -count % 2048)).reshape(-1, 128)
+    x_all, panels, out_part, small = gather_call(
+        dp_size, ctx_size, own_x, qkv_weight, expand_weight, dense_weight, shrink_weight, packed
+    )
+    x_all = x_all.reshape(tokens, width)
+    qkv_part = panels[:3]
+    expand_part = panels[3:]
+    small = unpack_small(small.reshape(devices, -1)[:, :count], lengths, devices)
     gain_attn, shift_attn, gain_mlp, shift_mlp, qkv_shift, dense_shift, expand_shift, shrink_shift = small
     qkv_shift = lax.dynamic_slice_in_dim(qkv_shift.reshape(3, ctx_size, HEAD), me, 1, 1).reshape(-1)
     expand_shift = lax.dynamic_slice_in_dim(
@@ -396,7 +791,8 @@
     hidden_mlp = low(normal * gain_mlp + shift_mlp)
 
     cos_table, sin_table = rope_tables(jnp.arange(SEQ, dtype=jnp.float32))
-    joined = jnp.dot(hidden_attn, qkv_part, preferred_element_type=jnp.float32) + qkv_shift
+    joined = jnp.einsum("td,pde->tpe", hidden_attn, qkv_part, preferred_element_type=jnp.float32)
+    joined = joined.reshape(tokens, -1) + qkv_shift
     joined = joined.reshape(sequences, SEQ, 3, HEAD)
 
     def turn(heads, sin_values):
@@ -418,10 +814,10 @@
     mixed = low(
         jnp.einsum("sqk,ske->sqe", probs_low, value_rows, preferred_element_type=jnp.float32)
     ).reshape(tokens, HEAD)
-    expanded = jnp.dot(hidden_mlp, expand_part, preferred_element_type=jnp.float32) + expand_shift
+    expanded = jnp.einsum("td,pde->tpe", hidden_mlp, expand_part, preferred_element_type=jnp.float32)
+    expanded = expanded.reshape(tokens, -1) + expand_shift
     activated = low(gelu_exact(expanded))
     features = jnp.concatenate([mixed, activated], axis=1)
-    out_part = jnp.concatenate([dense_part, shrink_part], axis=0)
     partial = low(jnp.dot(features, out_part, preferred_element_type=jnp.float32))
     reduced = lax.psum_scatter(
         partial.reshape(sequences, SEQ, width), "ctx", scatter_dimension=1, tiled=True
@@ -442,7 +838,12 @@
         dense_own.reshape(ctx_size * HEAD, width), ("dp", "ctx"), scatter_dimension=0, tiled=True
     )
     expand_grads = low(contract_rows(hidden_mlp, grad_expanded))
-    back_mlp = contract_cols(grad_expanded, expand_part)
+    back_mlp = jnp.einsum(
+        "tpe,pde->td",
+        grad_expanded.reshape(tokens, -1, HEAD),
+        expand_part,
+        preferred_element_type=jnp.float32,
+    )
 
     grad_probs = jnp.einsum("sqe,ske->sqk", grad_mixed, value_rows, preferred_element_type=jnp.float32)
     delta = jnp.sum(probs * grad_probs, axis=-1, keepdims=True)
@@ -458,7 +859,12 @@
         jnp.concatenate([turn(grad_queries, -sin_table), turn(grad_keys, -sin_table), grad_values], axis=-1)
     ).reshape(tokens, 3 * HEAD)
     qkv_grads = low(contract_rows(hidden_attn, grad_joined))
-    back_attn = contract_cols(grad_joined, qkv_part)
+    back_attn = jnp.einsum(
+        "tpe,pde->td",
+        grad_joined.reshape(tokens, -1, HEAD),
+        qkv_part,
+        preferred_element_type=jnp.float32,
+    )
     column_grads = jnp.concatenate([qkv_grads, expand_grads], axis=1)
     column_grads = lax.psum_scatter(column_grads, "dp", scatter_dimension=0, tiled=True)
     column_grads = lax.all_to_all(column_grads, "ctx", split_axis=0, concat_axis=0, tiled=True)
@@ -548,7 +954,7 @@
         P(("dp", "ctx")),
     )
     return jax.shard_map(
-        tensor_shards if mesh.shape["ctx"] == HEADS else shards,
+        tensor_shards if (mesh.shape["dp"], mesh.shape["ctx"]) == (4, HEADS) else shards,
         mesh=mesh,
         in_specs=placed,
         out_specs=(

time: 1160 us -> 1090 us (0.940)
  Pallas kernels: 0 us -> 203 us
  waiting for transfers between devices: 695 us -> 523 us
  blocking collectives: 138 us -> 0 us
  local copies, waits for them, and re-layouts: 65.5 us -> 90.9 us
    pallas_call x0 -> x1, Pallas kernels: none -> 203 us  [gather_call(): pl.pallas_call(functools.partial(gather_kernel, dp_size, ctx_size), out_s...]
    all_gather x4 -> x0, waiting for transfers between devices: 124 us -> none  [the longest x1 50.3 us: tensor_shards(): shrink_part = lax.all_gather(shrink_weight, 'dp', axis=0, tiled=True)]
    all_to_all x1 -> x0, blocking collectives: 94.2 us -> none  [tensor_shards(): lax.all_to_all(columns, 'ctx', split_axis=0, concat_axis=0, tiled=True)]
    all_gather x1, waiting for transfers between devices: 81.3 us -> 0.02 us  [tensor_shards(): lax.all_gather(own_g, 'ctx', axis=1, tiled=True).reshape(tokens, width)]
    unnamed x1 -> x0, blocking collectives: 43.8 us -> none
    dot_general x3 -> x1, matrix products: 53.2 us -> 15.3 us  [contract_cols(): lax.dot_general(left_mat, right_mat, (((1,), (1,)), ((), ())), preferred_...]
    dot_general x2 -> x4, matrix products: 45.1 us -> 81.4 us  [the longest x1 34 us: tensor_shards(): jnp.einsum('td,pde->tpe', hidden_mlp, expand_part, preferred_element_type...]
    unnamed x12 -> x8, waiting for transfers between devices: 111 us -> 130 us
  transfers between devices with their start and end apart: 12 -> 8, of which waited for: 9 -> 6; matrix products, arithmetic and copies ran while one was open for 16% -> 15% of each run, Pallas kernels for 0% -> 19%
where the time goes in v2:
time: 1090 us; the launch traced here: 1080 us
  waiting for transfers between devices  523 us (48%)
  Pallas kernels  203 us (19%)
  matrix products  175 us (16%)
  local copies, waits for them, and re-layouts  90.9 us (8%)
  other arithmetic  66.3 us (6%)
  between operations  15.3 us (1%)
    pallas_call x1, Pallas kernels, gather_call(): pl.pallas_call(functools.partial(gather_kernel, dp_size, ctx_size), out_s...  203 us
    reduce_scatter x1, waiting for transfers between devices, tensor_shards(): lax.psum_scatter(dense_own.reshape(ctx_size * HEAD, width), ('dp', 'ctx')...  142 us
    unnamed x8, waiting for transfers between devices  130 us
    reduce_scatter x1, waiting for transfers between devices, tensor_shards(): lax.psum_scatter(combined.reshape(sequences, SEQ, width), 'ctx', scatter_...  95.8 us
    reduce_scatter x1, waiting for transfers between devices, tensor_shards(): lax.psum_scatter(partial.reshape(sequences, SEQ, width), 'ctx', scatter_d...  88.5 us
    reduce_scatter x1, waiting for transfers between devices, tensor_shards(): lax.psum_scatter(out_grads[HEAD:], 'dp', scatter_dimension=0, tiled=True)  52.5 us
    dot_general x3, matrix products, contract_rows(): lax.dot_general(left_mat, right_mat, (((0,), (0,)), ((), ())), preferred_...  37.1 us
    dot_general x1, matrix products, tensor_shards(): jnp.einsum('td,pde->tpe', hidden_mlp, expand_part, preferred_element_type...  34 us
  transfers between devices with their start and end apart: 8, of which 6 were waited for; matrix products, arithmetic and copies ran while one was open for 15% of the time, Pallas kernels for 19%

profile of v2, /device:TPU:9, one launch (start us, length us, event | category | flops | bytes accessed | tf_op | source)
XLA Modules:
  0.0 1080.0 jit_solution(11963715381383704414)
XLA Ops:
  8.0 5.4 concatenate.40
  14.0 203.5 %gather_all.1 = (bf16[2,1024,2048]{2,1,0:T(8,128)(2,1)}, bf16[7,2048,256]{2,1,0:T(8,128)(2,1)}, bf16[1280,2048]{1,0:T(8,128)(2,1)}, bf16[32,16,128]{2,1,0:T(8,128)(2,1)}) custom-call(bf16[2,128,2048]{2,1,0:T(8,128)(2,1)} %bitcast.177, bf16[64,6144]{1,0:T(8,128)(2,1)} %qkv.1, bf16[64,8192]{1,0:T(8,128)(2,1)} %expand.1, bf16[64,2048]{1,0:T(8,128)(2,1)} %dense.1, ...), custom_call_target="tpu_custom_call" | custom-call | tf_op jit(solution)/shard_map/gather_all/pallas_call | solution.py:707
  221.0 3.1 copy.130
  224.1 4.7 convert_reduce_fusion
  228.9 5.8 multiply_reduce_fusion
  234.8 7.3 add_convert_fusion.3
  242.1 8.6 broadcast_add_fusion
  250.7 10.7 reshape.455
  261.4 4.4 slice_bitcast_fusion
  265.8 6.3 copy.138
  274.2 2.9 fusion.51
  277.1 5.0 fusion.60
  282.1 2.3 fusion.61
  286.5 8.6 fusion.62
  295.2 15.3 %convolution_bitcast_fusion = f32[2048,1280]{0,1:T(8,128)S(1)} fusion(bf16[1280,2048]{1,0:T(8,128)(2,1)} %get-tuple-element.22, bf16[2048,2048]{1,0:T(8,128)(2,1)} %bitcast.217), kind=kOutput, calls=%fused_computation.20 | convolution fusion | flops 10737418240 | bytes 24117248 | tf_op jit(solution)/shard_map/dot_general | solution.py:67
  310.5 4.0 copy-done.24
  317.9 5.0 multiply_reduce_fusion.1
  322.9 4.8 multiply_convert_fusion
  329.2 2.4 multiply_bitcast_fusion.1
  338.5 4.1 reshape.454
  342.6 13.1 %fusion.19 = f32[2048,2048,1]{1,0,2:T(8,128)} fusion(bf16[2048,3,256]{2,1,0:T(4,128)(2,1)} %reshape.454, bf16[7,2048,256]{2,1,0:T(8,128)(2,1)} %get-tuple-element.21), kind=kOutput, calls=%fused_computation.61 | convolution fusion | flops 6442450944 | bytes 24117248 | tf_op jit(solution)/shard_map/tpe,pde->td/dot_general | solution.py:862
  355.8 34.0 %convert_reduce_fusion.1 = (f32[1024]{0:T(1024)S(1)}, bf16[2048,1024]{0,1:T(8,128)(2,1)}, f32[2048,1024]{0,1:T(8,128)}, f32[2048,1024]{0,1:T(8,128)}) fusion(f32[2048,1280]{0,1:T(8,128)} %copy-done.24, f32[1024]{0:T(1024)S(1)} %bitcast.210, bf16[2048,2048]{1,0:T(8,128)(2,1)} %bitcast.187, bf16[1024,2048]{1,0:T(8,128)(2,1)S(1)} %bitcast.195), kind=kOutput, calls=%fused_computation.22 | convolution fusion | flops 8747219968 | bytes 41951232 | tf_op jit(solution)/shard_map/td,pde->tpe/dot_general | solution.py:817
  389.9 25.6 %bitcast_reduce_fusion = (f32[2048]{0:T(1024)S(1)}, f32[2048]{0:T(1024)S(1)}, bf16[2048,2048]{1,0:T(8,128)(2,1)}, f32[2048]{0:T(1024)S(1)}, f32[2048]{0:T(1024)S...) fusion(f32[2048]{0:T(1024)S(1)} %copy-done.35, f32[2048]{0:T(1024)S(1)} %copy-done.36, ...), kind=kOutput, calls=%fused_computation.3 | convolution fusion | flops 8669618176 | bytes 58802176 | tf_op jit(solution)/shard_map/tpe,pde->td/dot_general | solution.py:841
  415.5 14.1 %convolution_convert_fusion.2 = bf16[2048,1024]{0,1:T(8,128)(2,1)} fusion(bf16[2048,1024]{0,1:T(8,128)(2,1)} %get-tuple-element.105, bf16[2048,2048]{1,0:T(8,128)(2,1)} %get-tuple-element.112), kind=kOutput, calls=%fused_computation.54 | convolution fusion | flops 8592031744 | bytes 16777216 | tf_op jit(solution)/shard_map/dot_general | solution.py:61
  429.6 8.3 convolution_convert_fusion.3
  437.9 6.4 pad_maximum_fusion
  444.4 6.4 fusion.37
  450.9 2.5 copy.139
  456.5 9.2 multiply_convert_fusion.1
  465.8 14.7 %convolution_convert_fusion = bf16[1280,2048]{1,0:T(8,128)(2,1)S(1)} fusion(bf16[2048,2048]{1,0:T(8,128)(2,1)} %bitcast.218, bf16[2048,1024]{0,1:T(8,128)(2,1)} %multiply_convert_fusion.1, bf16[2048,256]{0,1:T(8,128)(2,1)S(1)} %copy-done.15), kind=kOutput, calls=%fused_computation.42 | convolution fusion | flops 10750525440 | bytes 18874368 | tf_op jit(solution)/shard_map/dot_general | solution.py:61
  480.5 2.3 copy-done.7
  485.2 4.3 broadcast_in_dim.24
  489.5 2.3 fusion.45
  492.5 16.7 %convolution_convert_fusion.1 = bf16[2048,2048]{1,0:T(8,128)(2,1)} fusion(bf16[1280,2048]{1,0:T(8,128)(2,1)} %get-tuple-element.22, bf16[2048,1024]{0,1:T(8,128)(2,1)} %multiply_convert_fusion.1, bf16[2048,256]{0,1:T(8,128)(2,1)S(1)} %copy-done.15), kind=kOutput, calls=%fused_computation.43 | convolution fusion | flops 10752098304 | bytes 18874368 | tf_op jit(solution)/shard_map/dot_general | solution.py:821
  509.2 13.8 %reduce-scatter.10.cloned.1.call-done = bf16[512,1792]{0,1:T(8,128)(2,1)} async-done(((bf16[2048,1792]{0,1:T(8,128)(2,1)}), bf16[512,1792]{0,1:T(8,128)(2,1)}) %reduce-scatter.10.cloned.1.call-update) | async-done | bytes 1835024 | tf_op jit(solution)/shard_map/reduce_scatter | solution.py:869
  523.0 3.8 copy.152
  526.8 5.7 all-to-all-start
  534.0 128.7 %all-reduce.4.cloned.1.call-done = f32[32,768]{1,0:T(8,128)} async-done(((f32[32,768]{1,0:T(8,128)}), f32[32,768]{1,0:T(8,128)}) %all-reduce.4.cloned.1.call-update) | async-done | bytes 98320
  666.7 52.5 %reduce-scatter.14.cloned.1.call-done = bf16[256,2048]{1,0:T(8,128)(2,1)} async-done(((bf16[1024,2048]{1,0:T(8,128)(2,1)}), bf16[256,2048]{1,0:T(8,128)(2,1)}) %reduce-scatter.14.cloned.1.call-update) | async-done | bytes 1048592 | tf_op jit(solution)/shard_map/reduce_scatter | solution.py:834
  719.2 2.8 convert_element_type.239
  722.0 141.9 %reduce-scatter.12.cloned.1.call-done = bf16[64,2048]{1,0:T(8,128)(2,1)} async-done(((bf16[2048,2048]{1,0:T(8,128)(2,1)}), bf16[64,2048]{1,0:T(8,128)(2,1)}) %reduce-scatter.12.cloned.1.call-update) | async-done | bytes 262160 | tf_op jit(solution)/shard_map/reduce_scatter | solution.py:837
  865.7 95.8 %reduce-scatter.8.cloned.1.call-done = bf16[2,128,2048]{2,1,0:T(8,128)(2,1)} async-done(((bf16[2,1024,2048]{2,1,0:T(8,128)(2,1)}), bf16[2,128,2048]{2,1,0:T(8,128)(2,1)}) %reduce-scatter.8.cloned.1.call-update) | async-done | bytes 1048592 | tf_op jit(solution)/shard_map/reduce_scatter | solution.py:877
  963.5 88.5 %reduce-scatter.6.cloned.1.call-done = bf16[2,128,2048]{2,1,0:T(8,128)(2,1)} async-done(((bf16[2,1024,2048]{2,1,0:T(8,128)(2,1)}), bf16[2,128,2048]{2,1,0:T(8,128)(2,1)}) %reduce-scatter.6.cloned.1.call-update) | async-done | bytes 1048592 | tf_op jit(solution)/shard_map/reduce_scatter | solution.py:822
  1051.9 4.0 fusion.44
  1056.0 4.8 reshape.448
  1060.7 2.7 slice.245
  1063.5 2.5 slice.243
  1067.3 2.5 copy.176
  (175 shorter events, 40.4 us)
Async XLA Ops:
  7.2 288.0 %all-gather.3.cloned.1.call-start = ((), (), s32[]{:S(2)}) async-start(), calls=%async_computation.11 | async-start | bytes 9437184 | tf_op jit(solution)/shard_map/all_gather | solution.py:769
  7.9 515.1 %reduce-scatter.10.cloned.1.call-start = ((), (), s32[]{:S(2)}) async-start(), calls=%async_computation.8 | async-start | bytes 9175040 | tf_op jit(solution)/shard_map/reduce_scatter | solution.py:869
  218.4 53.7 %copy-start.23 = (bf16[4,8,16,128]{3,1,2,0:T(8,128)(2,1)}, bf16[4,8,16,128]{3,1,2,0:T(8,128)(2,1)S(1)}, u32[]{:S(2)}) copy-start(bf16[4,8,16,128]{3,1,2,0:T(8,128)(2,1)S(1)} %copy.183) | copy-start | bytes 393220
  218.6 16.2 %copy-start.25 = (f32[2048]{0:T(1024)}, f32[2048]{0:T(1024)S(1)}, u32[]{:S(2)}) copy-start(f32[2048]{0:T(1024)S(1)} %reshape.441) | copy-start | bytes 24580
  218.7 16.1 %copy-start.27 = (f32[2048]{0:T(1024)}, f32[2048]{0:T(1024)S(1)}, u32[]{:S(2)}) copy-start(f32[2048]{0:T(1024)S(1)} %reshape.442) | copy-start | bytes 24580
  218.7 16.0 %copy-start.29 = (f32[2048]{0:T(1024)}, f32[2048]{0:T(1024)S(1)}, u32[]{:S(2)}) copy-start(f32[2048]{0:T(1024)S(1)} %reshape.444) | copy-start | bytes 24580
  218.8 16.0 %copy-start.31 = (f32[2048]{0:T(1024)}, f32[2048]{0:T(1024)S(1)}, u32[]{:S(2)}) copy-start(f32[2048]{0:T(1024)S(1)} %reshape.445) | copy-start | bytes 24580
  224.1 10.6 slice-start
  228.9 5.9 slice-start.1
  234.8 7.3 copy-start.13
  261.4 12.1 %copy-start.37 = (s32[2,1]{0,1:T(1,128)S(1)}, s32[2,1]{0,1:T(1,128)}, u32[]{:S(2)}) copy-start(s32[2,1]{0,1:T(1,128)} %param.17) | copy-start | bytes 28
  277.1 7.4 copy-start.8
  282.1 35.8 %copy-start.6 = (bf16[2,1024,3,256]{3,1,0,2:T(8,128)(2,1)}, bf16[2,1024,3,256]{3,1,0,2:T(8,128)(2,1)S(1)}, u32[]{:S(2)}) copy-start(bf16[2,1024,3,256]{3,1,0,2:T(8,128)(2,1)S(1)} %get-tuple-element.107) | copy-start | bytes 9437188
  295.1 36.5 %copy-start.33 = (f32[2,1024]{1,0:T(2,128)}, f32[2,1024]{1,0:T(2,128)S(1)}, u32[]{:S(2)}) copy-start(f32[2,1024]{1,0:T(2,128)S(1)} %get-tuple-element.148) | copy-start | bytes 24580
  310.5 4.0 copy-start.24
  322.8 4.8 copy-start.18
  322.8 4.8 copy-start.21
  322.8 4.8 copy-start.22
  327.7 3.9 slice-start.4
  327.7 3.9 copy-start.16
  329.2 3.0 slice-start.5
  332.2 2.0 copy-start.14
  333.5 3.5 copy-start.11
  342.6 13.1 %copy-start.10 = (bf16[4,256,2048]{2,1,0:T(8,128)(2,1)S(1)}, bf16[4,256,2048]{2,1,0:T(8,128)(2,1)}, u32[]{:S(2)}) copy-start(bf16[4,256,2048]{2,1,0:T(8,128)(2,1)} %copy.138) | copy-start | bytes 12582916
  342.6 47.2 %slice-start.2 = ((s8[8388608]{0:T(1024)(128)(4,1)}), s8[4194304]{0:T(1024)(128)(4,1)S(1)}, s32[]{:S(2)}) async-start(s8[8388608]{0:T(1024)(128)(4,1)} %bitcast.175), calls=%async_computation.15 | async-start | bytes 8388608
  355.7 34.1 %slice-start.3 = ((s8[8388608]{0:T(1024)(128)(4,1)}), s8[4194304]{0:T(1024)(128)(4,1)S(1)}, s32[]{:S(2)}) async-start(s8[8388608]{0:T(1024)(128)(4,1)} %bitcast.175), calls=%async_computation.16 | async-start | bytes 8388608
  355.7 34.1 %copy-start.26 = (f32[2048]{0:T(1024)S(1)}, f32[2048]{0:T(1024)}, u32[]{:S(2)}) copy-start(f32[2048]{0:T(1024)} %copy-done.25) | copy-start | bytes 24580
  355.7 34.1 %copy-start.28 = (f32[2048]{0:T(1024)S(1)}, f32[2048]{0:T(1024)}, u32[]{:S(2)}) copy-start(f32[2048]{0:T(1024)} %copy-done.27) | copy-start | bytes 24580
  355.7 34.1 %copy-start.30 = (f32[2048]{0:T(1024)S(1)}, f32[2048]{0:T(1024)}, u32[]{:S(2)}) copy-start(f32[2048]{0:T(1024)} %copy-done.29) | copy-start | bytes 24580
  355.7 34.1 %copy-start.32 = (f32[2048]{0:T(1024)S(1)}, f32[2048]{0:T(1024)}, u32[]{:S(2)}) copy-start(f32[2048]{0:T(1024)} %copy-done.31) | copy-start | bytes 24580
  355.7 34.1 %copy-start.35 = (f32[2048]{0:T(1024)S(1)}, f32[2048]{0:T(1024)}, u32[]{:S(2)}) copy-start(f32[2048]{0:T(1024)} %get-tuple-element.154) | copy-start | bytes 24580
  355.8 34.1 %copy-start.36 = (f32[2048]{0:T(1024)S(1)}, f32[2048]{0:T(1024)}, u32[]{:S(2)}) copy-start(f32[2048]{0:T(1024)} %get-tuple-element.155) | copy-start | bytes 24580
  415.5 14.1 %copy-start.3 = (bf16[2,1024,1,256]{3,1,0,2:T(8,128)(2,1)S(1)}, bf16[2,1024,1,256]{3,1,0,2:T(8,128)(2,1)}, u32[]{:S(2)}) copy-start(bf16[2,1024,1,256]{3,1,0,2:T(8,128)(2,1)} %copy-done.2) | copy-start | bytes 3145732
  415.5 14.1 %copy-start.5 = (bf16[2,1024,1,256]{3,1,0,2:T(8,128)(2,1)S(1)}, bf16[2,1024,1,256]{3,1,0,2:T(8,128)(2,1)}, u32[]{:S(2)}) copy-start(bf16[2,1024,1,256]{3,1,0,2:T(8,128)(2,1)} %copy-done.4) | copy-start | bytes 3145732
  415.5 14.1 %copy-start.12 = (bf16[2,1024,256]{2,1,0:T(8,128)(2,1)S(1)}, bf16[2,1024,256]{2,1,0:T(8,128)(2,1)}, u32[]{:S(2)}) copy-start(bf16[2,1024,256]{2,1,0:T(8,128)(2,1)} %copy-done.11) | copy-start | bytes 3145732
  415.5 14.1 %copy-start.39 = (bf16[2048,2048]{1,0:T(8,128)(2,1)S(1)}, bf16[2048,2048]{1,0:T(8,128)(2,1)}, u32[]{:S(2)}) copy-start(bf16[2048,2048]{1,0:T(8,128)(2,1)} %get-tuple-element.113) | copy-start | bytes 25165828
  437.9 6.5 copy-start.34
  444.4 9.0 copy-start.1
  444.4 218.4 %all-reduce.4.cloned.1.call-start = ((), (), s32[]{:S(2)}) async-start(), calls=%async_computation.12 | async-start | bytes 196608
  456.5 9.3 copy-start.15
  465.7 253.5 %reduce-scatter.14.cloned.1.call-start = ((), (), s32[]{:S(2)}) async-start(), calls=%async_computation.10 | async-start | bytes 5242880 | tf_op jit(solution)/shard_map/reduce_scatter | solution.py:834
  480.5 2.3 copy-start.7
  485.2 378.8 %reduce-scatter.12.cloned.1.call-start = ((), (), s32[]{:S(2)}) async-start(), calls=%async_computation.9 | async-start | bytes 8650752 | tf_op jit(solution)/shard_map/reduce_scatter | solution.py:837
  491.9 469.7 %reduce-scatter.8.cloned.1.call-start = ((), (), s32[]{:S(2)}) async-start(), calls=%async_computation.7 | async-start | bytes 9437184 | tf_op jit(solution)/shard_map/reduce_scatter | solution.py:877
  492.4 559.5 %reduce-scatter.6.cloned.1.call-start = ((), (), s32[]{:S(2)}) async-start(), calls=%async_computation.6 | async-start | bytes 9437184 | tf_op jit(solution)/shard_map/reduce_scatter | solution.py:822
  509.2 24.2 %copy-start = (bf16[2,1,128,2048]{3,2,1,0:T(8,128)(2,1)S(1)}, bf16[2,1,128,2048]{3,2,1,0:T(8,128)(2,1)}, u32[]{:S(2)}) copy-start(bf16[2,1,128,2048]{3,2,1,0:T(8,128)(2,1)} %param.15) | copy-start | bytes 3145732
  526.8 529.2 %all-to-all-start = ((bf16[8,64,1792]{2,1,0:T(8,128)(2,1)}), bf16[8,64,1792]{2,1,0:T(8,128)(2,1)}, u32[]{:S(2)}, u32[]{:S(2)}) async-start(bf16[8,64,1792]{2,1,0:T(8,128)(2,1)} %bitcast.193), calls=%async_computation.3 | async-start | bytes 3670016 | tf_op jit(solution)/shard_map/all_to_all | solution.py:870
  664.2 408.1 %copy-start.38 = (f32[64]{0:T(128)}, f32[64]{0:T(128)S(1)}, u32[]{:S(2)}) copy-start(f32[64]{0:T(128)S(1)} %get-tuple-element.181) | copy-start | bytes 772
  (6 other events, 8.8 us)
Sparse Core Ops, SparseCore 0:
  9.6 142.6 all-gather.2
  444.5 78.4 reduce-scatter.9
  529.1 133.5 all-reduce.3
  665.6 53.5 reduce-scatter.13
  721.4 142.4 reduce-scatter.11
  866.2 95.3 reduce-scatter.7
  963.9 87.9 reduce-scatter.5

commit v3 on v2

--- a/solution.py
+++ b/solution.py
@@ -728,6 +728,507 @@
     )(x, qkv, expand, dense, shrink, packed)
 
 
+def add_into(dst, srcs, rows):
+    chunk = 16 if dst.shape[-1] > 1024 else 64
+
+    def step(index, carry):
+        at = pl.ds(pl.multiple_of(index * chunk, 16), chunk)
+        total = srcs[0][at, :].astype(jnp.float32)
+        for src in srcs[1:]:
+            total = total + src[at, :].astype(jnp.float32)
+        dst[at, :] = total.astype(dst.dtype)
+        return carry
+
+    lax.fori_loop(0, rows // chunk, step, 0)
+
+
+def reduce_kernel(
+    dp_size,
+    ctx_size,
+    back,
+    qkv_grads,
+    expand_grads,
+    out_grads,
+    board,
+    back_out,
+    panel_out,
+    shrink_out,
+    dense_out,
+    tail_out,
+    back_own,
+    back_core,
+    back_chain,
+    panel_own,
+    panel_recv,
+    panel_last,
+    shrink_own,
+    shrink_recv,
+    shrink_last,
+    dense_own,
+    dense_recv,
+    board_recv,
+    load_sem,
+    core_send,
+    core_recv,
+    chain_send,
+    chain_recv,
+    first_send,
+    first_recv,
+    last_send,
+    last_recv,
+    out_send,
+    out_recv,
+    dense_send,
+    dense_sem,
+    board_sem,
+    store_sem,
+):
+    d = lax.axis_index("dp")
+    c = lax.axis_index("ctx")
+    z = c // 2
+    core = lax.rem(c, 2)
+    sibling = c + 1 - 2 * core
+    x_mate = d + 1 - 2 * lax.rem(d, 2)
+    y_mate = lax.rem(d + 2, 4)
+    diagonal = 3 - d
+    micro = back.shape[0]
+    span = back.shape[1] // ctx_size
+    levels = ctx_size // 2
+    devices = dp_size * ctx_size
+    me = d * ctx_size + c
+    n_panels = 3 + dp_size
+    group_rows = qkv_grads.shape[0] // dp_size
+    half = group_rows // 2
+    rows = group_rows // ctx_size
+    unit = (out_grads.shape[0] - HEAD) // dp_size
+    shrink_half = unit // 2
+    head_half = HEAD // 2
+
+    greet_all(d, c, dp_size, ctx_size)
+
+    def back_view(parity, level, m):
+        start = (2 * level + parity) * span
+        return back.at[m, pl.ds(pl.multiple_of(start, span), span)]
+
+    def back_load(level, m):
+        return pltpu.make_async_copy(back_view(core, level, m), back_own.at[level, m], load_sem.at[0, level * micro + m])
+
+    def core_copy(level, m):
+        return remote(
+            back_view(1 - core, level, m),
+            back_core.at[level, m],
+            core_send.at[level, m],
+            core_recv.at[level, m],
+            d,
+            sibling,
+        )
+
+    order = []
+    for pair in range((levels + 1) // 2):
+        for level in (levels - 1 - pair, pair):
+            if level not in order:
+                order.append(level)
+    for level in order:
+        for m in range(micro):
+            core_copy(level, m).start()
+            back_load(level, m).start()
+
+    mates = ((x_mate, y_mate), (y_mate, x_mate))
+
+    def panel_view(panel, owner, way):
+        at = pl.ds(pl.multiple_of(owner * group_rows + way * half, 16), half)
+        if panel < 3:
+            return qkv_grads.at[at, pl.ds(panel * HEAD, HEAD)]
+        return expand_grads.at[at, pl.ds((panel - 3) * HEAD, HEAD)]
+
+    def shrink_view(owner, way):
+        return out_grads.at[pl.ds(pl.multiple_of(HEAD + owner * unit + way * shrink_half, 16), shrink_half)]
+
+    def first_copies(index, view, recv):
+        copies = []
+        for way in range(2):
+            mate = mates[way][0]
+            for slot, owner in ((0, mate), (1, diagonal)):
+                copies.append(
+                    remote(
+                        view(owner, way),
+                        recv.at[way, slot],
+                        first_send.at[index, way, slot],
+                        first_recv.at[index, way, slot],
+                        mate,
+                        c,
+                    )
+                )
+        return copies
+
+    def own_loads(index, view, own):
+        copies = []
+        for way in range(2):
+            for slot, owner in ((0, d), (1, mates[way][1])):
+                copies.append(
+                    pltpu.make_async_copy(view(owner, way), own.at[way, slot], load_sem.at[1 + index, way * 2 + slot])
+                )
+        return copies
+
+    def last_copies(index, own, last):
+        return [
+            remote(
+                own.at[way, 1], last.at[way], last_send.at[index, way], last_recv.at[index, way], mates[way][1], c
+            )
+            for way in range(2)
+        ]
+
+    def unit_parts(index):
+        if index < n_panels:
+            return (
+                functools.partial(panel_view, index),
+                panel_own.at[index],
+                panel_recv.at[index],
+                panel_last.at[index],
+                half,
+            )
+        return shrink_view, shrink_own, shrink_recv, shrink_last, shrink_half
+
+    def open_unit(index):
+        view, own, recv, last, count = unit_parts(index)
+        for copy in first_copies(index, view, recv) + own_loads(index, view, own):
+            copy.start()
+
+    def first_step(index):
+        view, own, recv, last, count = unit_parts(index)
+        arrivals = first_copies(index, view, recv)
+        loads = own_loads(index, view, own)
+        sends = last_copies(index, own, last)
+        for way in range(2):
+            arrivals[way * 2 + 1].wait_recv()
+            loads[way * 2 + 1].wait()
+            add_into(own.at[way, 1], (own.at[way, 1], recv.at[way, 1]), count)
+            sends[way].start()
+
+    def last_step(index):
+        view, own, recv, last, count = unit_parts(index)
+        arrivals = first_copies(index, view, recv)
+        loads = own_loads(index, view, own)
+        ends = last_copies(index, own, last)
+        for way in range(2):
+            arrivals[way * 2].wait_recv()
+            loads[way * 2].wait()
+            ends[way].wait_recv()
+            add_into(own.at[way, 0], (own.at[way, 0], recv.at[way, 0], last.at[way]), count)
+
+    def close_unit(index):
+        view, own, recv, last, count = unit_parts(index)
+        for copy in first_copies(index, view, recv) + last_copies(index, own, last):
+            copy.wait_send()
+
+    per_half = half // rows
+
+    def panel_chunk(panel, target):
+        start = pl.multiple_of(lax.rem(target, per_half) * rows, rows)
+        return panel_own.at[panel, target // per_half, 0, pl.ds(start, rows)]
+
+    def panel_local(panel):
+        return pltpu.make_async_copy(panel_chunk(panel, c), panel_out.at[panel, c], store_sem.at[panel])
+
+    def send_panel(panel):
+        def push(step, carry):
+            target = lax.rem(c + step, ctx_size)
+            remote(
+                panel_chunk(panel, target), panel_out.at[panel, c], out_send.at[panel], out_recv.at[panel], d, target
+            ).start()
+            return carry
+
+        lax.fori_loop(1, ctx_size, push, 0)
+        panel_local(panel).start()
+
+    def end_panel(panel):
+        rest = panel_out.at[panel, pl.ds(0, ctx_size - 1)]
+        remote(rest, rest, out_send.at[panel], out_recv.at[panel], d, sibling).wait()
+        panel_local(panel).wait()
+
+    source = c // (ctx_size // dp_size)
+    at_source = d == source
+    from_x = x_mate == source
+    from_y = y_mate == source
+    across = diagonal == source
+    per_head = HEAD // rows
+
+    def dense_half(way):
+        return out_grads.at[pl.ds(way * head_half, head_half)]
+
+    def dense_copy(way, src, slot, mate):
+        return remote(src, dense_recv.at[slot], dense_send.at[way], dense_sem.at[slot], mate, c)
+
+    dense_load = pltpu.make_async_copy(out_grads.at[pl.ds(0, HEAD)], dense_own, load_sem.at[0, levels * micro])
+    dense_load.start()
+
+    @pl.when(across)
+    def _():
+        dense_copy(0, dense_half(0), 0, y_mate).start()
+        dense_copy(1, dense_half(1), 0, x_mate).start()
+
+    def middle(mate, mine, axis):
+        own = dense_own.at[pl.ds(mine * head_half, head_half)]
+        dense_copy(1 - mine, dense_half(1 - mine), 1 + 2 * axis + 1 - mine, mate).start()
+        dense_copy(mine, own, 0, mate).wait_recv()
+        add_into(own, (own, dense_recv.at[0]), head_half)
+        dense_copy(mine, own, 1 + 2 * axis + mine, mate).start()
+
+    def dense_chunk(piece):
+        return dense_own.at[pl.ds(piece * rows, rows)]
+
+    first_owner = lax.rem(c, ctx_size // per_head) * per_head
+
+    def dense_send_out(piece):
+        return remote(
+            dense_chunk(piece), dense_out, dense_send.at[2 + piece], dense_sem.at[5], d, first_owner + piece
+        )
+
+    def dense_store(piece):
+        return pltpu.make_async_copy(dense_chunk(piece), dense_out, store_sem.at[n_panels])
+
+    board_load = pltpu.make_async_copy(board.at[me], board_recv.at[me], load_sem.at[0, levels * micro + 1])
+    board_load.start()
+
+    def push_board(step, carry):
+        other = lax.rem(me + step, devices)
+        remote(
+            board.at[other],
+            board_recv.at[me],
+            board_sem.at[0],
+            board_sem.at[1],
+            other // ctx_size,
+            lax.rem(other, ctx_size),
+        ).start()
+        return carry
+
+    lax.fori_loop(1, devices, push_board, 0)
+
+    for index in range(n_panels):
+        open_unit(index)
+
+    for level in order:
+        for m in range(micro):
+            back_load(level, m).wait()
+            core_copy(level, m).wait_recv()
+            add_into(back_own.at[level, m], (back_own.at[level, m], back_core.at[level, m]), span)
+
+    def chain_copy(way, level, m):
+        return remote(
+            back_own.at[level, m],
+            back_chain.at[way, level, m],
+            chain_send.at[way, level, m],
+            chain_recv.at[way, level, m],
+            d,
+            c + (2 if way == 0 else -2),
+        )
+
+    def sends(way, level):
+        return z < level if way == 0 else z > level
+
+    def hears(way, level):
+        if way == 0:
+            return jnp.logical_and(z >= 1, z <= level)
+        return jnp.logical_and(z <= levels - 2, z >= level)
+
+    def chain_step(way, level):
+        for m in range(micro):
+            @pl.when(jnp.logical_and(sends(way, level), hears(way, level)))
+            def _(m=m):
+                chain_copy(way, level, m).wait_recv()
+                add_into(back_own.at[level, m], (back_own.at[level, m], back_chain.at[way, level, m]), span)
+
+            @pl.when(sends(way, level))
+            def _(m=m):
+                chain_copy(way, level, m).start()
+
+    def chain_end():
+        for level in range(levels):
+            for m in range(micro):
+                for way in range(2):
+                    @pl.when(jnp.logical_and(z == level, hears(way, level)))
+                    def _(way=way, level=level, m=m):
+                        chain_copy(way, level, m).wait_recv()
+                        add_into(back_own.at[level, m], (back_own.at[level, m], back_chain.at[way, level, m]), span)
+
+                @pl.when(z == level)
+                def _(level=level, m=m):
+                    pltpu.make_async_copy(back_own.at[level, m], back_out.at[m], store_sem.at[n_panels + 2 + m]).start()
+
+    chain_step(0, levels - 1)
+    chain_step(1, 0)
+    first_step(0)
+    first_step(1)
+    dense_load.wait()
+
+    @pl.when(from_x)
+    def _():
+        middle(x_mate, 0, 0)
+
+    @pl.when(from_y)
+    def _():
+        middle(y_mate, 1, 1)
+
+    first_step(2)
+    last_step(0)
+    send_panel(0)
+    chain_step(0, levels - 2)
+    chain_step(1, 1)
+    first_step(3)
+    last_step(1)
+    send_panel(1)
+    open_unit(n_panels)
+    first_step(4)
+    last_step(2)
+    send_panel(2)
+
+    @pl.when(at_source)
+    def _():
+        for slot in range(1, 5):
+            dense_copy(0, dense_half(0), slot, x_mate).wait_recv()
+        for way in range(2):
+            own = dense_own.at[pl.ds(way * head_half, head_half)]
+            add_into(own, (own, dense_recv.at[1 + way], dense_recv.at[3 + way]), head_half)
+        for piece in range(per_head):
+            @pl.when(first_owner + piece == c)
+            def _(piece=piece):
+                dense_store(piece).start()
+
+            @pl.when(first_owner + piece != c)
+            def _(piece=piece):
+                dense_send_out(piece).start()
+
+    first_step(5)
+    last_step(3)
+    send_panel(3)
+    chain_step(0, levels - 3)
+    chain_step(1, 2)
+    first_step(6)
+    last_step(4)
+    send_panel(4)
+    last_step(5)
+    send_panel(5)
+    last_step(6)
+    send_panel(6)
+    first_step(n_panels)
+    chain_end()
+    last_step(n_panels)
+    for way in range(2):
+        pltpu.make_async_copy(
+            shrink_own.at[way, 0],
+            shrink_out.at[pl.ds(way * shrink_half, shrink_half)],
+            store_sem.at[n_panels + 2 + micro + way],
+        ).start()
+
+    board_load.wait()
+    rest = board_recv.at[pl.ds(0, devices - 1)]
+    remote(rest, rest, board_sem.at[0], board_sem.at[1], d, sibling).wait()
+    tail_out[...] = jnp.sum(board_recv[...], axis=0)
+
+    for index in range(n_panels + 1):
+        close_unit(index)
+    for panel in range(n_panels):
+        end_panel(panel)
+    for level in range(levels):
+        for m in range(micro):
+            core_copy(level, m).wait_send()
+            for way in range(2):
+                @pl.when(sends(way, level))
+                def _(way=way, level=level, m=m):
+                    chain_copy(way, level, m).wait_send()
+
+    @pl.when(jnp.logical_not(at_source))
+    def _():
+        dense_copy(0, dense_half(0), 0, x_mate).wait_send()
+        dense_copy(1, dense_half(1), 0, x_mate).wait_send()
+
+    for piece in range(per_head):
+        @pl.when(jnp.logical_and(at_source, first_owner + piece != c))
+        def _(piece=piece):
+            dense_send_out(piece).wait_send()
+
+    stays = me // per_head == c
+
+    @pl.when(stays)
+    def _():
+        dense_store(0).wait()
+
+    @pl.when(jnp.logical_not(stays))
+    def _():
+        dense_send_out(0).wait_recv()
+
+    for m in range(micro):
+        pltpu.make_async_copy(back_own.at[0, m], back_out.at[m], store_sem.at[n_panels + 2 + m]).wait()
+    for way in range(2):
+        pltpu.make_async_copy(
+            shrink_own.at[way, 0],
+            shrink_out.at[pl.ds(way * shrink_half, shrink_half)],
+            store_sem.at[n_panels + 2 + micro + way],
+        ).wait()
+
+
+def reduce_call(dp_size, ctx_size, back, qkv_grads, expand_grads, out_grads, board):
+    micro, length, width = back.shape
+    span = length // ctx_size
+    n_panels = 3 + dp_size
+    group_rows = qkv_grads.shape[0] // dp_size
+    half = group_rows // 2
+    rows = group_rows // ctx_size
+    unit = (out_grads.shape[0] - HEAD) // dp_size
+    levels = ctx_size // 2
+    devices = dp_size * ctx_size
+    dma = pltpu.SemaphoreType.DMA
+    kind = back.dtype
+    vmem = pltpu.VMEM
+    out_shape = (
+        jax.ShapeDtypeStruct((micro, span, width), kind),
+        jax.ShapeDtypeStruct((n_panels, ctx_size, rows, HEAD), kind),
+        jax.ShapeDtypeStruct((unit, width), kind),
+        jax.ShapeDtypeStruct((HEAD // (HEAD // rows), width), kind),
+        jax.ShapeDtypeStruct(board.shape[1:], jnp.float32),
+    )
+    anywhere = pl.BlockSpec(memory_space=pl.ANY)
+    return pl.pallas_call(
+        functools.partial(reduce_kernel, dp_size, ctx_size),
+        out_shape=out_shape,
+        in_specs=[anywhere] * 5,
+        out_specs=(anywhere,) * 4 + (pl.BlockSpec(memory_space=pltpu.VMEM),),
+        scratch_shapes=[
+            vmem((levels, micro, span, width), kind),
+            vmem((levels, micro, span, width), kind),
+            vmem((2, levels, micro, span, width), kind),
+            vmem((n_panels, 2, 2, half, HEAD), kind),
+            vmem((n_panels, 2, 2, half, HEAD), kind),
+            vmem((n_panels, 2, half, HEAD), kind),
+            vmem((2, 2, unit // 2, width), kind),
+            vmem((2, 2, unit // 2, width), kind),
+            vmem((2, unit // 2, width), kind),
+            vmem((HEAD, width), kind),
+            vmem((5, HEAD // 2, width), kind),
+            vmem((devices,) + board.shape[1:], jnp.float32),
+            dma((n_panels + 2, levels * micro + 2)),
+            dma((levels, micro)),
+            dma((levels, micro)),
+            dma((2, levels, micro)),
+            dma((2, levels, micro)),
+            dma((n_panels + 1, 2, 2)),
+            dma((n_panels + 1, 2, 2)),
+            dma((n_panels + 1, 2)),
+            dma((n_panels + 1, 2)),
+            dma((n_panels,)),
+            dma((n_panels,)),
+            dma((2 + HEAD // rows,)),
+            dma((6,)),
+            dma((2,)),
+            dma((n_panels + 4 + micro,)),
+        ],
+        compiler_params=pltpu.CompilerParams(
+            collective_id=2, has_side_effects=True, vmem_limit_bytes=56 * 1024 * 1024
+        ),
+        name="reduce_all",
+    )(back, qkv_grads, expand_grads, out_grads, board)
+
+
 def tensor_shards(
     layer_input,
     out_grad,
@@ -831,12 +1332,6 @@
     unused, gelu_back = jax.vjp(gelu_exact, expanded)
     grad_expanded = low(gelu_back(grad_features[:, HEAD:])[0])
     grad_mixed = low(grad_features[:, :HEAD]).reshape(sequences, SEQ, HEAD)
-    shrink_grad = lax.psum_scatter(out_grads[HEAD:], "dp", scatter_dimension=0, tiled=True)
-    dense_own = jnp.zeros((ctx_size, HEAD, width), jnp.bfloat16)
-    dense_own = lax.dynamic_update_slice(dense_own, out_grads[:HEAD][None], (me, 0, 0))
-    dense_grad = lax.psum_scatter(
-        dense_own.reshape(ctx_size * HEAD, width), ("dp", "ctx"), scatter_dimension=0, tiled=True
-    )
     expand_grads = low(contract_rows(hidden_mlp, grad_expanded))
     back_mlp = jnp.einsum(
         "tpe,pde->td",
@@ -865,29 +1360,7 @@
         qkv_part,
         preferred_element_type=jnp.float32,
     )
-    column_grads = jnp.concatenate([qkv_grads, expand_grads], axis=1)
-    column_grads = lax.psum_scatter(column_grads, "dp", scatter_dimension=0, tiled=True)
-    column_grads = lax.all_to_all(column_grads, "ctx", split_axis=0, concat_axis=0, tiled=True)
-    column_grads = column_grads.reshape(ctx_size, row_share, 3 + dp_size, HEAD)
-    column_grads = jnp.transpose(column_grads, (1, 2, 0, 3)).astype(jnp.float32)
-    qkv_grad = column_grads[:, :3].reshape(row_share, 3 * width)
-    expand_grad = column_grads[:, 3:].reshape(row_share, ff)
-
     combined = low(back_attn * gain_attn + back_mlp * gain_mlp)
-    combined = lax.psum_scatter(
-        combined.reshape(sequences, SEQ, width), "ctx", scatter_dimension=1, tiled=True
-    ).astype(jnp.float32)
-    own = own_x.astype(jnp.float32)
-    own_center = own - jnp.mean(own, axis=-1, keepdims=True)
-    own_spread = lax.rsqrt(jnp.mean(own_center * own_center, axis=-1, keepdims=True) + 1e-05)
-    own_normal = own_center * own_spread
-    share = own_spread * (
-        combined
-        - jnp.mean(combined, axis=-1, keepdims=True)
-        - own_normal * jnp.mean(combined * own_normal, axis=-1, keepdims=True)
-    )
-    input_grad = low(own_g.astype(jnp.float32) + share).reshape(layer_input.shape)
-
     def place(values, parts):
         board = jnp.zeros((parts, ctx_size, values.shape[0] // parts), jnp.float32)
         board = lax.dynamic_update_slice(board, values.reshape(parts, 1, -1), (0, me, 0))
@@ -909,7 +1382,27 @@
         ],
         axis=1,
     )
-    tail = lax.psum_scatter(board, ("dp", "ctx"), scatter_dimension=0, tiled=True).reshape(-1)
+    used = board.shape[1]
+    board = jnp.pad(board, ((0, 0), (0, -used % 1024))).reshape(devices, -1, 128)
+    combined, panel_grads, shrink_grad, dense_grad, tail = reduce_call(
+        dp_size, ctx_size, combined.reshape(sequences, SEQ, width), qkv_grads, expand_grads, out_grads, board
+    )
+    combined = combined.astype(jnp.float32)
+    panel_grads = jnp.transpose(panel_grads.astype(jnp.float32), (2, 0, 1, 3))
+    qkv_grad = panel_grads[:, :3].reshape(row_share, 3 * width)
+    expand_grad = panel_grads[:, 3:].reshape(row_share, ff)
+    own = own_x.astype(jnp.float32)
+    own_center = own - jnp.mean(own, axis=-1, keepdims=True)
+    own_spread = lax.rsqrt(jnp.mean(own_center * own_center, axis=-1, keepdims=True) + 1e-05)
+    own_normal = own_center * own_spread
+    share = own_spread * (
+        combined
+        - jnp.mean(combined, axis=-1, keepdims=True)
+        - own_normal * jnp.mean(combined * own_normal, axis=-1, keepdims=True)
+    )
+    input_grad = low(own_g.astype(jnp.float32) + share).reshape(layer_input.shape)
+
+    tail = tail.reshape(-1)
     share_len = width // devices
     at = 0
     pieces = []

time: 1090 us -> 668 us (0.61)
  the two profiles are of different devices: /device:TPU:9 before, /device:TPU:8 now
where the time goes in v3:
time: 668 us; the launch traced here: 659 us
  Pallas kernels  361 us (54%)
  matrix products  175 us (26%)
  local copies, waits for them, and re-layouts  54.9 us (8%)
  other arithmetic  52.5 us (8%)
  between operations  15.2 us (2%)
    pallas_call x1, Pallas kernels, gather_call(): pl.pallas_call(functools.partial(gather_kernel, dp_size, ctx_size), out_s...  204 us
    pallas_call x1, Pallas kernels, reduce_call(): pl.pallas_call(functools.partial(reduce_kernel, dp_size, ctx_size), out_s...  157 us
    dot_general x3, matrix products, contract_rows(): lax.dot_general(left_mat, right_mat, (((0,), (0,)), ((), ())), preferred_...  37 us
    dot_general x1, matrix products, tensor_shards(): jnp.einsum('td,pde->tpe', hidden_mlp, expand_part, preferred_element_type...  34.3 us
    dot_general x1, matrix products, tensor_shards(): jnp.einsum('tpe,pde->td', grad_expanded.reshape(tokens, -1, HEAD), expand...  25.7 us
    dot_general x1, matrix products, tensor_shards(): jnp.dot(features, out_part, preferred_element_type=jnp.float32)  17.2 us
    dot_general x1, matrix products, contract_cols(): lax.dot_general(left_mat, right_mat, (((1,), (1,)), ((), ())), preferred_...  15.2 us
    convert_element_type x3, other arithmetic, low(): return values.astype(jnp.bfloat16)  14.1 us
  transfers between devices with their start and end apart: 2, of which 0 were waited for; matrix products, arithmetic and copies ran while one was open for 31% of the time, Pallas kernels for 55%

profile of v3, /device:TPU:8, one launch (start us, length us, event | category | flops | bytes accessed | tf_op | source)
XLA Modules:
  0.0 658.7 jit_solution(3245691175787007726)
XLA Ops:
  7.2 0.7 all-gather.3.cloned.1.call-update
  8.0 1.4 convert_reduce_fusion.5
  10.0 5.4 concatenate.37
  16.0 204.0 %gather_all.1 = (bf16[2,1024,2048]{2,1,0:T(8,128)(2,1)}, bf16[7,2048,256]{2,1,0:T(8,128)(2,1)}, bf16[1280,2048]{1,0:T(8,128)(2,1)}, bf16[32,16,128]{2,1,0:T(8,128)(2,1)}) custom-call(bf16[2,128,2048]{2,1,0:T(8,128)(2,1)} %bitcast.165, bf16[64,6144]{1,0:T(8,128)(2,1)} %qkv.1, bf16[64,8192]{1,0:T(8,128)(2,1)} %expand.1, bf16[64,2048]{1,0:T(8,128)(2,1)} %dense.1, ...), custom_call_target="tpu_custom_call" | custom-call | tf_op jit(solution)/shard_map/gather_all/pallas_call | solution.py:707
  220.0 0.9 copy.105
  222.2 2.1 slice_bitcast_fusion.1
  224.3 3.1 copy.50
  227.4 4.5 slice_bitcast_fusion
  231.9 6.3 copy.58
  238.2 4.7 convert_reduce_fusion
  242.9 5.8 multiply_reduce_fusion
  248.9 7.3 %add_convert_fusion.3 = (bf16[2,1024,2048]{2,1,0:T(8,128)(2,1)S(1)}, bf16[2,1024,2048]{2,1,0:T(8,128)(2,1)}) fusion(bf16[2,1024,2048]{2,1,0:T(8,128)(2,1)S(1)} %bitcast.164, f32[2048]{0:T(1024)S(1)} %reshape.433, f32[2048]{0:T(1024)S(1)} %reshape.432, f32[2,1024]{1,0:T(2,128)S(1)} %get-tuple-element.102, f32[2,1024]{1,0:T(2,128)S(1)} %get-tuple-element.100, ...), kind=kLoop, calls=%fused_computation.16 | loop fusion | flops 37748736 | bytes 25214976 | tf_op jit(solution)/shard_map/convert_element_type | solution.py:324
  256.2 8.6 %broadcast_add_fusion = f32[2048,768]{1,0:T(8,128)} fusion(f32[768]{0:T(1024)S(1)} %add.127, bf16[2048,2048]{1,0:T(8,128)(2,1)S(1)} %bitcast.177, bf16[768,2048]{1,0:T(8,128)(2,1)S(1)} %bitcast.183), kind=kOutput, calls=%fused_computation.66 | convolution fusion | flops 6444023808 | bytes 17828864 | tf_op jit(solution)/shard_map/td,pde->tpe/dot_general | solution.py:1295
  264.8 10.8 %reshape.445 = f32[2,1024,3,256]{3,2,1,0:T(4,128)} reshape(f32[2048,768]{1,0:T(8,128)} %broadcast_add_fusion) | data formatting | bytes 12582912 | tf_op jit(solution)/shard_map/reshape | solution.py:1297
  276.0 3.0 fusion.50
  279.0 5.0 fusion.59
  284.1 1.0 fusion.60
  285.1 2.1 subtract_convert_fusion.1
  287.2 8.0 %fusion.62 = (f32[2,1024]{1,0:T(2,128)S(1)}, f32[2,1024,1024]{1,2,0:T(8,128)}) fusion(pred[2,1024]{1,0:T(4,128)(4,1)S(1)} %iota_compare_fusion.1, pred[1024,1024]{0,1:T(8,128)(4,1)S(1)} %iota_compare_fusion, bf16[2,1024,1,192]{3,1,0,2:T(8,128)(2,1)S(1)} %get-tuple-element.90, bf16[2,1024,1,32]{3,1,0,2:T(8,128)(2,1)} %get-tuple-element.82, ...), kind=kOutput, calls=%fused_computation.149 | convolution fusion | flops 1090520064 | bytes 11544576 | tf_op jit(solution)/shard_map/sub | solution.py:1312
  295.2 5.4 fusion.37
  303.2 15.2 %convolution_bitcast_fusion = f32[2048,1280]{0,1:T(8,128)S(1)} fusion(bf16[1280,2048]{1,0:T(8,128)(2,1)} %get-tuple-element.27, bf16[2048,2048]{1,0:T(8,128)(2,1)} %bitcast.203), kind=kOutput, calls=%fused_computation.20 | convolution fusion | flops 10737418240 | bytes 24117248 | tf_op jit(solution)/shard_map/dot_general | solution.py:67
  318.5 4.0 copy-done.29
  323.2 34.3 %convert_reduce_fusion.1 = (f32[1024]{0:T(1024)S(1)}, bf16[2048,1024]{0,1:T(8,128)(2,1)}, f32[2048,1024]{0,1:T(8,128)S(1)}, f32[2048,1024]{0,1:T(8,128)S(1)}) fusion(f32[2048,1280]{0,1:T(8,128)} %copy-done.29, f32[1024]{0:T(1024)S(1)} %bitcast.196, bf16[2048,2048]{1,0:T(8,128)(2,1)} %bitcast.175, bf16[1024,2048]{1,0:T(8,128)(2,1)} %bitcast.180), kind=kOutput, calls=%fused_computation.22 | convolution fusion | flops 8747219968 | bytes 41951232 | tf_op jit(solution)/shard_map/td,pde->tpe/dot_general | solution.py:1318
  357.5 1.4 multiply_convert_fusion.1
  358.9 17.2 %convolution_convert_fusion.1 = bf16[2048,2048]{1,0:T(8,128)(2,1)} fusion(bf16[1280,2048]{1,0:T(8,128)(2,1)} %get-tuple-element.27, bf16[2048,1024]{0,1:T(8,128)(2,1)S(1)} %multiply_convert_fusion.1, bf16[2048,256]{0,1:T(8,128)(2,1)S(1)} %copy.59), kind=kOutput, calls=%fused_computation.43 | convolution fusion | flops 10752098304 | bytes 18874368 | tf_op jit(solution)/shard_map/dot_general | solution.py:1322
  376.2 5.0 multiply_reduce_fusion.1
  381.2 5.4 multiply_convert_fusion
  386.7 2.4 multiply_bitcast_fusion.1
  389.6 1.4 multiply_bitcast_fusion
  391.5 0.8 multiply_subtract_fusion.1
  392.3 1.9 maximum_convert_fusion
  394.7 1.3 fusion.40
  397.1 2.4 pad_maximum_fusion.3
  399.6 4.0 reshape.444
  403.7 13.1 %fusion.19 = f32[2048,2048,1]{1,0,2:T(8,128)} fusion(bf16[2048,3,256]{2,1,0:T(4,128)(2,1)} %reshape.444, bf16[7,2048,256]{2,1,0:T(8,128)(2,1)} %get-tuple-element.26), kind=kOutput, calls=%fused_computation.61 | convolution fusion | flops 6442450944 | bytes 24117248 | tf_op jit(solution)/shard_map/tpe,pde->td/dot_general | solution.py:1357
  416.9 25.7 %bitcast_reduce_fusion = (f32[2048]{0:T(1024)S(1)}, f32[2048]{0:T(1024)S(1)}, bf16[2048,2048]{1,0:T(8,128)(2,1)}, f32[2048]{0:T(1024)S(1)}, f32[2048]{0:T(1024)S...) fusion(f32[2048]{0:T(1024)S(1)} %copy-done.43, f32[2048]{0:T(1024)S(1)} %copy-done.44, ...), kind=kOutput, calls=%fused_computation.3 | convolution fusion | flops 8669618176 | bytes 58802176 | tf_op jit(solution)/shard_map/tpe,pde->td/dot_general | solution.py:1336
  443.0 0.7 copy.94
  443.7 10.7 %convolution_convert_fusion.3.qkv_grads = bf16[2048,768]{1,0:T(8,128)(2,1)} fusion(bf16[2048,2048]{1,0:T(8,128)(2,1)} %get-tuple-element.78, bf16[2048,256]{1,0:T(8,128)(2,1)S(1)} %bitcast.182, bf16[2048,256]{1,0:T(8,128)(2,1)S(1)} %bitcast.171, bf16[2048,256]{1,0:T(8,128)(2,1)S(1)} %bitcast.168), kind=kOutput, calls=%fused_computation.58 | convolution fusion | flops 6453460992 | bytes 14680064 | tf_op jit(solution)/shard_map/dot_general | solution.py:61
  454.5 12.8 %convolution_convert_fusion.2.expand_grads = bf16[2048,1024]{1,0:T(8,128)(2,1)} fusion(bf16[2048,2048]{1,0:T(8,128)(2,1)} %get-tuple-element.77, bf16[2048,1024]{0,1:T(8,128)(2,1)S(1)} %copy-done.49), kind=kOutput, calls=%fused_computation.53 | convolution fusion | flops 8592031744 | bytes 16777216 | tf_op jit(solution)/shard_map/dot_general | solution.py:61
  467.3 13.4 %convolution_convert_fusion.out_grads = bf16[1280,2048]{1,0:T(8,128)(2,1)} fusion(bf16[2048,2048]{1,0:T(8,128)(2,1)S(1)} %bitcast.206, bf16[2048,1024]{0,1:T(8,128)(2,1)S(1)} %copy-done.14, bf16[2048,256]{0,1:T(8,128)(2,1)S(1)} %copy-done.19), kind=kOutput, calls=%fused_computation.42 | convolution fusion | flops 10750525440 | bytes 18874368 | tf_op jit(solution)/shard_map/dot_general | solution.py:61
  480.7 156.6 %reduce_all.1 = (bf16[2,128,2048]{2,1,0:T(8,128)(2,1)}, bf16[7,8,64,256]{3,2,1,0:T(8,128)(2,1)}, bf16[256,2048]{1,0:T(8,128)(2,1)}, bf16[64,2048]{1,0:T(8,128)(2,1)}, f32[8,128]{1,0:T(8,128)}) custom-call(bf16[2,1024,2048]{2,1,0:T(8,128)(2,1)} %bitcast.176, bf16[2048,768]{1,0:T(8,128)(2,1)} %convolution_convert_fusion.3.qkv_grads, ...), custom_call_target="tpu_custom_call" | custom-call | tf_op jit(solution)/shard_map/reduce_all/pallas_call | solution.py:1191
  637.4 2.0 convert_bitcast_fusion
  640.5 0.8 convert_element_type.229
  641.3 1.5 copy.96
  642.8 1.3 copy.95
  644.1 1.5 convert_element_type.230
  645.6 0.7 convert_reduce_fusion.3
  647.4 3.7 fusion.44
  (174 shorter events, 11.7 us)
Async XLA Ops:
  7.2 296.1 %all-gather.3.cloned.1.call-start = ((), (), s32[]{:S(2)}) async-start(), calls=%async_computation.2 | async-start | bytes 9437184 | tf_op jit(solution)/shard_map/all_gather | solution.py:1270
  7.9 639.5 %reduce-scatter.2.cloned.1.call-start = ((), (), s32[]{:S(2)}) async-start(), calls=%async_computation.1 | async-start | bytes 9437184 | tf_op jit(solution)/shard_map/reduce_scatter | solution.py:1323
  222.0 26.8 %copy-start.32 = (f32[2048]{0:T(1024)}, f32[2048]{0:T(1024)S(1)}, u32[]{:S(2)}) copy-start(f32[2048]{0:T(1024)S(1)} %reshape.432) | copy-start | bytes 24580
  222.0 26.8 %copy-start.34 = (f32[2048]{0:T(1024)}, f32[2048]{0:T(1024)S(1)}, u32[]{:S(2)}) copy-start(f32[2048]{0:T(1024)S(1)} %reshape.436) | copy-start | bytes 24580
  222.1 26.7 %copy-start.36 = (f32[2048]{0:T(1024)}, f32[2048]{0:T(1024)S(1)}, u32[]{:S(2)}) copy-start(f32[2048]{0:T(1024)S(1)} %reshape.435) | copy-start | bytes 24580
  222.2 26.6 %copy-start.38 = (f32[2048]{0:T(1024)}, f32[2048]{0:T(1024)S(1)}, u32[]{:S(2)}) copy-start(f32[2048]{0:T(1024)S(1)} %reshape.433) | copy-start | bytes 24580
  238.2 10.6 %slice-start = ((s8[8388608]{0:T(1024)(128)(4,1)}), s8[4194304]{0:T(1024)(128)(4,1)S(1)}, s32[]{:S(2)}) async-start(s8[8388608]{0:T(1024)(128)(4,1)} %bitcast.163), calls=%async_computation.3 | async-start | bytes 8388608
  242.9 5.9 slice-start.1
  248.9 7.3 %copy-start.15 = (bf16[3,256,2048]{2,1,0:T(8,128)(2,1)S(1)}, bf16[3,256,2048]{2,1,0:T(8,128)(2,1)}, u32[]{:S(2)}) copy-start(bf16[3,256,2048]{2,1,0:T(8,128)(2,1)} %copy.50) | copy-start | bytes 9437188
  264.8 11.1 %copy-start.46 = (s32[2,1]{0,1:T(1,128)S(1)}, s32[2,1]{0,1:T(1,128)}, u32[]{:S(2)}) copy-start(s32[2,1]{0,1:T(1,128)} %param.17) | copy-start | bytes 28
  279.0 6.1 copy-start.8
  284.1 3.2 copy-start.7
  285.1 10.1 %copy-start.20 = (bf16[2,1024,1,192]{3,1,0,2:T(8,128)(2,1)}, bf16[2,1024,1,192]{3,1,0,2:T(8,128)(2,1)S(1)}, u32[]{:S(2)}) copy-start(bf16[2,1024,1,192]{3,1,0,2:T(8,128)(2,1)S(1)} %get-tuple-element.89) | copy-start | bytes 2359300
  285.1 10.1 %copy-start.22 = (bf16[2,1024,1,192]{3,1,0,2:T(8,128)(2,1)}, bf16[2,1024,1,192]{3,1,0,2:T(8,128)(2,1)S(1)}, u32[]{:S(2)}) copy-start(bf16[2,1024,1,192]{3,1,0,2:T(8,128)(2,1)S(1)} %get-tuple-element.90) | copy-start | bytes 2359300
  295.2 6.2 copy-start
  301.3 57.5 %copy-start.18 = (bf16[2048,256]{0,1:T(8,128)(2,1)}, bf16[2048,256]{0,1:T(8,128)(2,1)S(1)}, u32[]{:S(2)}) copy-start(bf16[2048,256]{0,1:T(8,128)(2,1)S(1)} %copy.59) | copy-start | bytes 3145732
  301.6 16.9 %copy-start.40 = (f32[2,128]{1,0:T(2,128)}, f32[2,128]{1,0:T(2,128)S(1)}, u32[]{:S(2)}) copy-start(f32[2,128]{1,0:T(2,128)S(1)} %broadcast_multiply_fusion.3) | copy-start | bytes 3076
  318.5 4.0 copy-start.29
  358.9 17.3 %copy-start.13 = (bf16[2048,1024]{0,1:T(8,128)(2,1)}, bf16[2048,1024]{0,1:T(8,128)(2,1)S(1)}, u32[]{:S(2)}) copy-start(bf16[2048,1024]{0,1:T(8,128)(2,1)S(1)} %multiply_convert_fusion.1) | copy-start | bytes 12582916
  381.2 5.5 copy-start.23
  381.2 5.5 copy-start.26
  381.2 5.5 copy-start.27
  391.0 3.1 slice-start.2
  391.4 3.2 slice-start.3
  403.6 13.2 %copy-start.33 = (f32[2048]{0:T(1024)S(1)}, f32[2048]{0:T(1024)}, u32[]{:S(2)}) copy-start(f32[2048]{0:T(1024)} %copy-done.32) | copy-start | bytes 24580
  403.6 13.2 %copy-start.35 = (f32[2048]{0:T(1024)S(1)}, f32[2048]{0:T(1024)}, u32[]{:S(2)}) copy-start(f32[2048]{0:T(1024)} %copy-done.34) | copy-start | bytes 24580
  403.6 13.2 %copy-start.37 = (f32[2048]{0:T(1024)S(1)}, f32[2048]{0:T(1024)}, u32[]{:S(2)}) copy-start(f32[2048]{0:T(1024)} %copy-done.36) | copy-start | bytes 24580
  403.6 13.2 %copy-start.39 = (f32[2048]{0:T(1024)S(1)}, f32[2048]{0:T(1024)}, u32[]{:S(2)}) copy-start(f32[2048]{0:T(1024)} %copy-done.38) | copy-start | bytes 24580
  403.6 13.2 %copy-start.43 = (f32[2048]{0:T(1024)S(1)}, f32[2048]{0:T(1024)}, u32[]{:S(2)}) copy-start(f32[2048]{0:T(1024)} %get-tuple-element.119) | copy-start | bytes 24580
  403.6 13.2 %copy-start.44 = (f32[2048]{0:T(1024)S(1)}, f32[2048]{0:T(1024)}, u32[]{:S(2)}) copy-start(f32[2048]{0:T(1024)} %get-tuple-element.120) | copy-start | bytes 24580
  403.6 13.2 %copy-start.48 = (bf16[2048,1024]{0,1:T(8,128)(2,1)S(1)}, bf16[2048,1024]{0,1:T(8,128)(2,1)}, u32[]{:S(2)}) copy-start(bf16[2048,1024]{0,1:T(8,128)(2,1)} %get-tuple-element.70) | copy-start | bytes 12582916
  416.8 26.0 %copy-start.30 = (f32[32,64]{1,0:T(8,128)S(1)}, f32[32,64]{1,0:T(8,128)}, u32[]{:S(2)}) copy-start(f32[32,64]{1,0:T(8,128)} %reshape.420) | copy-start | bytes 24580
  416.8 26.8 %copy-start.4 = (bf16[2,1024,1,256]{3,1,0,2:T(8,128)(2,1)S(1)}, bf16[2,1024,1,256]{3,1,0,2:T(8,128)(2,1)}, u32[]{:S(2)}) copy-start(bf16[2,1024,1,256]{3,1,0,2:T(8,128)(2,1)} %copy-done.3) | copy-start | bytes 3145732
  416.8 26.8 %copy-start.6 = (bf16[2,1024,1,256]{3,1,0,2:T(8,128)(2,1)S(1)}, bf16[2,1024,1,256]{3,1,0,2:T(8,128)(2,1)}, u32[]{:S(2)}) copy-start(bf16[2,1024,1,256]{3,1,0,2:T(8,128)(2,1)} %copy-done.5) | copy-start | bytes 3145732
  416.9 26.8 %copy-start.11 = (bf16[2,1024,256]{2,1,0:T(8,128)(2,1)S(1)}, bf16[2,1024,256]{2,1,0:T(8,128)(2,1)}, u32[]{:S(2)}) copy-start(bf16[2,1024,256]{2,1,0:T(8,128)(2,1)} %copy-done.10) | copy-start | bytes 3145732
  443.7 10.8 %copy-start.49 = (bf16[2048,1024]{0,1:T(8,128)(2,1)S(1)}, bf16[2048,1024]{0,1:T(8,128)(2,1)}, u32[]{:S(2)}) copy-start(bf16[2048,1024]{0,1:T(8,128)(2,1)} %get-tuple-element.70) | copy-start | bytes 12582916
  443.7 23.6 %slice-start.4 = ((s8[8388608]{0:T(1024)(128)(4,1)}), s8[4194304]{0:T(1024)(128)(4,1)S(1)}, s32[]{:S(2)}) async-start(s8[8388608]{0:T(1024)(128)(4,1)} %bitcast.204), calls=%async_computation.7 | async-start | bytes 8388608
  454.4 12.9 %copy-start.14 = (bf16[2048,1024]{0,1:T(8,128)(2,1)S(1)}, bf16[2048,1024]{0,1:T(8,128)(2,1)}, u32[]{:S(2)}) copy-start(bf16[2048,1024]{0,1:T(8,128)(2,1)} %copy-done.13) | copy-start | bytes 12582916
  454.4 12.9 %copy-start.19 = (bf16[2048,256]{0,1:T(8,128)(2,1)S(1)}, bf16[2048,256]{0,1:T(8,128)(2,1)}, u32[]{:S(2)}) copy-start(bf16[2048,256]{0,1:T(8,128)(2,1)} %copy-done.18) | copy-start | bytes 3145732
  454.4 12.9 %slice-start.5 = ((s8[8388608]{0:T(1024)(128)(4,1)}), s8[4194304]{0:T(1024)(128)(4,1)S(1)}, s32[]{:S(2)}) async-start(s8[8388608]{0:T(1024)(128)(4,1)} %bitcast.204), calls=%async_computation.8 | async-start | bytes 8388608
  639.4 4.6 copy-start.17
  639.6 6.1 copy-start.1
  639.6 6.1 copy-start.12
  639.6 6.1 copy-start.41
  639.6 6.0 copy-start.42
  639.6 7.8 %copy-start.2 = (bf16[2,1,128,2048]{3,2,1,0:T(8,128)(2,1)S(1)}, bf16[2,1,128,2048]{3,2,1,0:T(8,128)(2,1)}, u32[]{:S(2)}) copy-start(bf16[2,1,128,2048]{3,2,1,0:T(8,128)(2,1)} %param.16) | copy-start | bytes 3145732
  639.6 7.8 %copy-start.31 = (f32[2048]{0:T(1024)S(1)}, f32[2048]{0:T(1024)}, u32[]{:S(2)}) copy-start(f32[2048]{0:T(1024)} %add.139) | copy-start | bytes 24580
  640.4 10.7 %copy-start.47 = (f32[64]{0:T(128)}, f32[64]{0:T(128)S(1)}, u32[]{:S(2)}) copy-start(f32[64]{0:T(128)S(1)} %get-tuple-element.146) | copy-start | bytes 772
  (10 other events, 22.2 us)
Sparse Core Ops, SparseCore 0:
  9.6 141.9 all-gather.2
  376.3 85.8 reduce-scatter.1

commit v4 on v3

--- a/solution.py
+++ b/solution.py
@@ -1229,6 +1229,345 @@
     )(back, qkv_grads, expand_grads, out_grads, board)
 
 
+TILE = 256
+
+
+def turn_tables(length):
+    freqs = jnp.exp(jnp.arange(ROT // 2, dtype=jnp.float32) * (-2.0 * math.log(10000.0) / ROT))
+    angles = jnp.arange(length, dtype=jnp.float32)[:, None] * freqs[None, :]
+    cos, sin = jnp.cos(angles), jnp.sin(angles)
+    rest = jnp.zeros((length, 128 - ROT), jnp.float32)
+    return (
+        jnp.concatenate([cos, cos, rest + 1.0], axis=1),
+        jnp.concatenate([-sin, sin, rest], axis=1),
+    )
+
+
+def turn(head, cos, sin):
+    front = head[:, :128]
+    lane = lax.broadcasted_iota(jnp.int32, front.shape, 1)
+    other = jnp.where(lane < ROT // 2, pltpu.roll(front, 128 - ROT // 2, 1), pltpu.roll(front, ROT // 2, 1))
+    return jnp.concatenate([front * cos + other * sin, head[:, 128:]], axis=1)
+
+
+def dot_nn(a, b):
+    return lax.dot_general(a, b, (((1,), (0,)), ((), ())), preferred_element_type=jnp.float32)
+
+
+def dot_nt(a, b):
+    return lax.dot_general(a, b, (((1,), (1,)), ((), ())), preferred_element_type=jnp.float32)
+
+
+def dot_tn(a, b):
+    return lax.dot_general(a, b, (((0,), (0,)), ((), ())), preferred_element_type=jnp.float32)
+
+
+def forward_kernel(
+    tiles,
+    prefix,
+    x,
+    panels,
+    out_w,
+    gains,
+    qkv_shift,
+    expand_shift,
+    cos,
+    sin,
+    hidden_attn,
+    hidden_mlp,
+    heads,
+    probs,
+    features,
+    slopes,
+    partial,
+    head_rows,
+    acts,
+):
+    step = pl.program_id(0)
+    seq = step // (2 * tiles)
+    phase = lax.rem(step, 2 * tiles) // tiles
+    tile = lax.rem(step, tiles)
+    rows = pl.ds(pl.multiple_of(tile * TILE, TILE), TILE)
+    n_expand = panels.shape[0] - 3
+    scale = 1.0 / math.sqrt(HEAD)
+
+    @pl.when(phase == 0)
+    def _():
+        values_in = x[...].astype(jnp.float32)
+        centered = values_in - jnp.mean(values_in, axis=1, keepdims=True)
+        normal = centered * lax.rsqrt(jnp.mean(centered * centered, axis=1, keepdims=True) + 1e-05)
+        hidden_attn[...] = (normal * gains[0:1, :] + gains[1:2, :]).astype(jnp.bfloat16)
+        hidden_mlp[...] = (normal * gains[2:3, :] + gains[3:4, :]).astype(jnp.bfloat16)
+        for part in range(3):
+            joined = dot_nn(hidden_attn[...], panels[part]) + qkv_shift[:, part * HEAD : (part + 1) * HEAD]
+            if part < 2:
+                joined = turn(joined, cos[rows, :], sin[rows, :])
+            joined = joined.astype(jnp.bfloat16)
+            heads[part] = joined
+            head_rows[part, rows, :] = joined
+        for part in range(n_expand):
+            columns = slice(part * HEAD, (part + 1) * HEAD)
+            expanded = dot_nn(hidden_mlp[...], panels[3 + part]) + expand_shift[:, columns]
+            cdf = 0.5 * (1.0 + lax.erf(expanded * (1.0 / math.sqrt(2.0))))
+            acts[rows, columns] = (expanded * cdf).astype(jnp.bfloat16)
+            bell = jnp.exp(-0.5 * expanded * expanded) * (1.0 / math.sqrt(2.0 * math.pi))
+            slopes[:, columns] = (cdf + expanded * bell).astype(jnp.bfloat16)
+
+    @pl.when(phase == 1)
+    def _():
+        scores = dot_nt(head_rows[0, rows, :], head_rows[1]) * scale
+        key_at = lax.broadcasted_iota(jnp.int32, scores.shape, 1)
+        query_at = lax.broadcasted_iota(jnp.int32, scores.shape, 0) + tile * TILE
+        allowed = jnp.logical_or(key_at <= query_at, key_at < prefix[seq])
+        scores = jnp.where(allowed, scores, -1e30)
+        expo = jnp.exp(scores - jnp.max(scores, axis=1, keepdims=True))
+        low_probs = (expo * (1.0 / jnp.sum(expo, axis=1, keepdims=True))).astype(jnp.bfloat16)
+        probs[0] = low_probs
+        features[:, :HEAD] = dot_nn(low_probs, head_rows[2]).astype(jnp.bfloat16)
+        features[:, HEAD:] = acts[rows, :]
+        width = out_w.shape[1]
+        for start in range(0, width, 512):
+            columns = slice(start, start + 512)
+            partial[:, columns] = dot_nn(features[...], out_w[:, columns]).astype(jnp.bfloat16)
+
+
+def whole_spec(array):
+    zeros = (0,) * array.ndim
+    return pl.BlockSpec(array.shape, lambda step: zeros, pipeline_mode=pl.Buffered(1))
+
+
+def forward_call(prefix, x, panels, out_w, gains, qkv_shift, expand_shift, cos, sin):
+    tokens, width = x.shape
+    length = cos.shape[0]
+    tiles = length // TILE
+    steps = 2 * tokens // TILE
+    hidden = expand_shift.shape[1]
+
+    def early(step):
+        seq, at = step // (2 * tiles), lax.rem(step, 2 * tiles)
+        return seq * tiles + jnp.minimum(at, tiles - 1)
+
+    def late(step):
+        seq, at = step // (2 * tiles), lax.rem(step, 2 * tiles)
+        return seq * tiles + jnp.maximum(at - tiles, 0)
+
+    kind = jnp.bfloat16
+    return pl.pallas_call(
+        functools.partial(forward_kernel, tiles),
+        grid=(steps,),
+        out_shape=(
+            jax.ShapeDtypeStruct((tokens, width), kind),
+            jax.ShapeDtypeStruct((tokens, width), kind),
+            jax.ShapeDtypeStruct((3, tokens, HEAD), kind),
+            jax.ShapeDtypeStruct((tokens // length, length, length), kind),
+            jax.ShapeDtypeStruct((tokens, HEAD + hidden), kind),
+            jax.ShapeDtypeStruct((tokens, hidden), kind),
+            jax.ShapeDtypeStruct((tokens, width), kind),
+        ),
+        in_specs=[
+            pl.BlockSpec(memory_space=pltpu.SMEM),
+            pl.BlockSpec((TILE, width), lambda step: (early(step), 0)),
+            whole_spec(panels),
+            whole_spec(out_w),
+            whole_spec(gains),
+            whole_spec(qkv_shift),
+            whole_spec(expand_shift),
+            whole_spec(cos),
+            whole_spec(sin),
+        ],
+        out_specs=(
+            pl.BlockSpec((TILE, width), lambda step: (early(step), 0)),
+            pl.BlockSpec((TILE, width), lambda step: (early(step), 0)),
+            pl.BlockSpec((3, TILE, HEAD), lambda step: (0, early(step), 0)),
+            pl.BlockSpec((1, TILE, length), lambda step: (late(step) // tiles, lax.rem(late(step), tiles), 0)),
+            pl.BlockSpec((TILE, HEAD + hidden), lambda step: (late(step), 0)),
+            pl.BlockSpec((TILE, hidden), lambda step: (early(step), 0)),
+            pl.BlockSpec((TILE, width), lambda step: (late(step), 0)),
+        ),
+        scratch_shapes=[
+            pltpu.VMEM((3, length, HEAD), kind),
+            pltpu.VMEM((length, hidden), kind),
+        ],
+        compiler_params=pltpu.CompilerParams(vmem_limit_bytes=56 * 1024 * 1024),
+        cost_estimate=pl.CostEstimate(
+            flops=2 * tokens * width * (2 * hidden + 4 * HEAD) + 4 * tokens * length * HEAD,
+            bytes_accessed=64 * 1024 * 1024,
+            transcendentals=0,
+        ),
+        name="forward_part",
+    )(prefix, x, panels, out_w, gains, qkv_shift, expand_shift, cos, sin)
+
+
+def backward_kernel(
+    tiles,
+    g,
+    x,
+    panels,
+    out_w,
+    gains,
+    cos,
+    sin,
+    heads,
+    probs,
+    slopes,
+    grad_expanded,
+    grad_joined,
+    combined,
+    norm_sums,
+    joined_sums,
+    expand_sums,
+    grad_mixed,
+    back_mlp,
+    grad_queries,
+    grad_keys,
+    grad_values,
+):
+    step = pl.program_id(0)
+    phase = lax.rem(step, 3 * tiles) // tiles
+    tile = lax.rem(step, tiles)
+    rows = pl.ds(pl.multiple_of(tile * TILE, TILE), TILE)
+    n_expand = panels.shape[0] - 3
+    width = out_w.shape[1]
+    scale = 1.0 / math.sqrt(HEAD)
+
+    @pl.when(step == 0)
+    def _():
+        norm_sums[...] = jnp.zeros_like(norm_sums)
+        joined_sums[...] = jnp.zeros_like(joined_sums)
+        expand_sums[...] = jnp.zeros_like(expand_sums)
+
+    @pl.when(phase == 0)
+    def _():
+        grad_mixed[rows, :] = dot_nt(g[...], out_w[:HEAD, :]).astype(jnp.bfloat16)
+        for part in range(n_expand):
+            columns = slice(part * HEAD, (part + 1) * HEAD)
+            grad = dot_nt(g[...], out_w[(part + 1) * HEAD : (part + 2) * HEAD, :])
+            grad = (grad * slopes[:, columns].astype(jnp.float32)).astype(jnp.bfloat16)
+            grad_expanded[:, columns] = grad
+            expand_sums[:, columns] += jnp.sum(grad.astype(jnp.float32), axis=0, keepdims=True)
+        for start in range(0, width, 512):
+            columns = slice(start, start + 512)
+            total = dot_nt(grad_expanded[:, :HEAD], panels[3, columns, :])
+            for part in range(1, n_expand):
+                total += dot_nt(grad_expanded[:, part * HEAD : (part + 1) * HEAD], panels[3 + part, columns, :])
+            back_mlp[rows, columns] = total
+
+    @pl.when(phase == 1)
+    def _():
+        low_probs = probs[0]
+        own = grad_mixed[rows, :]
+        grad_probs = dot_nt(own, heads[2])
+        wide = low_probs.astype(jnp.float32)
+        delta = jnp.sum(wide * grad_probs, axis=1, keepdims=True)
+        grad_scores = (wide * (grad_probs - delta)).astype(jnp.bfloat16)
+        grad_queries[rows, :] = dot_nn(grad_scores, heads[1]) * scale
+        more_keys = dot_tn(grad_scores, heads[0, rows, :]) * scale
+        more_values = dot_tn(low_probs, own)
+
+        @pl.when(tile == 0)
+        def _():
+            grad_keys[...] = more_keys
+            grad_values[...] = more_values
+
+        @pl.when(tile > 0)
+        def _():
+            grad_keys[...] += more_keys
+            grad_values[...] += more_values
+
+    @pl.when(phase == 2)
+    def _():
+        cos_rows, sin_rows = cos[rows, :], -sin[rows, :]
+        parts = (
+            turn(grad_queries[rows, :], cos_rows, sin_rows),
+            turn(grad_keys[rows, :], cos_rows, sin_rows),
+            grad_values[rows, :],
+        )
+        for part in range(3):
+            columns = slice(part * HEAD, (part + 1) * HEAD)
+            joined = parts[part].astype(jnp.bfloat16)
+            grad_joined[:, columns] = joined
+            joined_sums[:, columns] += jnp.sum(joined.astype(jnp.float32), axis=0, keepdims=True)
+        values_in = x[...].astype(jnp.float32)
+        mean = jnp.mean(values_in, axis=1, keepdims=True)
+        centered = values_in - mean
+        spread = lax.rsqrt(jnp.mean(centered * centered, axis=1, keepdims=True) + 1e-05)
+        for start in range(0, width, 512):
+            columns = slice(start, start + 512)
+            normal = (x[:, columns].astype(jnp.float32) - mean) * spread
+            total = dot_nt(grad_joined[:, :HEAD], panels[0, columns, :])
+            for part in range(1, 3):
+                total += dot_nt(grad_joined[:, part * HEAD : (part + 1) * HEAD], panels[part, columns, :])
+            other = back_mlp[rows, columns]
+            for row, value in ((0, total * normal), (1, total), (2, other * normal), (3, other)):
+                norm_sums[row : row + 1, columns] += jnp.sum(value, axis=0, keepdims=True)
+            combined[:, columns] = (total * gains[0:1, columns] + other * gains[2:3, columns]).astype(jnp.bfloat16)
+
+
+def backward_call(g, x, panels, out_w, gains, cos, sin, heads, probs, slopes):
+    tokens, width = x.shape
+    length = cos.shape[0]
+    tiles = length // TILE
+    steps = 3 * tokens // TILE
+    hidden = slopes.shape[1]
+
+    def at_phase(phase):
+        def index(step):
+            seq, at = step // (3 * tiles), lax.rem(step, 3 * tiles)
+            return seq * tiles + jnp.clip(at - phase * tiles, 0, tiles - 1)
+
+        return index
+
+    first, second, third = (at_phase(phase) for phase in range(3))
+    kind = jnp.bfloat16
+    fixed = lambda step: (0, 0)
+    return pl.pallas_call(
+        functools.partial(backward_kernel, tiles),
+        grid=(steps,),
+        out_shape=(
+            jax.ShapeDtypeStruct((tokens, hidden), kind),
+            jax.ShapeDtypeStruct((tokens, 3 * HEAD), kind),
+            jax.ShapeDtypeStruct((tokens, width), kind),
+            jax.ShapeDtypeStruct((8, width), jnp.float32),
+            jax.ShapeDtypeStruct((1, 3 * HEAD), jnp.float32),
+            jax.ShapeDtypeStruct((1, hidden), jnp.float32),
+        ),
+        in_specs=[
+            pl.BlockSpec((TILE, width), lambda step: (first(step), 0)),
+            pl.BlockSpec((TILE, width), lambda step: (third(step), 0)),
+            whole_spec(panels),
+            whole_spec(out_w),
+            whole_spec(gains),
+            whole_spec(cos),
+            whole_spec(sin),
+            pl.BlockSpec((3, length, HEAD), lambda step: (0, step // (3 * tiles), 0)),
+            pl.BlockSpec((1, TILE, length), lambda step: (second(step) // tiles, lax.rem(second(step), tiles), 0)),
+            pl.BlockSpec((TILE, hidden), lambda step: (first(step), 0)),
+        ],
+        out_specs=(
+            pl.BlockSpec((TILE, hidden), lambda step: (first(step), 0)),
+            pl.BlockSpec((TILE, 3 * HEAD), lambda step: (third(step), 0)),
+            pl.BlockSpec((TILE, width), lambda step: (third(step), 0)),
+            pl.BlockSpec((8, width), fixed),
+            pl.BlockSpec((1, 3 * HEAD), fixed),
+            pl.BlockSpec((1, hidden), fixed),
+        ),
+        scratch_shapes=[
+            pltpu.VMEM((length, HEAD), kind),
+            pltpu.VMEM((length, width), jnp.float32),
+            pltpu.VMEM((length, HEAD), jnp.float32),
+            pltpu.VMEM((length, HEAD), jnp.float32),
+            pltpu.VMEM((length, HEAD), jnp.float32),
+        ],
+        compiler_params=pltpu.CompilerParams(vmem_limit_bytes=56 * 1024 * 1024),
+        cost_estimate=pl.CostEstimate(
+            flops=2 * tokens * width * (2 * hidden + 4 * HEAD) + 10 * tokens * length * HEAD,
+            bytes_accessed=48 * 1024 * 1024,
+            transcendentals=0,
+        ),
+        name="backward_part",
+    )(g, x, panels, out_w, gains, cos, sin, heads, probs, slopes)
+
+
 def tensor_shards(
     layer_input,
     out_grad,
@@ -1274,8 +1613,6 @@
         dp_size, ctx_size, own_x, qkv_weight, expand_weight, dense_weight, shrink_weight, packed
     )
     x_all = x_all.reshape(tokens, width)
-    qkv_part = panels[:3]
-    expand_part = panels[3:]
     small = unpack_small(small.reshape(devices, -1)[:, :count], lengths, devices)
     gain_attn, shift_attn, gain_mlp, shift_mlp, qkv_shift, dense_shift, expand_shift, shrink_shift = small
     qkv_shift = lax.dynamic_slice_in_dim(qkv_shift.reshape(3, ctx_size, HEAD), me, 1, 1).reshape(-1)
@@ -1283,43 +1620,11 @@
         expand_shift.reshape(dp_size, ctx_size, unit), me, 1, 1
     ).reshape(-1)
 
-    inputs = x_all.astype(jnp.float32)
-    row_mean = jnp.mean(inputs, axis=-1, keepdims=True)
-    centered = inputs - row_mean
-    spread = lax.rsqrt(jnp.mean(centered * centered, axis=-1, keepdims=True) + 1e-05)
-    normal = centered * spread
-    hidden_attn = low(normal * gain_attn + shift_attn)
-    hidden_mlp = low(normal * gain_mlp + shift_mlp)
-
-    cos_table, sin_table = rope_tables(jnp.arange(SEQ, dtype=jnp.float32))
-    joined = jnp.einsum("td,pde->tpe", hidden_attn, qkv_part, preferred_element_type=jnp.float32)
-    joined = joined.reshape(tokens, -1) + qkv_shift
-    joined = joined.reshape(sequences, SEQ, 3, HEAD)
-
-    def turn(heads, sin_values):
-        return rotate(heads[:, :, None, :], cos_table, sin_values)[:, :, 0]
-
-    queries = low(turn(joined[:, :, 0], sin_table))
-    key_rows = low(turn(joined[:, :, 1], sin_table))
-    value_rows = low(joined[:, :, 2])
-    positions = jnp.arange(SEQ, dtype=jnp.int32)
-    prefix = prefix_len.reshape(sequences)
-    allowed = (positions[None, :] <= positions[:, None])[None] | (
-        positions[None, None, :] < prefix[:, None, None]
-    )
-    scores = jnp.einsum("sqe,ske->sqk", queries, key_rows, preferred_element_type=jnp.float32) * scale
-    scores = jnp.where(allowed, scores, -1e30)
-    expo = jnp.exp(scores - jnp.max(scores, axis=-1, keepdims=True))
-    probs = expo / jnp.sum(expo, axis=-1, keepdims=True)
-    probs_low = low(probs)
-    mixed = low(
-        jnp.einsum("sqk,ske->sqe", probs_low, value_rows, preferred_element_type=jnp.float32)
-    ).reshape(tokens, HEAD)
-    expanded = jnp.einsum("td,pde->tpe", hidden_mlp, expand_part, preferred_element_type=jnp.float32)
-    expanded = expanded.reshape(tokens, -1) + expand_shift
-    activated = low(gelu_exact(expanded))
-    features = jnp.concatenate([mixed, activated], axis=1)
-    partial = low(jnp.dot(features, out_part, preferred_element_type=jnp.float32))
+    gains = jnp.stack([gain_attn, shift_attn, gain_mlp, shift_mlp])
+    cos, sin = turn_tables(SEQ)
+    hidden_attn, hidden_mlp, heads, probs, features, slopes, partial = forward_call(
+        prefix_len.reshape(sequences), x_all, panels, out_part, gains, qkv_shift[None], expand_shift[None], cos, sin
+    )
     reduced = lax.psum_scatter(
         partial.reshape(sequences, SEQ, width), "ctx", scatter_dimension=1, tiled=True
     )
@@ -1328,46 +1633,18 @@
     ).reshape(layer_input.shape)
 
     out_grads = low(contract_rows(features, g_all))
-    grad_features = contract_cols(g_all, out_part)
-    unused, gelu_back = jax.vjp(gelu_exact, expanded)
-    grad_expanded = low(gelu_back(grad_features[:, HEAD:])[0])
-    grad_mixed = low(grad_features[:, :HEAD]).reshape(sequences, SEQ, HEAD)
+    grad_expanded, grad_joined, combined, norm_sums, joined_sum, expand_sum = backward_call(
+        g_all, x_all, panels, out_part, gains, cos, sin, heads, probs, slopes
+    )
     expand_grads = low(contract_rows(hidden_mlp, grad_expanded))
-    back_mlp = jnp.einsum(
-        "tpe,pde->td",
-        grad_expanded.reshape(tokens, -1, HEAD),
-        expand_part,
-        preferred_element_type=jnp.float32,
-    )
-
-    grad_probs = jnp.einsum("sqe,ske->sqk", grad_mixed, value_rows, preferred_element_type=jnp.float32)
-    delta = jnp.sum(probs * grad_probs, axis=-1, keepdims=True)
-    grad_scores = low(probs * (grad_probs - delta))
-    grad_queries = (
-        jnp.einsum("sqk,ske->sqe", grad_scores, key_rows, preferred_element_type=jnp.float32) * scale
-    )
-    grad_keys = (
-        jnp.einsum("sqk,sqe->ske", grad_scores, queries, preferred_element_type=jnp.float32) * scale
-    )
-    grad_values = jnp.einsum("sqk,sqe->ske", probs_low, grad_mixed, preferred_element_type=jnp.float32)
-    grad_joined = low(
-        jnp.concatenate([turn(grad_queries, -sin_table), turn(grad_keys, -sin_table), grad_values], axis=-1)
-    ).reshape(tokens, 3 * HEAD)
     qkv_grads = low(contract_rows(hidden_attn, grad_joined))
-    back_attn = jnp.einsum(
-        "tpe,pde->td",
-        grad_joined.reshape(tokens, -1, HEAD),
-        qkv_part,
-        preferred_element_type=jnp.float32,
-    )
-    combined = low(back_attn * gain_attn + back_mlp * gain_mlp)
+    joined_sum, expand_sum = joined_sum[0], expand_sum[0]
+
     def place(values, parts):
         board = jnp.zeros((parts, ctx_size, values.shape[0] // parts), jnp.float32)
         board = lax.dynamic_update_slice(board, values.reshape(parts, 1, -1), (0, me, 0))
         return board.reshape(devices, -1)
 
-    joined_sum = jnp.sum(grad_joined.astype(jnp.float32), axis=0)
-    expand_sum = jnp.sum(grad_expanded.astype(jnp.float32), axis=0)
     out_sum = jnp.sum(own_g.astype(jnp.float32), axis=(0, 1))
     board = jnp.concatenate(
         [
@@ -1375,10 +1652,10 @@
             place(joined_sum[2 * HEAD :], 1),
             out_sum.reshape(devices, -1),
             place(expand_sum, dp_size),
-            jnp.sum(back_attn * normal, axis=0).reshape(devices, -1),
-            jnp.sum(back_attn, axis=0).reshape(devices, -1),
-            jnp.sum(back_mlp * normal, axis=0).reshape(devices, -1),
-            jnp.sum(back_mlp, axis=0).reshape(devices, -1),
+            norm_sums[0].reshape(devices, -1),
+            norm_sums[1].reshape(devices, -1),
+            norm_sums[2].reshape(devices, -1),
+            norm_sums[3].reshape(devices, -1),
         ],
         axis=1,
     )

time: 668 us -> 567 us (0.85)
  the two profiles are of different devices: /device:TPU:8 before, /device:TPU:9 now
where the time goes in v4:
time: 567 us; the launch traced here: 559 us
  Pallas kernels  469 us (83%)
  matrix products  40.1 us (7%)
  local copies, waits for them, and re-layouts  20.7 us (4%)
  other arithmetic  14.2 us (3%)
  between operations  14.2 us (3%)
    pallas_call x1, Pallas kernels, gather_call(): pl.pallas_call(functools.partial(gather_kernel, dp_size, ctx_size), out_s...  203 us
    pallas_call x1, Pallas kernels, reduce_call(): pl.pallas_call(functools.partial(reduce_kernel, dp_size, ctx_size), out_s...  150 us
    pallas_call x1, Pallas kernels, backward_call(): pl.pallas_call(functools.partial(backward_kernel, tiles), grid=(steps,),...  61.1 us
    pallas_call x1, Pallas kernels, forward_call(): pl.pallas_call(functools.partial(forward_kernel, tiles), grid=(steps,), o...  54.5 us
    dot_general x3, matrix products, contract_rows(): lax.dot_general(left_mat, right_mat, (((0,), (0,)), ((), ())), preferred_...  40.1 us
  transfers between devices with their start and end apart: 2, of which 0 were waited for; matrix products, arithmetic and copies ran while one was open for 12% of the time, Pallas kernels for 84%

profile of v4, /device:TPU:9, one launch (start us, length us, event | category | flops | bytes accessed | tf_op | source)
XLA Modules:
  0.0 559.1 jit_solution(11156339205657930217)
XLA Ops:
  7.2 0.7 all-gather.3.cloned.1.call-update
  8.0 0.1 pad.15.clone
  8.1 0.1 pad.12.clone
  8.1 5.4 concatenate.12
  13.5 0.6 pad_bitcast_fusion.1.packed
  14.1 203.5 %gather_all.1 = (bf16[2,1024,2048]{2,1,0:T(8,128)(2,1)}, bf16[7,2048,256]{2,1,0:T(8,128)(2,1)}, bf16[1280,2048]{1,0:T(8,128)(2,1)}, bf16[32,16,128]{2,1,0:T(8,128)(2,1)}) custom-call(bf16[2,128,2048]{2,1,0:T(8,128)(2,1)} %bitcast.68, bf16[64,6144]{1,0:T(8,128)(2,1)} %qkv.1, bf16[64,8192]{1,0:T(8,128)(2,1)} %expand.1, bf16[64,2048]{1,0:T(8,128)(2,1)} %dense.1, ...), custom_call_target="tpu_custom_call" | custom-call | tf_op jit(solution)/shard_map/gather_all/pallas_call | solution.py:707
  217.6 0.9 copy.61
  218.6 0.1 reshape.223
  218.7 0.1 fusion.16
  218.8 0.1 convert_element_type.115
  218.8 0.1 convert_element_type.118
  218.9 0.1 convert_element_type.117
  219.0 0.1 convert_element_type.116
  219.1 0.6 constant_dynamic-slice_fusion
  219.7 0.6 dynamic-slice_convert_fusion
  220.3 0.7 maximum_convert_fusion.gains
  221.0 2.0 fusion.15
  222.9 1.3 maximum_maximum_fusion
  224.2 54.5 %forward_part.1 = (bf16[2048,2048]{1,0:T(8,128)(2,1)}, bf16[2048,2048]{1,0:T(8,128)(2,1)}, bf16[3,2048,256]{2,1,0:T(8,128)(2,1)}, bf16[2,1024,1024]{2,1,0:T(8,12...) custom-call(s32[2]{0:T(128)} %bitcast.91, ...), custom_call_target="tpu_custom_call" | custom-call | flops 27917287424 | bytes 67108864 | tf_op jit(solution)/shard_map/forward_part/pallas_call | solution.py:1355
  278.7 1.2 copy-done.2
  279.9 0.2 convert_reduce_fusion.2
  280.2 0.1 convert_add_fusion.1
  280.3 0.2 convert_reduce_fusion.1
  280.6 0.4 fusion.7
  281.0 61.1 %backward_part.1 = (bf16[2048,1024]{1,0:T(8,128)(2,1)}, bf16[2048,768]{1,0:T(8,128)(2,1)}, bf16[2048,2048]{1,0:T(8,128)(2,1)}, f32[8,2048]{1,0:T(8,128)}, f32[1,768]{1,0:T(1,128)}, /*index=5*/f32[1,1024]{1,0:T(1,128)}) custom-call(bf16[2048,2048]{1,0:T(8,128)(2,1)} %bitcast.87, bf16[2048,2048]{1,0:T(8,128)(2,1)} %bitcast.90, ...), custom_call_target="tpu_custom_call" | custom-call | flops 31138512896 | bytes 50331648 | tf_op jit(solution)/shard_map/backward_part/pallas_call | solution.py:1523
  342.1 0.7 slice.97
  342.9 0.7 slice_bitcast_fusion.2
  343.7 1.1 slice_reduce_fusion
  345.0 0.7 dynamic_update_slice.11
  345.8 0.1 concatenate.15
  345.9 0.7 copy.55
  346.5 14.2 %convolution_convert_fusion.1.expand_grads = bf16[2048,1024]{1,0:T(8,128)(2,1)} fusion(bf16[2048,2048]{1,0:T(8,128)(2,1)} %get-tuple-element.48, bf16[2048,1024]{1,0:T(8,128)(2,1)} %get-tuple-element.49), kind=kOutput, calls=%fused_computation.1 | convolution fusion | flops 8592031744 | bytes 16777216 | tf_op jit(solution)/shard_map/dot_general | solution.py:61
  360.8 10.7 %convolution_convert_fusion.2.qkv_grads = bf16[2048,768]{1,0:T(8,128)(2,1)} fusion(bf16[2048,2048]{1,0:T(8,128)(2,1)} %get-tuple-element.46, bf16[2048,768]{1,0:T(8,128)(2,1)S(1)} %copy-done.9), kind=kOutput, calls=%fused_computation.3 | convolution fusion | flops 6444023808 | bytes 14680064 | tf_op jit(solution)/shard_map/dot_general | solution.py:61
  371.5 15.1 %convolution_convert_fusion.out_grads = bf16[1280,2048]{1,0:T(8,128)(2,1)} fusion(bf16[2048,1280]{1,0:T(8,128)(2,1)} %get-tuple-element.50, bf16[2048,2048]{1,0:T(8,128)(2,1)S(1)} %bitcast.88), kind=kOutput, calls=%fused_computation | convolution fusion | flops 10740039680 | bytes 18874368 | tf_op jit(solution)/shard_map/dot_general | solution.py:61
  386.6 150.0 %reduce_all.1 = (bf16[2,128,2048]{2,1,0:T(8,128)(2,1)}, bf16[7,8,64,256]{3,2,1,0:T(8,128)(2,1)}, bf16[256,2048]{1,0:T(8,128)(2,1)}, bf16[64,2048]{1,0:T(8,128)(2,1)}, f32[8,128]{1,0:T(8,128)}) custom-call(bf16[2,1024,2048]{2,1,0:T(8,128)(2,1)} %bitcast.71, bf16[2048,768]{1,0:T(8,128)(2,1)} %convolution_convert_fusion.2.qkv_grads, ...), custom_call_target="tpu_custom_call" | custom-call | tf_op jit(solution)/shard_map/reduce_all/pallas_call | solution.py:1191
  536.6 2.0 convert_bitcast_fusion
  538.6 0.2 slice.124
  538.8 1.6 copy-done.1
  540.5 0.6 fusion.17
  541.1 0.8 convert_element_type.133
  541.9 1.5 copy.57
  543.4 1.3 copy.56
  544.7 1.6 convert_element_type.134
  546.3 0.7 convert_reduce_fusion
  547.0 0.5 slice_bitcast_fusion.3
  547.5 0.6 slice_bitcast_fusion.1
  548.1 3.7 fusion.12
  551.8 0.5 copy.66
  (48 shorter events, 0.8 us)
Async XLA Ops:
  7.2 273.8 %all-gather.3.cloned.1.call-start = ((), (), s32[]{:S(2)}) async-start(), calls=%async_computation.2 | async-start | bytes 9437184 | tf_op jit(solution)/shard_map/all_gather | solution.py:1609
  7.9 540.1 %reduce-scatter.2.cloned.1.call-start = ((), (), s32[]{:S(2)}) async-start(), calls=%async_computation.1 | async-start | bytes 9437184 | tf_op jit(solution)/shard_map/reduce_scatter | solution.py:1628
  278.7 1.2 copy-start.2
  278.7 1.6 copy-start
  346.5 14.2 %copy-start.9 = (bf16[2048,768]{1,0:T(8,128)(2,1)S(1)}, bf16[2048,768]{1,0:T(8,128)(2,1)}, u32[]{:S(2)}) copy-start(bf16[2048,768]{1,0:T(8,128)(2,1)} %get-tuple-element.47) | copy-start | bytes 9437188
  360.8 10.8 %copy-start.8 = (bf16[2,1,1024,2048]{3,2,1,0:T(8,128)(2,1)S(1)}, bf16[2,1,1024,2048]{3,2,1,0:T(8,128)(2,1)}, u32[]{:S(2)}) copy-start(bf16[2,1,1024,2048]{3,2,1,0:T(8,128)(2,1)} %all-gather.3.cloned.1.call-done) | copy-start | bytes 25165828
  538.6 1.9 copy-start.1
  538.6 1.9 copy-start.6
  538.6 2.4 copy-start.5
  540.5 3.0 slice-start
  541.1 10.7 %copy-start.7 = (f32[64]{0:T(128)}, f32[64]{0:T(128)S(1)}, u32[]{:S(2)}) copy-start(f32[64]{0:T(128)S(1)} %get-tuple-element.152) | copy-start | bytes 772
  541.9 2.8 copy-start.4
  543.4 2.8 copy-start.3
Sparse Core Ops, SparseCore 0:
  9.6 142.8 all-gather.2
  278.9 87.5 reduce-scatter.1

commit v5 on v2

--- a/solution.py
+++ b/solution.py
@@ -354,6 +354,111 @@
     pl.semaphore_wait(barrier, devices - 1)
 
 
+def chain_gather(src, dst, sems, d, c, levels):
+    block_send, block_recv, core_send, core_recv, local = sems
+    micro, span = src.shape[0], src.shape[1]
+    z = c // 2
+    sibling = c + 1 - 2 * lax.rem(c, 2)
+
+    def block(origin, m):
+        return dst.at[m, pl.ds(pl.multiple_of(origin * span, span), span)]
+
+    def link(way, hop, m):
+        step = 2 if way == 0 else -2
+        origin = c - step * hop
+        view = src.at[m] if hop == 0 else block(origin, m)
+        return remote(view, block(origin, m), block_send.at[way, hop, m], block_recv.at[way, hop, m], d, c + step)
+
+    def leaves(way, hop):
+        if way == 0:
+            return jnp.logical_and(z >= hop, z <= levels - 2)
+        return jnp.logical_and(z + hop <= levels - 1, z >= 1)
+
+    def arrives(way, hop):
+        return z >= hop + 1 if way == 0 else z + hop + 1 <= levels - 1
+
+    def slot_of(way, hop):
+        return 1 + way * (levels - 1) + hop
+
+    def core_copy(slot, origin, m):
+        view = src.at[m] if slot == 0 else block(origin, m)
+        return remote(view, block(origin, m), core_send.at[slot, m], core_recv.at[slot, m], d, sibling)
+
+    def own_copy(m):
+        return pltpu.make_async_copy(src.at[m], block(c, m), local.at[m])
+
+    def start(m):
+        for way in range(2):
+            @pl.when(leaves(way, 0))
+            def _(way=way):
+                link(way, 0, m).start()
+
+        core_copy(0, c, m).start()
+        own_copy(m).start()
+
+    def hop_step(hop, m):
+        for way in range(2):
+            step = 2 if way == 0 else -2
+
+            @pl.when(arrives(way, hop))
+            def _(way=way, step=step):
+                link(way, hop, m).wait_recv()
+                if hop + 1 <= levels - 2:
+                    @pl.when(leaves(way, hop + 1))
+                    def _():
+                        link(way, hop + 1, m).start()
+
+                core_copy(slot_of(way, hop), c - step * (hop + 1), m).start()
+
+    def finish(m):
+        own_copy(m).wait()
+        core_copy(0, c, m).wait_send()
+        core_copy(0, sibling, m).wait_recv()
+        for way in range(2):
+            step = 2 if way == 0 else -2
+            for hop in range(levels - 1):
+                @pl.when(leaves(way, hop))
+                def _(way=way, hop=hop):
+                    link(way, hop, m).wait_send()
+
+                @pl.when(arrives(way, hop))
+                def _(way=way, hop=hop, step=step):
+                    slot = slot_of(way, hop)
+                    core_copy(slot, c - step * (hop + 1), m).wait_send()
+                    core_copy(slot, sibling - step * (hop + 1), m).wait_recv()
+
+    return start, hop_step, finish
+
+
+def chain_scratch(levels, micro):
+    dma = pltpu.SemaphoreType.DMA
+    return [
+        dma((2, levels - 1, micro)),
+        dma((2, levels - 1, micro)),
+        dma((2 * levels - 1, micro)),
+        dma((2 * levels - 1, micro)),
+        dma((micro,)),
+    ]
+
+
+def greet_line(d, c, levels):
+    barrier = pltpu.get_barrier_semaphore()
+    z = c // 2
+    sibling = c + 1 - 2 * lax.rem(c, 2)
+    pl.semaphore_signal(barrier, inc=1, device_id=(d, sibling), device_id_type=MESH_ID)
+
+    @pl.when(z >= 1)
+    def _():
+        pl.semaphore_signal(barrier, inc=1, device_id=(d, c - 2), device_id_type=MESH_ID)
+
+    @pl.when(z <= levels - 2)
+    def _():
+        pl.semaphore_signal(barrier, inc=1, device_id=(d, c + 2), device_id_type=MESH_ID)
+
+    peers = 1 + (z >= 1).astype(jnp.int32) + (z <= levels - 2).astype(jnp.int32)
+    pl.semaphore_wait(barrier, peers)
+
+
 def gather_kernel(
     dp_size,
     ctx_size,
@@ -373,6 +478,7 @@
     block_recv,
     core_send,
     core_recv,
+    block_local,
     panel_send,
     panel_recv,
     share_send,
@@ -450,42 +556,13 @@
     def _():
         dense_out.start()
 
-    def block(origin, m):
-        return x_all.at[m, pl.ds(pl.multiple_of(origin * span, span), span)]
-
-    x_local = []
+    x_start, x_hop, x_finish = chain_gather(
+        x, x_all, (block_send, block_recv, core_send, core_recv, block_local), d, c, levels
+    )
     for m in range(micro):
-        copy = pltpu.make_async_copy(x.at[m], block(c, m), local_sem.at[n_panels + 2 + m])
-        copy.start()
-        x_local.append(copy)
-
-    def chain(way, hop, m):
-        step = 2 if way == 0 else -2
-        origin = c - step * hop
-        src = x.at[m] if hop == 0 else block(origin, m)
-        exists = jnp.logical_and(z >= hop, z <= levels - 2) if way == 0 else jnp.logical_and(
-            z + hop <= levels - 1, z >= 1
-        )
-        copy = remote(src, block(origin, m), block_send.at[way, hop, m], block_recv.at[way, hop, m], d, c + step)
-        return exists, copy
-
-    def arrives(way, hop):
-        return z >= hop + 1 if way == 0 else z + hop + 1 <= levels - 1
-
-    def core_copy(slot, origin, m):
-        src = x.at[m] if slot == 0 else block(origin, m)
-        return remote(src, block(origin, m), core_send.at[slot, m], core_recv.at[slot, m], d, sibling)
-
-    for m in range(micro):
-        core_copy(0, c, m).start()
-        for way in range(2):
-            exists, copy = chain(way, 0, m)
-
-            @pl.when(exists)
-            def _(copy=copy):
-                copy.start()
-
-    small_copy = pltpu.make_async_copy(packed, small.at[me], local_sem.at[n_panels + 2 + micro])
+        x_start(m)
+
+    small_copy = pltpu.make_async_copy(packed, small.at[me], local_sem.at[n_panels + 2])
     small_copy.start()
 
     def push_small(step, carry):
@@ -502,29 +579,6 @@
 
     lax.fori_loop(1, devices, push_small, 0)
 
-    def slot_of(way, hop):
-        return 1 + way * (levels - 1) + hop
-
-    def hop_step(hop):
-        for m in range(micro):
-            for way in range(2):
-                step = 2 if way == 0 else -2
-
-                @pl.when(arrives(way, hop))
-                def _(way=way, m=m, step=step):
-                    origin = c - step * (hop + 1)
-                    remote(
-                        block(origin, m), block(origin, m), block_send.at[way, hop, m], block_recv.at[way, hop, m], d, c - step
-                    ).wait_recv()
-                    core_copy(slot_of(way, hop), origin, m).start()
-
-                if hop + 1 <= levels - 2:
-                    exists, copy = chain(way, hop + 1, m)
-
-                    @pl.when(exists)
-                    def _(copy=copy):
-                        copy.start()
-
     def group_rows(owner, offset, count):
         return pl.ds(pl.multiple_of(owner * panel_rows + offset, 16), count)
 
@@ -569,11 +623,8 @@
     half_head = HEAD // 2
 
     def dense_share(way, mate):
-        return remote(head_rows, head_rows, share_send.at[n_panels + 1, way], share_recv.at[n_panels + 1, way], mate, c)
-
-    def dense_pass(way, mate):
         view = out_w.at[pl.ds(way * half_head, half_head)]
-        return remote(view, view, pass_send.at[n_panels + 1, way], pass_recv.at[n_panels + 1, way], mate, c)
+        return remote(view, view, share_send.at[n_panels + 1, way], share_recv.at[n_panels + 1, way], mate, c)
 
     owns_share = jnp.logical_and(at_source, stays)
 
@@ -597,12 +648,20 @@
         @pl.when(from_x)
         def _():
             dense_share(0, x_mate).wait_recv()
-            dense_pass(0, y_mate).start()
+            dense_share(0, y_mate).start()
 
         @pl.when(from_y)
         def _():
             dense_share(1, y_mate).wait_recv()
-            dense_pass(1, x_mate).start()
+            dense_share(1, x_mate).start()
+
+    def dense_last_step():
+        @pl.when(across)
+        def _():
+            dense_share(0, y_mate).wait_recv()
+            dense_share(0, x_mate).start()
+            dense_share(1, x_mate).wait_recv()
+            dense_share(1, y_mate).start()
 
     across = jnp.logical_not(jnp.logical_or(at_source, jnp.logical_or(from_x, from_y)))
 
@@ -612,17 +671,25 @@
     shrink_pass(0).start()
     shrink_share_wait(1, y_mate)
     shrink_pass(1).start()
-    dense_gather_step()
-    hop_step(0)
     for panel in range(3, n_panels):
         panel_step(panel)
-        panel_forward(panel - 3)
-    hop_step(1)
+    dense_gather_step()
+    panel_forward(0)
+    panel_forward(1)
+    x_hop(0, 0)
+    panel_forward(2)
+    x_hop(0, 1)
     dense_forward_step()
-    for panel in range(n_panels - 3, n_panels):
-        panel_forward(panel)
+    panel_forward(3)
+    panel_forward(4)
+    x_hop(1, 0)
+    panel_forward(5)
+    x_hop(1, 1)
+    dense_last_step()
+    panel_forward(6)
     for hop in range(2, levels - 1):
-        hop_step(hop)
+        for m in range(micro):
+            x_hop(hop, m)
 
     for panel in range(n_panels):
         for way, mate in ((0, x_mate), (1, y_mate)):
@@ -655,35 +722,21 @@
 
     @pl.when(from_x)
     def _():
-        dense_pass(0, y_mate).wait_send()
+        dense_share(0, y_mate).wait_send()
+        dense_share(1, y_mate).wait_recv()
 
     @pl.when(from_y)
     def _():
-        dense_pass(1, x_mate).wait_send()
+        dense_share(1, x_mate).wait_send()
+        dense_share(0, x_mate).wait_recv()
 
     @pl.when(across)
     def _():
-        dense_pass(0, y_mate).wait_recv()
-        dense_pass(1, x_mate).wait_recv()
+        dense_share(0, x_mate).wait_send()
+        dense_share(1, y_mate).wait_send()
 
     for m in range(micro):
-        x_local[m].wait()
-        core_copy(0, c, m).wait_send()
-        core_copy(0, sibling, m).wait_recv()
-        for way in range(2):
-            step = 2 if way == 0 else -2
-            for hop in range(levels - 1):
-                exists, copy = chain(way, hop, m)
-
-                @pl.when(exists)
-                def _(copy=copy):
-                    copy.wait_send()
-
-                @pl.when(arrives(way, hop))
-                def _(way=way, hop=hop, m=m, step=step):
-                    slot = slot_of(way, hop)
-                    core_copy(slot, c - step * (hop + 1), m).wait_send()
-                    core_copy(slot, sibling - step * (hop + 1), m).wait_recv()
+        x_finish(m)
 
     small_copy.wait()
     rest = small.at[pl.ds(0, devices - 1)]
@@ -710,12 +763,9 @@
         in_specs=[anywhere] * 6,
         out_specs=(anywhere,) * 4,
         scratch_shapes=[
-            dma((n_panels + 3 + micro,)),
+            dma((n_panels + 3,)),
             dma((2,)),
-            dma((2, levels - 1, micro)),
-            dma((2, levels - 1, micro)),
-            dma((2 * levels - 1, micro)),
-            dma((2 * levels - 1, micro)),
+            *chain_scratch(levels, micro),
             dma((n_panels + 1,)),
             dma((n_panels + 1,)),
             dma((n_panels + 2, 2)),
@@ -726,6 +776,1209 @@
         compiler_params=pltpu.CompilerParams(collective_id=1, has_side_effects=True),
         name="gather_all",
     )(x, qkv, expand, dense, shrink, packed)
+
+
+def add_into(dst, srcs, rows):
+    chunk = 16 if dst.shape[-1] > 1024 else 64
+
+    def step(index, carry):
+        at = pl.ds(pl.multiple_of(index * chunk, 16), chunk)
+        total = srcs[0][at, :].astype(jnp.float32)
+        for src in srcs[1:]:
+            total = total + src[at, :].astype(jnp.float32)
+        dst[at, :] = total.astype(dst.dtype)
+        return carry
+
+    lax.fori_loop(0, rows // chunk, step, 0)
+
+
+TILE = 256
+
+
+def turn_tables(length):
+    freqs = jnp.exp(jnp.arange(ROT // 2, dtype=jnp.float32) * (-2.0 * math.log(10000.0) / ROT))
+    angles = jnp.arange(length, dtype=jnp.float32)[:, None] * freqs[None, :]
+    cos, sin = jnp.cos(angles), jnp.sin(angles)
+    rest = jnp.zeros((length, 128 - ROT), jnp.float32)
+    return (
+        jnp.concatenate([cos, cos, rest + 1.0], axis=1),
+        jnp.concatenate([-sin, sin, rest], axis=1),
+    )
+
+
+def turn(head, cos, sin):
+    front = head[:, :128]
+    lane = lax.broadcasted_iota(jnp.int32, front.shape, 1)
+    other = jnp.where(lane < ROT // 2, pltpu.roll(front, 128 - ROT // 2, 1), pltpu.roll(front, ROT // 2, 1))
+    return jnp.concatenate([front * cos + other * sin, head[:, 128:]], axis=1)
+
+
+def dot_nn(a, b):
+    return lax.dot_general(a, b, (((1,), (0,)), ((), ())), preferred_element_type=jnp.float32)
+
+
+def dot_nt(a, b):
+    return lax.dot_general(a, b, (((1,), (1,)), ((), ())), preferred_element_type=jnp.float32)
+
+
+def dot_tn(a, b):
+    return lax.dot_general(a, b, (((0,), (0,)), ((), ())), preferred_element_type=jnp.float32)
+
+
+def forward_kernel(
+    tiles,
+    levels,
+    prefix,
+    x,
+    own_g,
+    panels,
+    out_w,
+    gains,
+    qkv_shift,
+    expand_shift,
+    cos,
+    sin,
+    hidden_attn,
+    hidden_mlp,
+    heads,
+    probs,
+    features,
+    slopes,
+    partial,
+    g_all,
+    head_rows,
+    acts,
+    *g_sems,
+):
+    step = pl.program_id(0)
+    micro = own_g.shape[0]
+    d = lax.axis_index("dp")
+    c = lax.axis_index("ctx")
+    g_start, g_hop, g_finish = chain_gather(own_g, g_all, g_sems, d, c, levels)
+
+    @pl.when(step == 0)
+    def _():
+        greet_line(d, c, levels)
+        for m in range(micro):
+            g_start(m)
+
+    last = 4 * tiles - 1
+    for at, hop, m in ((4, 0, 0), (7, 0, 1), (11, 1, 0), (14, 1, 1)):
+        @pl.when(step == at)
+        def _(hop=hop, m=m):
+            g_hop(hop, m)
+
+    seq = step // (2 * tiles)
+    phase = lax.rem(step, 2 * tiles) // tiles
+    tile = lax.rem(step, tiles)
+    rows = pl.ds(pl.multiple_of(tile * TILE, TILE), TILE)
+    n_expand = panels.shape[0] - 3
+    scale = 1.0 / math.sqrt(HEAD)
+
+    @pl.when(phase == 0)
+    def _():
+        values_in = x[...].astype(jnp.float32)
+        centered = values_in - jnp.mean(values_in, axis=1, keepdims=True)
+        normal = centered * lax.rsqrt(jnp.mean(centered * centered, axis=1, keepdims=True) + 1e-05)
+        hidden_attn[...] = (normal * gains[0:1, :] + gains[1:2, :]).astype(jnp.bfloat16)
+        hidden_mlp[...] = (normal * gains[2:3, :] + gains[3:4, :]).astype(jnp.bfloat16)
+        for part in range(3):
+            joined = dot_nn(hidden_attn[...], panels[part]) + qkv_shift[:, part * HEAD : (part + 1) * HEAD]
+            if part < 2:
+                joined = turn(joined, cos[rows, :], sin[rows, :])
+            joined = joined.astype(jnp.bfloat16)
+            heads[part] = joined
+            head_rows[part, rows, :] = joined
+        for part in range(n_expand):
+            columns = slice(part * HEAD, (part + 1) * HEAD)
+            expanded = dot_nn(hidden_mlp[...], panels[3 + part]) + expand_shift[:, columns]
+            cdf = 0.5 * (1.0 + lax.erf(expanded * (1.0 / math.sqrt(2.0))))
+            acts[rows, columns] = (expanded * cdf).astype(jnp.bfloat16)
+            bell = jnp.exp(-0.5 * expanded * expanded) * (1.0 / math.sqrt(2.0 * math.pi))
+            slopes[:, columns] = (cdf + expanded * bell).astype(jnp.bfloat16)
+
+    @pl.when(phase == 1)
+    def _():
+        scores = dot_nt(head_rows[0, rows, :], head_rows[1]) * scale
+        key_at = lax.broadcasted_iota(jnp.int32, scores.shape, 1)
+        query_at = lax.broadcasted_iota(jnp.int32, scores.shape, 0) + tile * TILE
+        allowed = jnp.logical_or(key_at <= query_at, key_at < prefix[seq])
+        scores = jnp.where(allowed, scores, -1e30)
+        expo = jnp.exp(scores - jnp.max(scores, axis=1, keepdims=True))
+        low_probs = (expo * (1.0 / jnp.sum(expo, axis=1, keepdims=True))).astype(jnp.bfloat16)
+        probs[0] = low_probs
+        features[:, :HEAD] = dot_nn(low_probs, head_rows[2]).astype(jnp.bfloat16)
+        features[:, HEAD:] = acts[rows, :]
+        width = out_w.shape[1]
+        for start in range(0, width, 512):
+            columns = slice(start, start + 512)
+            partial[:, columns] = dot_nn(features[...], out_w[:, columns]).astype(jnp.bfloat16)
+
+    @pl.when(step == last)
+    def _():
+        for m in range(micro):
+            for hop in range(2, levels - 1):
+                g_hop(hop, m)
+        for m in range(micro):
+            g_finish(m)
+
+
+def whole_spec(array):
+    zeros = (0,) * array.ndim
+    return pl.BlockSpec(array.shape, lambda step: zeros, pipeline_mode=pl.Buffered(1))
+
+
+def forward_call(levels, prefix, x, own_g, panels, out_w, gains, qkv_shift, expand_shift, cos, sin):
+    tokens, width = x.shape
+    length = cos.shape[0]
+    tiles = length // TILE
+    steps = 2 * tokens // TILE
+    hidden = expand_shift.shape[1]
+
+    def early(step):
+        seq, at = step // (2 * tiles), lax.rem(step, 2 * tiles)
+        return seq * tiles + jnp.minimum(at, tiles - 1)
+
+    def late(step):
+        seq, at = step // (2 * tiles), lax.rem(step, 2 * tiles)
+        return seq * tiles + jnp.maximum(at - tiles, 0)
+
+    kind = jnp.bfloat16
+    return pl.pallas_call(
+        functools.partial(forward_kernel, tiles, levels),
+        grid=(steps,),
+        out_shape=(
+            jax.ShapeDtypeStruct((tokens, width), kind),
+            jax.ShapeDtypeStruct((tokens, width), kind),
+            jax.ShapeDtypeStruct((3, tokens, HEAD), kind),
+            jax.ShapeDtypeStruct((tokens // length, length, length), kind),
+            jax.ShapeDtypeStruct((tokens, HEAD + hidden), kind),
+            jax.ShapeDtypeStruct((tokens, hidden), kind),
+            jax.ShapeDtypeStruct((tokens, width), kind),
+            jax.ShapeDtypeStruct((tokens // length, length, width), kind),
+        ),
+        in_specs=[
+            pl.BlockSpec(memory_space=pltpu.SMEM),
+            pl.BlockSpec((TILE, width), lambda step: (early(step), 0)),
+            pl.BlockSpec(memory_space=pl.ANY),
+            whole_spec(panels),
+            whole_spec(out_w),
+            whole_spec(gains),
+            whole_spec(qkv_shift),
+            whole_spec(expand_shift),
+            whole_spec(cos),
+            whole_spec(sin),
+        ],
+        out_specs=(
+            pl.BlockSpec((TILE, width), lambda step: (early(step), 0)),
+            pl.BlockSpec((TILE, width), lambda step: (early(step), 0)),
+            pl.BlockSpec((3, TILE, HEAD), lambda step: (0, early(step), 0)),
+            pl.BlockSpec((1, TILE, length), lambda step: (late(step) // tiles, lax.rem(late(step), tiles), 0)),
+            pl.BlockSpec((TILE, HEAD + hidden), lambda step: (late(step), 0)),
+            pl.BlockSpec((TILE, hidden), lambda step: (early(step), 0)),
+            pl.BlockSpec((TILE, width), lambda step: (late(step), 0)),
+            pl.BlockSpec(memory_space=pl.ANY),
+        ),
+        scratch_shapes=[
+            pltpu.VMEM((3, length, HEAD), kind),
+            pltpu.VMEM((length, hidden), kind),
+            *chain_scratch(levels, tokens // length),
+        ],
+        compiler_params=pltpu.CompilerParams(
+            collective_id=3, has_side_effects=True, vmem_limit_bytes=56 * 1024 * 1024
+        ),
+        cost_estimate=pl.CostEstimate(
+            flops=2 * tokens * width * (2 * hidden + 4 * HEAD) + 4 * tokens * length * HEAD,
+            bytes_accessed=64 * 1024 * 1024,
+            transcendentals=0,
+        ),
+        name="forward_part",
+    )(prefix, x, own_g, panels, out_w, gains, qkv_shift, expand_shift, cos, sin)
+
+
+def outside_in(levels):
+    return [levels - 1 - place // 2 if place % 2 == 0 else place // 2 for place in range(levels)]
+
+
+def chain_reduce(own, recv, sems, d, c, levels):
+    chain_send, chain_recv = sems
+    z = c // 2
+    span = recv.shape[2]
+
+    def copy(way, level):
+        return remote(
+            own(level),
+            recv.at[way, level - 1 + way],
+            chain_send.at[way, level],
+            chain_recv.at[way, level],
+            d,
+            c + (2 if way == 0 else -2),
+        )
+
+    def sends(way, level):
+        return z < level if way == 0 else z > level
+
+    def hears(way, level):
+        if way == 0:
+            return jnp.logical_and(z >= 1, z <= level)
+        return jnp.logical_and(z <= levels - 2, z >= level)
+
+    def add(way, level):
+        copy(way, level).wait_recv()
+        add_into(own(level), (own(level), recv.at[way, level - 1 + way]), span)
+
+    def open_level(level):
+        for way, place in ((0, 0), (1, levels - 1)):
+            if place != level:
+                @pl.when(z == place)
+                def _(way=way):
+                    copy(way, level).start()
+
+    def turn_round(index):
+        for level in range(levels):
+            for way in range(2):
+                behind = levels - 1 - level if way == 0 else level
+                place = index - behind if way == 0 else levels - 1 - (index - behind)
+                if behind < index and (place < level if way == 0 else place > level):
+                    @pl.when(z == place)
+                    def _(way=way, level=level):
+                        add(way, level)
+                        copy(way, level).start()
+
+    def end(store):
+        for level in range(levels):
+            for way in range(2):
+                if 0 <= level - 1 + way < levels - 1:
+                    @pl.when(jnp.logical_and(z == level, hears(way, level)))
+                    def _(way=way, level=level):
+                        add(way, level)
+
+            @pl.when(z == level)
+            def _(level=level):
+                store(level).start()
+
+    def finish(store):
+        for level in range(levels):
+            for way in range(2):
+                if 0 <= level - 1 + way < levels - 1:
+                    @pl.when(sends(way, level))
+                    def _(way=way, level=level):
+                        copy(way, level).wait_send()
+
+        store(0).wait()
+
+    return open_level, turn_round, end, finish
+
+
+def square_sum(first, passing, recv, last, final, sems, d, c, count):
+    first_send, first_recv, last_send, last_recv = sems
+    x_mate = d + 1 - 2 * lax.rem(d, 2)
+    y_mate = lax.rem(d + 2, 4)
+    mates = ((x_mate, y_mate), (y_mate, x_mate))
+
+    def first_copy(way, slot):
+        return remote(
+            first(way, slot), recv.at[way, slot], first_send.at[way, slot], first_recv.at[way, slot], mates[way][0], c
+        )
+
+    def last_copy(way):
+        return remote(passing(way), last.at[way], last_send.at[way], last_recv.at[way], mates[way][1], c)
+
+    def pass_on(way):
+        first_copy(way, 1).wait_recv()
+        add_into(passing(way), (passing(way), recv.at[way, 1]), count)
+        last_copy(way).start()
+
+    def arrive(way):
+        first_copy(way, 0).wait_recv()
+        last_copy(way).wait_recv()
+
+    def add_final(way, start, rows):
+        at = pl.ds(start, rows)
+        own = final(way).at[at]
+        add_into(own, (own, recv.at[way, 0, at], last.at[way, at]), rows)
+
+    def finish():
+        for way in range(2):
+            first_copy(way, 0).wait_send()
+            first_copy(way, 1).wait_send()
+            last_copy(way).wait_send()
+
+    return first_copy, pass_on, arrive, add_final, finish
+
+
+def square_scratch():
+    dma = pltpu.SemaphoreType.DMA
+    return [dma((2, 2)), dma((2, 2)), dma((2,)), dma((2,))]
+
+
+def backward_kernel(
+    tiles,
+    dp_size,
+    ctx_size,
+    g,
+    x,
+    panels,
+    out_w,
+    gains,
+    cos,
+    sin,
+    heads,
+    probs,
+    slopes,
+    features,
+    grads,
+    grad_expanded,
+    grad_joined,
+    combined,
+    norm_sums,
+    joined_sums,
+    expand_sums,
+    back_out,
+    shrink_out,
+    dense_out,
+    grad_queries,
+    grad_keys,
+    grad_values,
+    board,
+    back_core,
+    back_chain,
+    left,
+    right,
+    out_own,
+    out_recv,
+    out_last,
+    dense_own,
+    dense_recv,
+    left_sem,
+    right_sem,
+    core_send,
+    core_recv,
+    chain_send,
+    chain_recv,
+    first_send,
+    first_recv,
+    last_send,
+    last_recv,
+    dense_send,
+    dense_sem,
+    store_sem,
+):
+    step = pl.program_id(0)
+    seq = step // (2 * tiles)
+    phase = lax.rem(step, 2 * tiles) // tiles
+    tile = lax.rem(step, tiles)
+    tile = jnp.where(phase == 0, tile, jnp.where(lax.rem(tile, 2) == 0, tiles - 1 - tile // 2, tile // 2))
+    rows = pl.ds(pl.multiple_of(tile * TILE, TILE), TILE)
+    n_expand = panels.shape[0] - 3
+    width = out_w.shape[1]
+    scale = 1.0 / math.sqrt(HEAD)
+
+    d = lax.axis_index("dp")
+    c = lax.axis_index("ctx")
+    z = c // 2
+    core = lax.rem(c, 2)
+    sibling = c + 1 - 2 * core
+    x_mate = d + 1 - 2 * lax.rem(d, 2)
+    y_mate = lax.rem(d + 2, 4)
+    diagonal = 3 - d
+    levels = ctx_size // 2
+    me = d * ctx_size + c
+    span = board.shape[2]
+    share = dense_out.shape[0]
+    unit = (features.shape[1] - HEAD) // dp_size
+    out_half = unit // 2
+    head_half = HEAD // 2
+
+    def left_copy(index):
+        if index == 0:
+            columns = pl.ds(0, HEAD)
+        else:
+            owner = (diagonal, x_mate, y_mate, d)[index - 1]
+            columns = pl.ds(pl.multiple_of(HEAD + owner * unit, HEAD), unit)
+        return pltpu.make_async_copy(features.at[:, columns], left.at[index % 2], left_sem.at[index % 2])
+
+    right_copy = pltpu.make_async_copy(grads, right, right_sem.at[0])
+
+    def compute(index):
+        if index < dp_size:
+            left_copy(index + 1).start()
+        left_copy(index).wait()
+        target = dense_own if index == 0 else out_own.at[index - 1]
+        for start in range(0, width, 1024):
+            columns = slice(start, start + 1024)
+            target[:, columns] = dot_tn(left[index % 2], right[:, columns]).astype(jnp.bfloat16)
+
+    def out_rows(index, way):
+        return out_own.at[index, pl.ds(way * out_half, out_half)]
+
+    first_copy, pass_on, arrive, add_final, square_finish = square_sum(
+        lambda way, slot: out_rows(0 if slot == 1 else 1 + way, way),
+        lambda way: out_rows(2 - way, way),
+        out_recv,
+        out_last,
+        lambda way: out_rows(3, way),
+        (first_send, first_recv, last_send, last_recv),
+        d,
+        c,
+        out_half,
+    )
+
+    def out_store(way):
+        return pltpu.make_async_copy(
+            out_rows(3, way), shrink_out.at[pl.ds(way * out_half, out_half)], store_sem.at[way]
+        )
+
+    source = c // (ctx_size // dp_size)
+    at_source = d == source
+    from_x = x_mate == source
+    from_y = y_mate == source
+    across = diagonal == source
+    per_head = HEAD // share
+
+    def dense_half(way):
+        return dense_own.at[pl.ds(way * head_half, head_half)]
+
+    def dense_copy(way, mate):
+        return remote(dense_half(way), dense_recv.at[way], dense_send.at[way], dense_sem.at[way], mate, c)
+
+    def dense_add(way, mate):
+        dense_copy(way, mate).wait_recv()
+        add_into(dense_half(way), (dense_half(way), dense_recv.at[way]), head_half)
+
+    def dense_open():
+        @pl.when(from_y)
+        def _():
+            dense_copy(0, x_mate).start()
+
+        @pl.when(from_x)
+        def _():
+            dense_copy(1, y_mate).start()
+
+    def dense_second():
+        @pl.when(across)
+        def _():
+            dense_add(0, y_mate)
+            dense_copy(0, y_mate).start()
+            dense_add(1, x_mate)
+            dense_copy(1, x_mate).start()
+
+    def dense_third():
+        @pl.when(from_x)
+        def _():
+            dense_add(0, x_mate)
+            dense_copy(0, x_mate).start()
+
+        @pl.when(from_y)
+        def _():
+            dense_add(1, y_mate)
+            dense_copy(1, y_mate).start()
+
+    first_owner = lax.rem(c, ctx_size // per_head) * per_head
+
+    def dense_chunk(piece):
+        return dense_own.at[pl.ds(piece * share, share)]
+
+    def dense_send_out(piece):
+        return remote(
+            dense_chunk(piece), dense_out, dense_send.at[2 + piece], dense_sem.at[2], d, first_owner + piece
+        )
+
+    def dense_store(piece):
+        return pltpu.make_async_copy(dense_chunk(piece), dense_out, store_sem.at[2])
+
+    def dense_fourth():
+        @pl.when(at_source)
+        def _():
+            dense_add(0, x_mate)
+            dense_add(1, y_mate)
+            for piece in range(per_head):
+                @pl.when(first_owner + piece == c)
+                def _(piece=piece):
+                    dense_store(piece).start()
+
+                @pl.when(first_owner + piece != c)
+                def _(piece=piece):
+                    dense_send_out(piece).start()
+
+    def dense_finish():
+        @pl.when(jnp.logical_or(jnp.logical_or(from_y, across), from_x))
+        def _():
+            dense_copy(0, x_mate).wait_send()
+            dense_copy(1, x_mate).wait_send()
+
+        for piece in range(per_head):
+            @pl.when(jnp.logical_and(at_source, first_owner + piece != c))
+            def _(piece=piece):
+                dense_send_out(piece).wait_send()
+
+        stays = me // per_head == c
+
+        @pl.when(stays)
+        def _():
+            dense_store(0).wait()
+
+        @pl.when(jnp.logical_not(stays))
+        def _():
+            dense_send_out(0).wait_recv()
+
+    def own_block(level):
+        return board.at[level, core]
+
+    def core_copy(level):
+        return remote(
+            board.at[level, 1 - core], back_core.at[level], core_send.at[level], core_recv.at[level], d, sibling
+        )
+
+    def core_add(level):
+        core_copy(level).wait_recv()
+        add_into(own_block(level), (own_block(level), back_core.at[level]), span)
+
+    chain_open, chain_round, chain_end, chain_finish = chain_reduce(
+        own_block, back_chain, (chain_send, chain_recv), d, c, levels
+    )
+
+    def back_store(level):
+        return pltpu.make_async_copy(own_block(level), back_out, store_sem.at[3])
+
+    def at(when):
+        return pl.when(step == when)
+
+    @at(0)
+    def _():
+        greet_all(d, c, dp_size, ctx_size)
+        left_copy(0).start()
+        right_copy.start()
+        norm_sums[...] = jnp.zeros_like(norm_sums)
+        joined_sums[...] = jnp.zeros_like(joined_sums)
+        expand_sums[...] = jnp.zeros_like(expand_sums)
+
+    @at(1)
+    def _():
+        right_copy.wait()
+        compute(0)
+        dense_open()
+
+    @at(2)
+    def _():
+        compute(1)
+        first_copy(0, 1).start()
+        first_copy(1, 1).start()
+
+    @at(3)
+    def _():
+        compute(2)
+        first_copy(0, 0).start()
+        compute(3)
+        first_copy(1, 0).start()
+
+    @at(4)
+    def _():
+        compute(4)
+
+    for place, level in enumerate(outside_in(levels)):
+        @at(tiles + 1 + place)
+        def _(level=level):
+            core_copy(level).start()
+
+        @at(tiles + 2 + place)
+        def _(level=level):
+            core_add(level)
+            chain_open(level)
+
+    @at(6)
+    def _():
+        dense_second()
+
+    @at(7)
+    def _():
+        pass_on(0)
+        pass_on(1)
+
+    @at(10)
+    def _():
+        chain_round(1)
+        dense_third()
+
+    @at(13)
+    def _():
+        chain_round(2)
+        for way in range(2):
+            arrive(way)
+            add_final(way, 0, out_half)
+            out_store(way).start()
+
+    @at(14)
+    def _():
+        dense_fourth()
+
+    @pl.when(phase == 0)
+    def _():
+        low_probs = probs[0]
+        own = dot_nt(g[...], out_w[:HEAD, :]).astype(jnp.bfloat16)
+        grad_probs = dot_nt(own, heads[2])
+        wide = low_probs.astype(jnp.float32)
+        delta = jnp.sum(wide * grad_probs, axis=1, keepdims=True)
+        grad_scores = (wide * (grad_probs - delta)).astype(jnp.bfloat16)
+        grad_queries[rows, :] = dot_nn(grad_scores, heads[1]) * scale
+        more_keys = dot_tn(grad_scores, heads[0, rows, :]) * scale
+        more_values = dot_tn(low_probs, own)
+
+        @pl.when(tile == 0)
+        def _():
+            grad_keys[...] = more_keys
+            grad_values[...] = more_values
+
+        @pl.when(tile > 0)
+        def _():
+            grad_keys[...] += more_keys
+            grad_values[...] += more_values
+
+    @pl.when(phase == 1)
+    def _():
+        for part in range(n_expand):
+            columns = slice(part * HEAD, (part + 1) * HEAD)
+            grad = dot_nt(g[...], out_w[(part + 1) * HEAD : (part + 2) * HEAD, :])
+            grad = (grad * slopes[:, columns].astype(jnp.float32)).astype(jnp.bfloat16)
+            grad_expanded[:, columns] = grad
+            expand_sums[:, columns] += jnp.sum(grad.astype(jnp.float32), axis=0, keepdims=True)
+        cos_rows, sin_rows = cos[rows, :], -sin[rows, :]
+        parts = (
+            turn(grad_queries[rows, :], cos_rows, sin_rows),
+            turn(grad_keys[rows, :], cos_rows, sin_rows),
+            grad_values[rows, :],
+        )
+        for part in range(3):
+            columns = slice(part * HEAD, (part + 1) * HEAD)
+            joined = parts[part].astype(jnp.bfloat16)
+            grad_joined[:, columns] = joined
+            joined_sums[:, columns] += jnp.sum(joined.astype(jnp.float32), axis=0, keepdims=True)
+        values_in = x[...].astype(jnp.float32)
+        mean = jnp.mean(values_in, axis=1, keepdims=True)
+        centered = values_in - mean
+        spread = lax.rsqrt(jnp.mean(centered * centered, axis=1, keepdims=True) + 1e-05)
+        for start in range(0, width, 512):
+            columns = slice(start, start + 512)
+            normal = (x[:, columns].astype(jnp.float32) - mean) * spread
+            total = dot_nt(grad_joined[:, :HEAD], panels[0, columns, :])
+            for part in range(1, 3):
+                total += dot_nt(grad_joined[:, part * HEAD : (part + 1) * HEAD], panels[part, columns, :])
+            other = dot_nt(grad_expanded[:, :HEAD], panels[3, columns, :])
+            for part in range(1, n_expand):
+                other += dot_nt(grad_expanded[:, part * HEAD : (part + 1) * HEAD], panels[3 + part, columns, :])
+            for row, value in ((0, total * normal), (1, total), (2, other * normal), (3, other)):
+                norm_sums[row : row + 1, columns] += jnp.sum(value, axis=0, keepdims=True)
+            value = (total * gains[0:1, columns] + other * gains[2:3, columns]).astype(jnp.bfloat16)
+
+            @pl.when(seq == 0)
+            def _(columns=columns, value=value):
+                for parity in range(2):
+                    board[tile, parity, :, columns] = value[parity * span : (parity + 1) * span]
+
+            @pl.when(seq > 0)
+            def _(columns=columns, value=value):
+                combined[:, columns] = value
+
+    @at(4 * tiles - 1)
+    def _():
+        chain_end(back_store)
+        square_finish()
+        for way in range(2):
+            out_store(way).wait()
+        dense_finish()
+        for level in range(levels):
+            core_copy(level).wait_send()
+        chain_finish(back_store)
+
+
+def backward_call(dp_size, ctx_size, g, x, panels, out_w, gains, cos, sin, heads, probs, slopes, features):
+    tokens, width = x.shape
+    length = cos.shape[0]
+    tiles = length // TILE
+    steps = 2 * tokens // TILE
+    hidden = slopes.shape[1]
+    levels = ctx_size // 2
+    span = length // ctx_size
+    unit = hidden // dp_size
+    share = width // (dp_size * ctx_size)
+    dma = pltpu.SemaphoreType.DMA
+    vmem = pltpu.VMEM
+
+    def first(step):
+        seq, at = step // (2 * tiles), lax.rem(step, 2 * tiles)
+        return seq * tiles + jnp.minimum(at, tiles - 1)
+
+    def mixed_order(place):
+        return jnp.where(lax.rem(place, 2) == 0, tiles - 1 - place // 2, place // 2)
+
+    def second(step):
+        seq, at = step // (2 * tiles), lax.rem(step, 2 * tiles)
+        return seq * tiles + mixed_order(jnp.maximum(at - tiles, 0))
+
+    def both(step):
+        seq, at = step // (2 * tiles), lax.rem(step, 2 * tiles)
+        return seq * tiles + jnp.where(at < tiles, at, mixed_order(at - tiles))
+
+    def late(step):
+        return jnp.where(step < 2 * tiles, mixed_order(0), second(step) - tiles)
+
+    kind = jnp.bfloat16
+    fixed = lambda step: (0, 0)
+    anywhere = pl.BlockSpec(memory_space=pl.ANY)
+    return pl.pallas_call(
+        functools.partial(backward_kernel, tiles, dp_size, ctx_size),
+        grid=(steps,),
+        out_shape=(
+            jax.ShapeDtypeStruct((tokens, hidden), kind),
+            jax.ShapeDtypeStruct((tokens, 3 * HEAD), kind),
+            jax.ShapeDtypeStruct((length, width), kind),
+            jax.ShapeDtypeStruct((8, width), jnp.float32),
+            jax.ShapeDtypeStruct((1, 3 * HEAD), jnp.float32),
+            jax.ShapeDtypeStruct((1, hidden), jnp.float32),
+            jax.ShapeDtypeStruct((span, width), kind),
+            jax.ShapeDtypeStruct((unit, width), kind),
+            jax.ShapeDtypeStruct((share, width), kind),
+        ),
+        in_specs=[
+            pl.BlockSpec((TILE, width), lambda step: (both(step), 0)),
+            pl.BlockSpec((TILE, width), lambda step: (second(step), 0)),
+            whole_spec(panels),
+            whole_spec(out_w),
+            whole_spec(gains),
+            whole_spec(cos),
+            whole_spec(sin),
+            pl.BlockSpec((3, length, HEAD), lambda step: (0, step // (2 * tiles), 0)),
+            pl.BlockSpec((1, TILE, length), lambda step: (first(step) // tiles, lax.rem(first(step), tiles), 0)),
+            pl.BlockSpec((TILE, hidden), lambda step: (second(step), 0)),
+            anywhere,
+            anywhere,
+        ],
+        out_specs=(
+            pl.BlockSpec((TILE, hidden), lambda step: (second(step), 0)),
+            pl.BlockSpec((TILE, 3 * HEAD), lambda step: (second(step), 0)),
+            pl.BlockSpec((TILE, width), lambda step: (late(step), 0)),
+            pl.BlockSpec((8, width), fixed),
+            pl.BlockSpec((1, 3 * HEAD), fixed),
+            pl.BlockSpec((1, hidden), fixed),
+            anywhere,
+            anywhere,
+            anywhere,
+        ),
+        scratch_shapes=[
+            vmem((length, HEAD), jnp.float32),
+            vmem((length, HEAD), jnp.float32),
+            vmem((length, HEAD), jnp.float32),
+            vmem((levels, 2, span, width), kind),
+            vmem((levels, span, width), kind),
+            vmem((2, levels - 1, span, width), kind),
+            vmem((2, tokens, HEAD), kind),
+            vmem((tokens, width), kind),
+            vmem((dp_size, unit, width), kind),
+            vmem((2, 2, unit // 2, width), kind),
+            vmem((2, unit // 2, width), kind),
+            vmem((HEAD, width), kind),
+            vmem((2, HEAD // 2, width), kind),
+            dma((2,)),
+            dma((1,)),
+            dma((levels,)),
+            dma((levels,)),
+            dma((2, levels)),
+            dma((2, levels)),
+            *square_scratch(),
+            dma((2 + HEAD // share,)),
+            dma((3,)),
+            dma((4,)),
+        ],
+        compiler_params=pltpu.CompilerParams(
+            collective_id=4, has_side_effects=True, vmem_limit_bytes=60 * 1024 * 1024
+        ),
+        name="backward_part",
+    )(g, x, panels, out_w, gains, cos, sin, heads, probs, slopes, features, g)
+
+
+def reduce_kernel(
+    dp_size,
+    ctx_size,
+    back,
+    hidden_attn,
+    hidden_mlp,
+    grad_joined,
+    grad_expanded,
+    board,
+    back_out,
+    attn_out,
+    mlp_out,
+    tail_out,
+    back_own,
+    back_core,
+    back_chain,
+    left,
+    right_attn,
+    right_mlp,
+    attn_own,
+    attn_recv,
+    attn_last,
+    mlp_own,
+    mlp_recv,
+    mlp_last,
+    board_recv,
+    load_sem,
+    left_sem,
+    right_sem,
+    core_send,
+    core_recv,
+    chain_send,
+    chain_recv,
+    first_send_a,
+    first_recv_a,
+    last_send_a,
+    last_recv_a,
+    first_send_m,
+    first_recv_m,
+    last_send_m,
+    last_recv_m,
+    row_send,
+    row_recv,
+    board_sem,
+    store_sem,
+):
+    d = lax.axis_index("dp")
+    c = lax.axis_index("ctx")
+    core = lax.rem(c, 2)
+    sibling = c + 1 - 2 * core
+    x_mate = d + 1 - 2 * lax.rem(d, 2)
+    y_mate = lax.rem(d + 2, 4)
+    diagonal = 3 - d
+    span = back.shape[0] // ctx_size
+    levels = ctx_size // 2
+    devices = dp_size * ctx_size
+    me = d * ctx_size + c
+    group_rows = hidden_attn.shape[1] // dp_size
+    half = group_rows // 2
+    rows = group_rows // ctx_size
+
+    greet_all(d, c, dp_size, ctx_size)
+
+    def back_view(parity, level):
+        start = (2 * level + parity) * span
+        return back.at[pl.ds(pl.multiple_of(start, span), span)]
+
+    def back_load(level):
+        return pltpu.make_async_copy(back_view(core, level), back_own.at[level], load_sem.at[level])
+
+    def core_copy(level):
+        return remote(
+            back_view(1 - core, level), back_core.at[level], core_send.at[level], core_recv.at[level], d, sibling
+        )
+
+    order = outside_in(levels)
+
+    tile_of = []
+    for owners in ((diagonal, diagonal), (x_mate, y_mate), (y_mate, x_mate), (d, d)):
+        for way in range(2):
+            tile_of.append((owners[way], way))
+    sequence = [(0, index) for index in range(6)]
+    sequence += [(1, index) for index in range(4)]
+    sequence += [(0, index) for index in range(6, 8)]
+    sequence += [(1, index) for index in range(4, 8)]
+
+    def left_copy(place):
+        kind, index = sequence[place]
+        owner, way = tile_of[index]
+        columns = pl.ds(pl.multiple_of(owner * group_rows + way * half, half), half)
+        source = (hidden_attn, hidden_mlp)[kind]
+        return pltpu.make_async_copy(source.at[:, columns], left.at[place % 2], left_sem.at[place % 2])
+
+    right_copies = (
+        pltpu.make_async_copy(grad_joined, right_attn, right_sem.at[0]),
+        pltpu.make_async_copy(grad_expanded, right_mlp, right_sem.at[1]),
+    )
+
+    def compute(kind, index):
+        place = sequence.index((kind, index))
+        if place + 1 < len(sequence):
+            left_copy(place + 1).start()
+        left_copy(place).wait()
+        if index == 0:
+            right_copies[kind].wait()
+        target, right = ((attn_own, right_attn), (mlp_own, right_mlp))[kind]
+        target[index] = dot_tn(left[place % 2], right[...]).astype(jnp.bfloat16)
+
+    def square(own, recv, last, sems):
+        return square_sum(
+            lambda way, slot: own.at[way + 2 * (1 - slot)],
+            lambda way: own.at[4 + way],
+            recv,
+            last,
+            lambda way: own.at[6 + way],
+            sems,
+            d,
+            c,
+            half,
+        )
+
+    squares = (
+        square(attn_own, attn_recv, attn_last, (first_send_a, first_recv_a, last_send_a, last_recv_a)),
+        square(mlp_own, mlp_recv, mlp_last, (first_send_m, first_recv_m, last_send_m, last_recv_m)),
+    )
+
+    per_half = half // rows
+
+    def row_chunk(kind, way, piece):
+        return (attn_own, mlp_own)[kind].at[6 + way, pl.ds(piece * rows, rows)]
+
+    def row_copy(kind, way, piece):
+        target = way * per_half + piece
+        out = (attn_out, mlp_out)[kind]
+        return remote(
+            row_chunk(kind, way, piece), out.at[c], row_send.at[kind, target], row_recv.at[kind], d, target
+        )
+
+    def row_local(kind, way, piece):
+        out = (attn_out, mlp_out)[kind]
+        return pltpu.make_async_copy(row_chunk(kind, way, piece), out.at[c], store_sem.at[kind])
+
+    def tile_end(kind):
+        first_copy, pass_on, arrive, add_final, finish = squares[kind]
+        for way in range(2):
+            arrive(way)
+            for piece in range(per_half):
+                add_final(way, piece * rows, rows)
+                target = way * per_half + piece
+
+                @pl.when(c != target)
+                def _(way=way, piece=piece):
+                    row_copy(kind, way, piece).start()
+
+                @pl.when(c == target)
+                def _(way=way, piece=piece):
+                    row_local(kind, way, piece).start()
+
+    board_load = pltpu.make_async_copy(board.at[me], board_recv.at[me], load_sem.at[levels])
+
+    def board_start():
+        board_load.start()
+
+        def push_board(step, carry):
+            other = lax.rem(me + step, devices)
+            remote(
+                board.at[other],
+                board_recv.at[me],
+                board_sem.at[0],
+                board_sem.at[1],
+                other // ctx_size,
+                lax.rem(other, ctx_size),
+            ).start()
+            return carry
+
+        lax.fori_loop(1, devices, push_board, 0)
+
+    def board_end():
+        board_load.wait()
+        rest = board_recv.at[pl.ds(0, devices - 1)]
+        remote(rest, rest, board_sem.at[0], board_sem.at[1], d, sibling).wait()
+        tail_out[...] = jnp.sum(board_recv[...], axis=0)
+
+    chain_open, chain_round, chain_end, chain_finish = chain_reduce(
+        lambda level: back_own.at[level], back_chain, (chain_send, chain_recv), d, c, levels
+    )
+
+    def back_store(level):
+        return pltpu.make_async_copy(back_own.at[level], back_out, store_sem.at[2])
+
+    right_copies[0].start()
+    left_copy(0).start()
+    for level in order:
+        core_copy(level).start()
+        back_load(level).start()
+    right_copies[1].start()
+
+    for way in range(2):
+        compute(0, way)
+        squares[0][0](way, 1).start()
+    for way in range(2):
+        compute(0, 2 + way)
+        squares[0][0](way, 0).start()
+    for level in order:
+        back_load(level).wait()
+        core_copy(level).wait_recv()
+        own = back_own.at[level]
+        add_into(own, (own, back_core.at[level]), span)
+        chain_open(level)
+    compute(0, 4)
+    compute(0, 5)
+    squares[0][1](0)
+    squares[0][1](1)
+    for way in range(2):
+        compute(1, way)
+        squares[1][0](way, 1).start()
+    for way in range(2):
+        compute(1, 2 + way)
+        squares[1][0](way, 0).start()
+    chain_round(1)
+    board_start()
+    compute(0, 6)
+    compute(0, 7)
+    compute(1, 4)
+    compute(1, 5)
+    tile_end(0)
+    chain_round(2)
+    compute(1, 6)
+    compute(1, 7)
+    squares[1][1](0)
+    squares[1][1](1)
+    chain_end(back_store)
+    tile_end(1)
+    board_end()
+
+    for kind in range(2):
+        squares[kind][4]()
+        for way in range(2):
+            for piece in range(per_half):
+                target = way * per_half + piece
+
+                @pl.when(c != target)
+                def _(kind=kind, way=way, piece=piece):
+                    row_copy(kind, way, piece).wait_send()
+
+        out = (attn_out, mlp_out)[kind]
+        rest = out.at[pl.ds(0, ctx_size - 1)]
+        remote(rest, rest, row_send.at[kind, 0], row_recv.at[kind], d, sibling).wait_recv()
+        row_local(kind, 0, 0).wait()
+    for level in range(levels):
+        core_copy(level).wait_send()
+    chain_finish(back_store)
+
+
+def reduce_call(dp_size, ctx_size, back, hidden_attn, hidden_mlp, grad_joined, grad_expanded, board):
+    length, width = back.shape
+    tokens = hidden_attn.shape[0]
+    span = length // ctx_size
+    group_rows = width // dp_size
+    half = group_rows // 2
+    rows = group_rows // ctx_size
+    joined, hidden = grad_joined.shape[1], grad_expanded.shape[1]
+    levels = ctx_size // 2
+    devices = dp_size * ctx_size
+    dma = pltpu.SemaphoreType.DMA
+    kind = back.dtype
+    vmem = pltpu.VMEM
+    out_shape = (
+        jax.ShapeDtypeStruct((span, width), kind),
+        jax.ShapeDtypeStruct((ctx_size, rows, joined), kind),
+        jax.ShapeDtypeStruct((ctx_size, rows, hidden), kind),
+        jax.ShapeDtypeStruct(board.shape[1:], jnp.float32),
+    )
+    anywhere = pl.BlockSpec(memory_space=pl.ANY)
+    return pl.pallas_call(
+        functools.partial(reduce_kernel, dp_size, ctx_size),
+        out_shape=out_shape,
+        in_specs=[anywhere] * 6,
+        out_specs=(anywhere,) * 3 + (pl.BlockSpec(memory_space=pltpu.VMEM),),
+        scratch_shapes=[
+            vmem((levels, span, width), kind),
+            vmem((levels, span, width), kind),
+            vmem((2, levels - 1, span, width), kind),
+            vmem((2, tokens, HEAD), kind),
+            vmem((tokens, joined), kind),
+            vmem((tokens, hidden), kind),
+            vmem((8, half, joined), kind),
+            vmem((2, 2, half, joined), kind),
+            vmem((2, half, joined), kind),
+            vmem((8, half, hidden), kind),
+            vmem((2, 2, half, hidden), kind),
+            vmem((2, half, hidden), kind),
+            vmem((devices,) + board.shape[1:], jnp.float32),
+            dma((levels + 1,)),
+            dma((2,)),
+            dma((2,)),
+            dma((levels,)),
+            dma((levels,)),
+            dma((2, levels)),
+            dma((2, levels)),
+            *square_scratch(),
+            *square_scratch(),
+            dma((2, ctx_size)),
+            dma((2,)),
+            dma((2,)),
+            dma((3,)),
+        ],
+        compiler_params=pltpu.CompilerParams(
+            collective_id=2, has_side_effects=True, vmem_limit_bytes=60 * 1024 * 1024
+        ),
+        name="reduce_all",
+    )(back, hidden_attn, hidden_mlp, grad_joined, grad_expanded, board)
+
+
+def finish_kernel(
+    attn_rows,
+    mlp_rows,
+    shrink_rows,
+    dense_rows,
+    back_first,
+    back_last,
+    x,
+    g,
+    reduced,
+    out_shift,
+    qkv_grad,
+    expand_grad,
+    shrink_grad,
+    dense_grad,
+    layer_output,
+    input_grad,
+):
+    ctx_size = attn_rows.shape[0]
+    for rows, target in ((attn_rows, qkv_grad), (mlp_rows, expand_grad)):
+        for member in range(ctx_size):
+            for part in range(rows.shape[2] // HEAD):
+                start = (part * ctx_size + member) * HEAD
+                target[:, start : start + HEAD] = rows[member, :, part * HEAD : (part + 1) * HEAD].astype(jnp.float32)
+    shrink_grad[...] = shrink_rows[...].astype(jnp.float32)
+    dense_grad[...] = dense_rows[...].astype(jnp.float32)
+    for m, back in enumerate((back_first, back_last)):
+        own = x[m].astype(jnp.float32)
+        layer_output[m] = (own + reduced[m].astype(jnp.float32) + out_shift[...]).astype(jnp.bfloat16)
+        centered = own - jnp.mean(own, axis=1, keepdims=True)
+        spread = lax.rsqrt(jnp.mean(centered * centered, axis=1, keepdims=True) + 1e-05)
+        normal = centered * spread
+        grad = back[...].astype(jnp.float32)
+        share = spread * (
+            grad
+            - jnp.mean(grad, axis=1, keepdims=True)
+            - normal * jnp.mean(grad * normal, axis=1, keepdims=True)
+        )
+        input_grad[m] = (g[m].astype(jnp.float32) + share).astype(jnp.bfloat16)
+
+
+def finish_call(attn_rows, mlp_rows, shrink_rows, dense_rows, back_first, back_last, x, g, reduced, out_shift):
+    steps = 4
+    arrays = (attn_rows, mlp_rows, shrink_rows, dense_rows, back_first, back_last, x, g, reduced)
+    micro = x.shape[0]
+    ctx_size, rows, joined = attn_rows.shape
+
+    def spec(shape):
+        block = shape[:-2] + (shape[-2] // steps, shape[-1])
+        lead = (0,) * (len(shape) - 2)
+        return pl.BlockSpec(block, lambda step: lead + (step, 0))
+
+    outs = (
+        jax.ShapeDtypeStruct((rows, joined * ctx_size), jnp.float32),
+        jax.ShapeDtypeStruct((rows, mlp_rows.shape[2] * ctx_size), jnp.float32),
+        jax.ShapeDtypeStruct(shrink_rows.shape, jnp.float32),
+        jax.ShapeDtypeStruct(dense_rows.shape, jnp.float32),
+        jax.ShapeDtypeStruct(x.shape, jnp.bfloat16),
+        jax.ShapeDtypeStruct(x.shape, jnp.bfloat16),
+    )
+    return pl.pallas_call(
+        finish_kernel,
+        grid=(steps,),
+        out_shape=outs,
+        in_specs=[spec(array.shape) for array in arrays] + [whole_spec(out_shift)],
+        out_specs=tuple(spec(out.shape) for out in outs),
+        compiler_params=pltpu.CompilerParams(vmem_limit_bytes=40 * 1024 * 1024),
+        name="finish_part",
+    )(*arrays, out_shift)
 
 
 def tensor_shards(
@@ -766,15 +2019,12 @@
     )
     own_x = layer_input.reshape(sequences, span, width)
     own_g = out_grad.reshape(sequences, span, width)
-    g_all = lax.all_gather(own_g, "ctx", axis=1, tiled=True).reshape(tokens, width)
     count = packed.shape[0]
     packed = jnp.pad(packed, (0, -count % 2048)).reshape(-1, 128)
     x_all, panels, out_part, small = gather_call(
         dp_size, ctx_size, own_x, qkv_weight, expand_weight, dense_weight, shrink_weight, packed
     )
     x_all = x_all.reshape(tokens, width)
-    qkv_part = panels[:3]
-    expand_part = panels[3:]
     small = unpack_small(small.reshape(devices, -1)[:, :count], lengths, devices)
     gain_attn, shift_attn, gain_mlp, shift_mlp, qkv_shift, dense_shift, expand_shift, shrink_shift = small
     qkv_shift = lax.dynamic_slice_in_dim(qkv_shift.reshape(3, ctx_size, HEAD), me, 1, 1).reshape(-1)
@@ -782,119 +2032,46 @@
         expand_shift.reshape(dp_size, ctx_size, unit), me, 1, 1
     ).reshape(-1)
 
-    inputs = x_all.astype(jnp.float32)
-    row_mean = jnp.mean(inputs, axis=-1, keepdims=True)
-    centered = inputs - row_mean
-    spread = lax.rsqrt(jnp.mean(centered * centered, axis=-1, keepdims=True) + 1e-05)
-    normal = centered * spread
-    hidden_attn = low(normal * gain_attn + shift_attn)
-    hidden_mlp = low(normal * gain_mlp + shift_mlp)
-
-    cos_table, sin_table = rope_tables(jnp.arange(SEQ, dtype=jnp.float32))
-    joined = jnp.einsum("td,pde->tpe", hidden_attn, qkv_part, preferred_element_type=jnp.float32)
-    joined = joined.reshape(tokens, -1) + qkv_shift
-    joined = joined.reshape(sequences, SEQ, 3, HEAD)
-
-    def turn(heads, sin_values):
-        return rotate(heads[:, :, None, :], cos_table, sin_values)[:, :, 0]
-
-    queries = low(turn(joined[:, :, 0], sin_table))
-    key_rows = low(turn(joined[:, :, 1], sin_table))
-    value_rows = low(joined[:, :, 2])
-    positions = jnp.arange(SEQ, dtype=jnp.int32)
-    prefix = prefix_len.reshape(sequences)
-    allowed = (positions[None, :] <= positions[:, None])[None] | (
-        positions[None, None, :] < prefix[:, None, None]
-    )
-    scores = jnp.einsum("sqe,ske->sqk", queries, key_rows, preferred_element_type=jnp.float32) * scale
-    scores = jnp.where(allowed, scores, -1e30)
-    expo = jnp.exp(scores - jnp.max(scores, axis=-1, keepdims=True))
-    probs = expo / jnp.sum(expo, axis=-1, keepdims=True)
-    probs_low = low(probs)
-    mixed = low(
-        jnp.einsum("sqk,ske->sqe", probs_low, value_rows, preferred_element_type=jnp.float32)
-    ).reshape(tokens, HEAD)
-    expanded = jnp.einsum("td,pde->tpe", hidden_mlp, expand_part, preferred_element_type=jnp.float32)
-    expanded = expanded.reshape(tokens, -1) + expand_shift
-    activated = low(gelu_exact(expanded))
-    features = jnp.concatenate([mixed, activated], axis=1)
-    partial = low(jnp.dot(features, out_part, preferred_element_type=jnp.float32))
+    gains = jnp.stack([gain_attn, shift_attn, gain_mlp, shift_mlp])
+    cos, sin = turn_tables(SEQ)
+    hidden_attn, hidden_mlp, heads, probs, features, slopes, partial, g_all = forward_call(
+        ctx_size // 2,
+        prefix_len.reshape(sequences),
+        x_all,
+        own_g,
+        panels,
+        out_part,
+        gains,
+        qkv_shift[None],
+        expand_shift[None],
+        cos,
+        sin,
+    )
+    g_all = g_all.reshape(tokens, width)
     reduced = lax.psum_scatter(
         partial.reshape(sequences, SEQ, width), "ctx", scatter_dimension=1, tiled=True
     )
-    layer_output = low(
-        own_x.astype(jnp.float32) + reduced.astype(jnp.float32) + (dense_shift + shrink_shift)
-    ).reshape(layer_input.shape)
-
-    out_grads = low(contract_rows(features, g_all))
-    grad_features = contract_cols(g_all, out_part)
-    unused, gelu_back = jax.vjp(gelu_exact, expanded)
-    grad_expanded = low(gelu_back(grad_features[:, HEAD:])[0])
-    grad_mixed = low(grad_features[:, :HEAD]).reshape(sequences, SEQ, HEAD)
-    shrink_grad = lax.psum_scatter(out_grads[HEAD:], "dp", scatter_dimension=0, tiled=True)
-    dense_own = jnp.zeros((ctx_size, HEAD, width), jnp.bfloat16)
-    dense_own = lax.dynamic_update_slice(dense_own, out_grads[:HEAD][None], (me, 0, 0))
-    dense_grad = lax.psum_scatter(
-        dense_own.reshape(ctx_size * HEAD, width), ("dp", "ctx"), scatter_dimension=0, tiled=True
-    )
-    expand_grads = low(contract_rows(hidden_mlp, grad_expanded))
-    back_mlp = jnp.einsum(
-        "tpe,pde->td",
-        grad_expanded.reshape(tokens, -1, HEAD),
-        expand_part,
-        preferred_element_type=jnp.float32,
-    )
-
-    grad_probs = jnp.einsum("sqe,ske->sqk", grad_mixed, value_rows, preferred_element_type=jnp.float32)
-    delta = jnp.sum(probs * grad_probs, axis=-1, keepdims=True)
-    grad_scores = low(probs * (grad_probs - delta))
-    grad_queries = (
-        jnp.einsum("sqk,ske->sqe", grad_scores, key_rows, preferred_element_type=jnp.float32) * scale
-    )
-    grad_keys = (
-        jnp.einsum("sqk,sqe->ske", grad_scores, queries, preferred_element_type=jnp.float32) * scale
-    )
-    grad_values = jnp.einsum("sqk,sqe->ske", probs_low, grad_mixed, preferred_element_type=jnp.float32)
-    grad_joined = low(
-        jnp.concatenate([turn(grad_queries, -sin_table), turn(grad_keys, -sin_table), grad_values], axis=-1)
-    ).reshape(tokens, 3 * HEAD)
-    qkv_grads = low(contract_rows(hidden_attn, grad_joined))
-    back_attn = jnp.einsum(
-        "tpe,pde->td",
-        grad_joined.reshape(tokens, -1, HEAD),
-        qkv_part,
-        preferred_element_type=jnp.float32,
-    )
-    column_grads = jnp.concatenate([qkv_grads, expand_grads], axis=1)
-    column_grads = lax.psum_scatter(column_grads, "dp", scatter_dimension=0, tiled=True)
-    column_grads = lax.all_to_all(column_grads, "ctx", split_axis=0, concat_axis=0, tiled=True)
-    column_grads = column_grads.reshape(ctx_size, row_share, 3 + dp_size, HEAD)
-    column_grads = jnp.transpose(column_grads, (1, 2, 0, 3)).astype(jnp.float32)
-    qkv_grad = column_grads[:, :3].reshape(row_share, 3 * width)
-    expand_grad = column_grads[:, 3:].reshape(row_share, ff)
-
-    combined = low(back_attn * gain_attn + back_mlp * gain_mlp)
-    combined = lax.psum_scatter(
-        combined.reshape(sequences, SEQ, width), "ctx", scatter_dimension=1, tiled=True
-    ).astype(jnp.float32)
-    own = own_x.astype(jnp.float32)
-    own_center = own - jnp.mean(own, axis=-1, keepdims=True)
-    own_spread = lax.rsqrt(jnp.mean(own_center * own_center, axis=-1, keepdims=True) + 1e-05)
-    own_normal = own_center * own_spread
-    share = own_spread * (
-        combined
-        - jnp.mean(combined, axis=-1, keepdims=True)
-        - own_normal * jnp.mean(combined * own_normal, axis=-1, keepdims=True)
-    )
-    input_grad = low(own_g.astype(jnp.float32) + share).reshape(layer_input.shape)
+
+    (
+        grad_expanded,
+        grad_joined,
+        combined,
+        norm_sums,
+        joined_sum,
+        expand_sum,
+        back_first,
+        shrink_rows,
+        dense_rows,
+    ) = backward_call(
+        dp_size, ctx_size, g_all, x_all, panels, out_part, gains, cos, sin, heads, probs, slopes, features
+    )
+    joined_sum, expand_sum = joined_sum[0], expand_sum[0]
 
     def place(values, parts):
         board = jnp.zeros((parts, ctx_size, values.shape[0] // parts), jnp.float32)
         board = lax.dynamic_update_slice(board, values.reshape(parts, 1, -1), (0, me, 0))
         return board.reshape(devices, -1)
 
-    joined_sum = jnp.sum(grad_joined.astype(jnp.float32), axis=0)
-    expand_sum = jnp.sum(grad_expanded.astype(jnp.float32), axis=0)
     out_sum = jnp.sum(own_g.astype(jnp.float32), axis=(0, 1))
     board = jnp.concatenate(
         [
@@ -902,14 +2079,33 @@
             place(joined_sum[2 * HEAD :], 1),
             out_sum.reshape(devices, -1),
             place(expand_sum, dp_size),
-            jnp.sum(back_attn * normal, axis=0).reshape(devices, -1),
-            jnp.sum(back_attn, axis=0).reshape(devices, -1),
-            jnp.sum(back_mlp * normal, axis=0).reshape(devices, -1),
-            jnp.sum(back_mlp, axis=0).reshape(devices, -1),
+            norm_sums[0].reshape(devices, -1),
+            norm_sums[1].reshape(devices, -1),
+            norm_sums[2].reshape(devices, -1),
+            norm_sums[3].reshape(devices, -1),
         ],
         axis=1,
     )
-    tail = lax.psum_scatter(board, ("dp", "ctx"), scatter_dimension=0, tiled=True).reshape(-1)
+    used = board.shape[1]
+    board = jnp.pad(board, ((0, 0), (0, -used % 1024))).reshape(devices, -1, 128)
+    back_last, attn_rows, mlp_rows, tail = reduce_call(
+        dp_size, ctx_size, combined, hidden_attn, hidden_mlp, grad_joined, grad_expanded, board
+    )
+    qkv_grad, expand_grad, shrink_grad, dense_grad, layer_output, input_grad = finish_call(
+        attn_rows,
+        mlp_rows,
+        shrink_rows,
+        dense_rows,
+        back_first,
+        back_last,
+        own_x,
+        own_g,
+        reduced,
+        (dense_shift + shrink_shift)[None],
+    )
+    layer_output = layer_output.reshape(layer_input.shape)
+    input_grad = input_grad.reshape(layer_input.shape)
+    tail = tail.reshape(-1)
     share_len = width // devices
     at = 0
     pieces = []
@@ -922,11 +2118,11 @@
         qkv_grad,
         pieces[0],
         pieces[1],
-        dense_grad.astype(jnp.float32),
+        dense_grad,
         pieces[2],
         expand_grad,
         pieces[3],
-        shrink_grad.astype(jnp.float32),
+        shrink_grad,
         pieces[2],
         pieces[4],
         pieces[5],

time: 1090 us -> 503 us (0.46)
  waiting for transfers between devices: 523 us -> 0.02 us
  Pallas kernels: 203 us -> 452 us
  matrix products: 175 us -> 0 us
  local copies, waits for them, and re-layouts: 90.9 us -> 23.9 us
  other arithmetic: 66.3 us -> 4.79 us
    pallas_call x0 -> x4, Pallas kernels: none -> 329 us  [the longest x1 137 us: backward_call(): pl.pallas_call(functools.partial(backward_kernel, tiles, dp_size, ctx_siz...]
    reduce_scatter x4 -> x0, waiting for transfers between devices: 304 us -> none  [the longest x1 142 us: tensor_shards(): lax.psum_scatter(dense_own.reshape(ctx_size * HEAD, width), ('dp', 'ctx')...]
    dot_general x14 -> x0, matrix products: 167 us -> none  [the longest x3 37.1 us: contract_rows(): lax.dot_general(left_mat, right_mat, (((0,), (0,)), ((), ())), preferred_...]
    unnamed x8 -> x1, waiting for transfers between devices: 130 us -> 0.02 us
    reduce_scatter x1, waiting for transfers between devices: 88.5 us -> 0.01 us  [tensor_shards(): lax.psum_scatter(partial.reshape(sequences, SEQ, width), 'ctx', scatter_d...]
    pallas_call x1, Pallas kernels: 203 us -> 123 us  [gather_call(): pl.pallas_call(functools.partial(gather_kernel, dp_size, ctx_size), out_s...]
    convert_element_type x5 -> x0, other arithmetic: 25.8 us -> none  [the longest x3 21.2 us: low(): return values.astype(jnp.bfloat16)]
    dot_general x4 -> x0, local copies, waits for them, and re-layouts: 15.9 us -> none  [the longest x2 10.7 us: tensor_shards(): jnp.einsum('td,pde->tpe', hidden_mlp, expand_part, preferred_element_type...]
  transfers between devices with their start and end apart: 8 -> 1, of which waited for: 6 -> 0; matrix products, arithmetic and copies ran while one was open for 15% -> 2% of each run, Pallas kernels for 19% -> 49%
where the time goes in v5:
time: 503 us; the launch traced here: 495 us
  Pallas kernels  452 us (90%)
  local copies, waits for them, and re-layouts  23.9 us (5%)
  between operations  14.6 us (3%)
    pallas_call x1, Pallas kernels, backward_call(): pl.pallas_call(functools.partial(backward_kernel, tiles, dp_size, ctx_siz...  137 us
    pallas_call x1, Pallas kernels, gather_call(): pl.pallas_call(functools.partial(gather_kernel, dp_size, ctx_size), out_s...  123 us
    pallas_call x1, Pallas kernels, reduce_call(): pl.pallas_call(functools.partial(reduce_kernel, dp_size, ctx_size), out_s...  108 us
    pallas_call x1, Pallas kernels, forward_call(): pl.pallas_call(functools.partial(forward_kernel, tiles, levels), grid=(st...  80.3 us
  transfers between devices with their start and end apart: 1, of which 0 were waited for; matrix products, arithmetic and copies ran while one was open for 2% of the time, Pallas kernels for 49%

profile of v5, /device:TPU:9, one launch (start us, length us, event | category | flops | bytes accessed | tf_op | source)
XLA Modules:
  0.0 495.0 jit_solution(8233956311249590573)
XLA Ops:
  7.2 0.0 reduce-scatter.2.cloned.1.call-start
  7.2 5.4 %concatenate.12 = bf16[832]{0:T(1024)(128)(2,1)S(1)} concatenate(bf16[64]{0:T(256)(128)(2,1)} %param.26, bf16[64]{0:T(256)(128)(2,1)} %param.27, bf16[64]{0:T(256)(128)(2,1)} %param.28, bf16[64]{0:T(256)(128)(2,1)} %param.29, bf16[192]{0:T(256)(128)(2,1)} %param.19, bf16[64]{0:T(256)(128)(2,1)} %param.21, bf16[256]{0:T(256)(128)(2,1)} %param.23, bf16[64]{0:T(256)(128)(2,1)} %param.25), dimensions={0} | concatenate | bytes 3328 | tf_op jit(solution)/shard_map/concatenate | solution.py:2017
  12.7 0.6 pad_bitcast_fusion.1.packed
  13.3 122.8 %gather_all.1 = (bf16[2,1024,2048]{2,1,0:T(8,128)(2,1)}, bf16[7,2048,256]{2,1,0:T(8,128)(2,1)}, bf16[1280,2048]{1,0:T(8,128)(2,1)}, bf16[32,16,128]{2,1,0:T(8,128)(2,1)}) custom-call(bf16[2,128,2048]{2,1,0:T(8,128)(2,1)} %bitcast.37, bf16[64,6144]{1,0:T(8,128)(2,1)} %qkv.1, bf16[64,8192]{1,0:T(8,128)(2,1)} %expand.1, bf16[64,2048]{1,0:T(8,128)(2,1)} %dense.1, ...), custom_call_target="tpu_custom_call" | custom-call | tf_op jit(solution)/shard_map/gather_all/pallas_call | solution.py:760
  136.1 0.9 copy.50
  137.0 0.1 fusion.3
  137.1 0.1 pad.15.clone
  137.2 0.1 pad.12.clone
  137.3 2.0 fusion.2
  139.2 0.1 reshape.203
  139.3 0.6 dynamic-slice_convert_fusion
  139.9 0.6 constant_dynamic-slice_fusion
  140.5 0.1 convert_element_type.87
  140.6 0.1 convert_element_type.90
  140.7 0.1 convert_element_type.89
  140.8 0.1 convert_element_type.88
  140.9 0.7 maximum_convert_fusion.gains
  141.5 1.3 maximum_maximum_fusion
  142.8 80.3 %forward_part.1 = (bf16[2048,2048]{1,0:T(8,128)(2,1)}, bf16[2048,2048]{1,0:T(8,128)(2,1)}, bf16[3,2048,256]{2,1,0:T(8,128)(2,1)}, bf16[2,1024,1024]{2,1,0:T(8,12...) custom-call(s32[2]{0:T(128)} %bitcast.60, ...), custom_call_target="tpu_custom_call" | custom-call | flops 27917287424 | bytes 67108864 | tf_op jit(solution)/shard_map/forward_part/pallas_call | solution.py:947
  223.1 0.0 reduce-scatter.2.cloned.1.call-update
  223.1 1.2 copy-done.1
  224.3 0.2 convert_reduce_fusion
  224.5 0.1 reshape.196
  224.6 0.1 convert_add_fusion
  224.6 0.1 add.32.out_shift
  224.7 136.6 %backward_part.1 = (bf16[2048,1024]{1,0:T(8,128)(2,1)}, bf16[2048,768]{1,0:T(8,128)(2,1)}, bf16[1024,2048]{1,0:T(8,128)(2,1)}, f32[8,2048]{1,0:T(8,128)}, f32[1,...) custom-call(bf16[2048,2048]{1,0:T(8,128)(2,1)} %bitcast.41, ...), custom_call_target="tpu_custom_call" | custom-call | tf_op jit(solution)/shard_map/backward_part/pallas_call | solution.py:1528
  361.3 0.7 slice.89
  362.1 0.6 slice_bitcast_fusion.2
  362.7 0.1 reshape.195
  362.8 1.1 slice_reduce_fusion
  363.9 0.1 reshape_squeeze.19
  363.9 0.1 reshape_squeeze.18
  364.0 0.1 reshape_squeeze.17
  364.1 0.1 reshape_squeeze.16
  364.1 0.7 dynamic_update_slice.11
  364.9 0.1 concatenate.15
  365.0 0.7 copy.48
  365.6 107.5 %reduce_all.1 = (bf16[128,2048]{1,0:T(8,128)(2,1)}, bf16[8,64,768]{2,1,0:T(8,128)(2,1)}, bf16[8,64,1024]{2,1,0:T(8,128)(2,1)}, f32[8,128]{1,0:T(8,128)}) custom-call(bf16[1024,2048]{1,0:T(8,128)(2,1)} %get-tuple-element.55.back, bf16[2048,2048]{1,0:T(8,128)(2,1)} %get-tuple-element.56.hidden_attn, bf16[2048,2048]{1,0:T(8,128)(2,1)} %get-tuple-element.57.hidden_mlp, ...), custom_call_target="tpu_custom_call" | custom-call | tf_op jit(solution)/shard_map/reduce_all/pallas_call | solution.py:1873
  473.2 1.5 fusion.4
  474.6 1.2 slice_bitcast_fusion.3
  475.8 1.2 slice_bitcast_fusion.1
  477.1 1.2 copy-done.2
  478.3 1.2 copy-done.4
  479.5 1.1 copy-done.5
  480.7 1.0 copy-done.6
  481.7 1.0 copy-done.7
  482.8 4.5 finish_part.1
  487.2 0.5 copy.55
  (27 shorter events, 0.1 us)
Async XLA Ops:
  7.2 469.9 %reduce-scatter.2.cloned.1.call-start = ((), (), s32[]{:S(2)}) async-start(), calls=%async_computation.1 | async-start | bytes 9437184 | tf_op jit(solution)/shard_map/reduce_scatter | solution.py:2051
  223.1 1.2 copy-start.1
  365.6 111.4 %copy-start = (bf16[2,1,128,2048]{3,2,1,0:T(8,128)(2,1)S(1)}, bf16[2,1,128,2048]{3,2,1,0:T(8,128)(2,1)}, u32[]{:S(2)}) copy-start(bf16[2,1,128,2048]{3,2,1,0:T(8,128)(2,1)} %param.15) | copy-start | bytes 3145732
  365.6 111.4 %copy-start.3 = (bf16[256,2048]{1,0:T(8,128)(2,1)S(1)}, bf16[256,2048]{1,0:T(8,128)(2,1)}, u32[]{:S(2)}) copy-start(bf16[256,2048]{1,0:T(8,128)(2,1)} %get-tuple-element.65.shrink_rows) | copy-start | bytes 3145732
  365.6 111.4 %copy-start.8 = (bf16[64,2048]{1,0:T(8,128)(2,1)S(1)}, bf16[64,2048]{1,0:T(8,128)(2,1)}, u32[]{:S(2)}) copy-start(bf16[64,2048]{1,0:T(8,128)(2,1)} %get-tuple-element.66.dense_rows) | copy-start | bytes 786436
  474.6 13.1 %copy-start.9 = (f32[64]{0:T(128)}, f32[64]{0:T(128)S(1)}, u32[]{:S(2)}) copy-start(f32[64]{0:T(128)S(1)} %get-tuple-element.166) | copy-start | bytes 772
  477.1 1.2 copy-start.2
  478.3 1.2 copy-start.4
  479.5 1.1 copy-start.5
  480.7 1.0 copy-start.6
  481.7 1.0 copy-start.7
Sparse Core Ops, SparseCore 0:
  223.2 105.6 reduce-scatter.1

commit v6 on v5

--- a/solution.py
+++ b/solution.py
@@ -846,8 +846,17 @@
     slopes,
     partial,
     g_all,
+    first_out,
     head_rows,
     acts,
+    board,
+    out_core,
+    out_chain,
+    core_send,
+    core_recv,
+    chain_send,
+    chain_recv,
+    store_sem,
     *g_sems,
 ):
     step = pl.program_id(0)
@@ -856,11 +865,49 @@
     c = lax.axis_index("ctx")
     g_start, g_hop, g_finish = chain_gather(own_g, g_all, g_sems, d, c, levels)
 
+    core = lax.rem(c, 2)
+    span = board.shape[2]
+
+    def own_block(level):
+        return board.at[level, core]
+
+    def core_copy(level):
+        return remote(
+            board.at[level, 1 - core],
+            out_core.at[level],
+            core_send.at[level],
+            core_recv.at[level],
+            d,
+            c + 1 - 2 * core,
+        )
+
+    chain_open, chain_round, chain_end, chain_finish = chain_reduce(
+        own_block, out_chain, (chain_send, chain_recv), d, c, levels
+    )
+
+    def out_store(level):
+        return pltpu.make_async_copy(own_block(level), first_out, store_sem.at[0])
+
     @pl.when(step == 0)
     def _():
         greet_line(d, c, levels)
         for m in range(micro):
             g_start(m)
+
+    for place, level in enumerate(outside_in(levels)):
+        @pl.when(step == tiles + 1 + place)
+        def _(level=level):
+            core_copy(level).start()
+
+        @pl.when(step == tiles + 2 + place)
+        def _(level=level):
+            core_copy(level).wait_recv()
+            add_into(own_block(level), (own_block(level), out_core.at[level]), span)
+            chain_open(level)
+
+    @pl.when(step == 12)
+    def _():
+        chain_round(1)
 
     last = 4 * tiles - 1
     for at, hop, m in ((4, 0, 0), (7, 0, 1), (11, 1, 0), (14, 1, 1)):
@@ -871,6 +918,7 @@
     seq = step // (2 * tiles)
     phase = lax.rem(step, 2 * tiles) // tiles
     tile = lax.rem(step, tiles)
+    tile = jnp.where(phase == 0, tile, jnp.where(lax.rem(tile, 2) == 0, tiles - 1 - tile // 2, tile // 2))
     rows = pl.ds(pl.multiple_of(tile * TILE, TILE), TILE)
     n_expand = panels.shape[0] - 3
     scale = 1.0 / math.sqrt(HEAD)
@@ -882,16 +930,19 @@
         normal = centered * lax.rsqrt(jnp.mean(centered * centered, axis=1, keepdims=True) + 1e-05)
         hidden_attn[...] = (normal * gains[0:1, :] + gains[1:2, :]).astype(jnp.bfloat16)
         hidden_mlp[...] = (normal * gains[2:3, :] + gains[3:4, :]).astype(jnp.bfloat16)
+        wide = jnp.concatenate([panels[part] for part in range(3)], axis=1)
+        all_joined = dot_nn(hidden_attn[...], wide) + qkv_shift[...]
         for part in range(3):
-            joined = dot_nn(hidden_attn[...], panels[part]) + qkv_shift[:, part * HEAD : (part + 1) * HEAD]
+            joined = all_joined[:, part * HEAD : (part + 1) * HEAD]
             if part < 2:
                 joined = turn(joined, cos[rows, :], sin[rows, :])
             joined = joined.astype(jnp.bfloat16)
             heads[part] = joined
             head_rows[part, rows, :] = joined
-        for part in range(n_expand):
-            columns = slice(part * HEAD, (part + 1) * HEAD)
-            expanded = dot_nn(hidden_mlp[...], panels[3 + part]) + expand_shift[:, columns]
+        for part in range(0, n_expand, 2):
+            columns = slice(part * HEAD, (part + 2) * HEAD)
+            wide = jnp.concatenate([panels[3 + part], panels[4 + part]], axis=1)
+            expanded = dot_nn(hidden_mlp[...], wide) + expand_shift[:, columns]
             cdf = 0.5 * (1.0 + lax.erf(expanded * (1.0 / math.sqrt(2.0))))
             acts[rows, columns] = (expanded * cdf).astype(jnp.bfloat16)
             bell = jnp.exp(-0.5 * expanded * expanded) * (1.0 / math.sqrt(2.0 * math.pi))
@@ -910,17 +961,31 @@
         features[:, :HEAD] = dot_nn(low_probs, head_rows[2]).astype(jnp.bfloat16)
         features[:, HEAD:] = acts[rows, :]
         width = out_w.shape[1]
-        for start in range(0, width, 512):
-            columns = slice(start, start + 512)
-            partial[:, columns] = dot_nn(features[...], out_w[:, columns]).astype(jnp.bfloat16)
+        for start in range(0, width, 1024):
+            columns = slice(start, start + 1024)
+            value = dot_nn(features[...], out_w[:, columns]).astype(jnp.bfloat16)
+
+            @pl.when(seq == 0)
+            def _(columns=columns, value=value):
+                for parity in range(2):
+                    board[tile, parity, :, columns] = value[parity * span : (parity + 1) * span]
+
+            @pl.when(seq > 0)
+            def _(columns=columns, value=value):
+                partial[:, columns] = value
 
     @pl.when(step == last)
     def _():
+        chain_round(2)
         for m in range(micro):
             for hop in range(2, levels - 1):
                 g_hop(hop, m)
+        chain_end(out_store)
         for m in range(micro):
             g_finish(m)
+        for level in range(levels):
+            core_copy(level).wait_send()
+        chain_finish(out_store)
 
 
 def whole_spec(array):
@@ -934,6 +999,8 @@
     tiles = length // TILE
     steps = 2 * tokens // TILE
     hidden = expand_shift.shape[1]
+    span = own_g.shape[1]
+    dma = pltpu.SemaphoreType.DMA
 
     def early(step):
         seq, at = step // (2 * tiles), lax.rem(step, 2 * tiles)
@@ -941,7 +1008,11 @@
 
     def late(step):
         seq, at = step // (2 * tiles), lax.rem(step, 2 * tiles)
-        return seq * tiles + jnp.maximum(at - tiles, 0)
+        place = jnp.maximum(at - tiles, 0)
+        return seq * tiles + jnp.where(lax.rem(place, 2) == 0, tiles - 1 - place // 2, place // 2)
+
+    def last_only(step):
+        return jnp.where(step < 2 * tiles, tiles - 1, late(step) - tiles)
 
     kind = jnp.bfloat16
     return pl.pallas_call(
@@ -954,8 +1025,9 @@
             jax.ShapeDtypeStruct((tokens // length, length, length), kind),
             jax.ShapeDtypeStruct((tokens, HEAD + hidden), kind),
             jax.ShapeDtypeStruct((tokens, hidden), kind),
-            jax.ShapeDtypeStruct((tokens, width), kind),
+            jax.ShapeDtypeStruct((length, width), kind),
             jax.ShapeDtypeStruct((tokens // length, length, width), kind),
+            jax.ShapeDtypeStruct((span, width), kind),
         ),
         in_specs=[
             pl.BlockSpec(memory_space=pltpu.SMEM),
@@ -976,16 +1048,25 @@
             pl.BlockSpec((1, TILE, length), lambda step: (late(step) // tiles, lax.rem(late(step), tiles), 0)),
             pl.BlockSpec((TILE, HEAD + hidden), lambda step: (late(step), 0)),
             pl.BlockSpec((TILE, hidden), lambda step: (early(step), 0)),
-            pl.BlockSpec((TILE, width), lambda step: (late(step), 0)),
+            pl.BlockSpec((TILE, width), lambda step: (last_only(step), 0)),
+            pl.BlockSpec(memory_space=pl.ANY),
             pl.BlockSpec(memory_space=pl.ANY),
         ),
         scratch_shapes=[
             pltpu.VMEM((3, length, HEAD), kind),
             pltpu.VMEM((length, hidden), kind),
+            pltpu.VMEM((levels, 2, span, width), kind),
+            pltpu.VMEM((levels, span, width), kind),
+            pltpu.VMEM((2, levels - 1, span, width), kind),
+            dma((levels,)),
+            dma((levels,)),
+            dma((2, levels)),
+            dma((2, levels)),
+            dma((1,)),
             *chain_scratch(levels, tokens // length),
         ],
         compiler_params=pltpu.CompilerParams(
-            collective_id=3, has_side_effects=True, vmem_limit_bytes=56 * 1024 * 1024
+            collective_id=3, has_side_effects=True, vmem_limit_bytes=60 * 1024 * 1024
         ),
         cost_estimate=pl.CostEstimate(
             flops=2 * tokens * width * (2 * hidden + 4 * HEAD) + 4 * tokens * length * HEAD,
@@ -1436,12 +1517,10 @@
 
     @pl.when(phase == 1)
     def _():
-        for part in range(n_expand):
-            columns = slice(part * HEAD, (part + 1) * HEAD)
-            grad = dot_nt(g[...], out_w[(part + 1) * HEAD : (part + 2) * HEAD, :])
-            grad = (grad * slopes[:, columns].astype(jnp.float32)).astype(jnp.bfloat16)
-            grad_expanded[:, columns] = grad
-            expand_sums[:, columns] += jnp.sum(grad.astype(jnp.float32), axis=0, keepdims=True)
+        grad = dot_nt(g[...], out_w[HEAD:, :])
+        grad = (grad * slopes[...].astype(jnp.float32)).astype(jnp.bfloat16)
+        grad_expanded[...] = grad
+        expand_sums[...] += jnp.sum(grad.astype(jnp.float32), axis=0, keepdims=True)
         cos_rows, sin_rows = cos[rows, :], -sin[rows, :]
         parts = (
             turn(grad_queries[rows, :], cos_rows, sin_rows),
@@ -1457,15 +1536,13 @@
         mean = jnp.mean(values_in, axis=1, keepdims=True)
         centered = values_in - mean
         spread = lax.rsqrt(jnp.mean(centered * centered, axis=1, keepdims=True) + 1e-05)
-        for start in range(0, width, 512):
-            columns = slice(start, start + 512)
+        for start in range(0, width, 1024):
+            columns = slice(start, start + 1024)
             normal = (x[:, columns].astype(jnp.float32) - mean) * spread
-            total = dot_nt(grad_joined[:, :HEAD], panels[0, columns, :])
-            for part in range(1, 3):
-                total += dot_nt(grad_joined[:, part * HEAD : (part + 1) * HEAD], panels[part, columns, :])
-            other = dot_nt(grad_expanded[:, :HEAD], panels[3, columns, :])
-            for part in range(1, n_expand):
-                other += dot_nt(grad_expanded[:, part * HEAD : (part + 1) * HEAD], panels[3 + part, columns, :])
+            wide = jnp.concatenate([panels[part, columns, :] for part in range(3)], axis=1)
+            total = dot_nt(grad_joined[...], wide)
+            wide = jnp.concatenate([panels[3 + part, columns, :] for part in range(n_expand)], axis=1)
+            other = dot_nt(grad_expanded[...], wide)
             for row, value in ((0, total * normal), (1, total), (2, other * normal), (3, other)):
                 norm_sums[row : row + 1, columns] += jnp.sum(value, axis=0, keepdims=True)
             value = (total * gains[0:1, columns] + other * gains[2:3, columns]).astype(jnp.bfloat16)
@@ -1919,16 +1996,27 @@
     back_last,
     x,
     g,
-    reduced,
+    out_first,
+    out_last,
     out_shift,
+    tail,
     qkv_grad,
     expand_grad,
     shrink_grad,
     dense_grad,
     layer_output,
     input_grad,
+    *small_grads,
 ):
     ctx_size = attn_rows.shape[0]
+    at = 0
+    for target in small_grads:
+        size = target.shape[0] * target.shape[1]
+        for row in range(target.shape[0]):
+            start = at + row * target.shape[1]
+            lane = start % 128
+            target[row : row + 1, :] = tail[start // 128 : start // 128 + 1, lane : lane + target.shape[1]]
+        at += size
     for rows, target in ((attn_rows, qkv_grad), (mlp_rows, expand_grad)):
         for member in range(ctx_size):
             for part in range(rows.shape[2] // HEAD):
@@ -1936,9 +2024,9 @@
                 target[:, start : start + HEAD] = rows[member, :, part * HEAD : (part + 1) * HEAD].astype(jnp.float32)
     shrink_grad[...] = shrink_rows[...].astype(jnp.float32)
     dense_grad[...] = dense_rows[...].astype(jnp.float32)
-    for m, back in enumerate((back_first, back_last)):
+    for m, (back, out) in enumerate(((back_first, out_first), (back_last, out_last))):
         own = x[m].astype(jnp.float32)
-        layer_output[m] = (own + reduced[m].astype(jnp.float32) + out_shift[...]).astype(jnp.bfloat16)
+        layer_output[m] = (own + out[...].astype(jnp.float32) + out_shift[...]).astype(jnp.bfloat16)
         centered = own - jnp.mean(own, axis=1, keepdims=True)
         spread = lax.rsqrt(jnp.mean(centered * centered, axis=1, keepdims=True) + 1e-05)
         normal = centered * spread
@@ -1951,9 +2039,9 @@
         input_grad[m] = (g[m].astype(jnp.float32) + share).astype(jnp.bfloat16)
 
 
-def finish_call(attn_rows, mlp_rows, shrink_rows, dense_rows, back_first, back_last, x, g, reduced, out_shift):
+def finish_call(attn_rows, mlp_rows, shrink_rows, dense_rows, back_first, back_last, x, g, out_first, out_last, out_shift, tail, lengths):
     steps = 4
-    arrays = (attn_rows, mlp_rows, shrink_rows, dense_rows, back_first, back_last, x, g, reduced)
+    arrays = (attn_rows, mlp_rows, shrink_rows, dense_rows, back_first, back_last, x, g, out_first, out_last)
     micro = x.shape[0]
     ctx_size, rows, joined = attn_rows.shape
 
@@ -1970,15 +2058,19 @@
         jax.ShapeDtypeStruct(x.shape, jnp.bfloat16),
         jax.ShapeDtypeStruct(x.shape, jnp.bfloat16),
     )
+    smalls = tuple(
+        jax.ShapeDtypeStruct((max(1, length // 128), min(length, 128)), jnp.float32) for length in lengths
+    )
     return pl.pallas_call(
         finish_kernel,
         grid=(steps,),
-        out_shape=outs,
-        in_specs=[spec(array.shape) for array in arrays] + [whole_spec(out_shift)],
-        out_specs=tuple(spec(out.shape) for out in outs),
-        compiler_params=pltpu.CompilerParams(vmem_limit_bytes=40 * 1024 * 1024),
+        out_shape=outs + smalls,
+        in_specs=[spec(array.shape) for array in arrays] + [whole_spec(out_shift), whole_spec(tail)],
+        out_specs=tuple(spec(out.shape) for out in outs)
+        + tuple(pl.BlockSpec(out.shape, lambda step: (0, 0)) for out in smalls),
+        compiler_params=pltpu.CompilerParams(vmem_limit_bytes=60 * 1024 * 1024),
         name="finish_part",
-    )(*arrays, out_shift)
+    )(*arrays, out_shift, tail)
 
 
 def tensor_shards(
@@ -2034,7 +2126,7 @@
 
     gains = jnp.stack([gain_attn, shift_attn, gain_mlp, shift_mlp])
     cos, sin = turn_tables(SEQ)
-    hidden_attn, hidden_mlp, heads, probs, features, slopes, partial, g_all = forward_call(
+    hidden_attn, hidden_mlp, heads, probs, features, slopes, partial, g_all, out_first = forward_call(
         ctx_size // 2,
         prefix_len.reshape(sequences),
         x_all,
@@ -2048,9 +2140,7 @@
         sin,
     )
     g_all = g_all.reshape(tokens, width)
-    reduced = lax.psum_scatter(
-        partial.reshape(sequences, SEQ, width), "ctx", scatter_dimension=1, tiled=True
-    )
+    out_last = lax.psum_scatter(partial, "ctx", scatter_dimension=0, tiled=True)
 
     (
         grad_expanded,
@@ -2091,7 +2181,9 @@
     back_last, attn_rows, mlp_rows, tail = reduce_call(
         dp_size, ctx_size, combined, hidden_attn, hidden_mlp, grad_joined, grad_expanded, board
     )
-    qkv_grad, expand_grad, shrink_grad, dense_grad, layer_output, input_grad = finish_call(
+    share_len = width // devices
+    small_lengths = (2 * share_len, share_len, share_len, ff // devices) + (share_len,) * 4
+    qkv_grad, expand_grad, shrink_grad, dense_grad, layer_output, input_grad, *pieces = finish_call(
         attn_rows,
         mlp_rows,
         shrink_rows,
@@ -2100,18 +2192,15 @@
         back_last,
         own_x,
         own_g,
-        reduced,
+        out_first,
+        out_last,
         (dense_shift + shrink_shift)[None],
-    )
+        tail,
+        small_lengths,
+    )
+    pieces = [piece.reshape(-1) for piece in pieces]
     layer_output = layer_output.reshape(layer_input.shape)
     input_grad = input_grad.reshape(layer_input.shape)
-    tail = tail.reshape(-1)
-    share_len = width // devices
-    at = 0
-    pieces = []
-    for length in (2 * share_len, share_len, share_len, ff // devices, share_len, share_len, share_len, share_len):
-        pieces.append(tail[at : at + length])
-        at += length
     return (
         layer_output,
         input_grad,

time: 503 us -> 472 us (0.938)
  Pallas kernels: 452 us -> 429 us
  local copies, waits for them, and re-layouts: 23.9 us -> 15.6 us
    pallas_call x1, Pallas kernels: 137 us -> 99.5 us  [backward_call(): pl.pallas_call(functools.partial(backward_kernel, tiles, dp_size, ctx_siz...]
    pallas_call x1, Pallas kernels: 80.3 us -> 91.6 us  [forward_call(): pl.pallas_call(functools.partial(forward_kernel, tiles, levels), grid=(st...]
  transfers between devices with their start and end apart: 1 -> 1, of which waited for: 0 -> 0; matrix products, arithmetic and copies ran while one was open for 2% -> 1% of each run, Pallas kernels for 49% -> 45%
where the time goes in v6:
time: 472 us; the launch traced here: 464 us
  Pallas kernels  429 us (91%)
  local copies, waits for them, and re-layouts  15.6 us (3%)
  between operations  14.6 us (3%)
  other arithmetic  4.79 us (1%)
    pallas_call x1, Pallas kernels, gather_call(): pl.pallas_call(functools.partial(gather_kernel, dp_size, ctx_size), out_s...  123 us
    pallas_call x1, Pallas kernels, reduce_call(): pl.pallas_call(functools.partial(reduce_kernel, dp_size, ctx_size), out_s...  108 us
    pallas_call x1, Pallas kernels, backward_call(): pl.pallas_call(functools.partial(backward_kernel, tiles, dp_size, ctx_siz...  99.5 us
    pallas_call x1, Pallas kernels, forward_call(): pl.pallas_call(functools.partial(forward_kernel, tiles, levels), grid=(st...  91.6 us
  transfers between devices with their start and end apart: 1, of which 0 were waited for; matrix products, arithmetic and copies ran while one was open for 1% of the time, Pallas kernels for 45%

profile of v6, /device:TPU:9, one launch (start us, length us, event | category | flops | bytes accessed | tf_op | source)
XLA Modules:
  0.0 464.3 jit_solution(10224229908327055896)
XLA Ops:
  7.2 0.0 reduce-scatter.2.cloned.1.call-start
  7.2 5.4 %concatenate.12 = bf16[832]{0:T(1024)(128)(2,1)S(1)} concatenate(bf16[64]{0:T(256)(128)(2,1)} %param.26, bf16[64]{0:T(256)(128)(2,1)} %param.27, bf16[64]{0:T(256)(128)(2,1)} %param.28, bf16[64]{0:T(256)(128)(2,1)} %param.29, bf16[192]{0:T(256)(128)(2,1)} %param.19, bf16[64]{0:T(256)(128)(2,1)} %param.21, bf16[256]{0:T(256)(128)(2,1)} %param.23, bf16[64]{0:T(256)(128)(2,1)} %param.25), dimensions={0} | concatenate | bytes 3328 | tf_op jit(solution)/shard_map/concatenate | solution.py:2109
  12.7 0.6 pad_bitcast_fusion.1.packed
  13.3 122.8 %gather_all.1 = (bf16[2,1024,2048]{2,1,0:T(8,128)(2,1)}, bf16[7,2048,256]{2,1,0:T(8,128)(2,1)}, bf16[1280,2048]{1,0:T(8,128)(2,1)}, bf16[32,16,128]{2,1,0:T(8,128)(2,1)}) custom-call(bf16[2,128,2048]{2,1,0:T(8,128)(2,1)} %bitcast.43, bf16[64,6144]{1,0:T(8,128)(2,1)} %qkv.1, bf16[64,8192]{1,0:T(8,128)(2,1)} %expand.1, bf16[64,2048]{1,0:T(8,128)(2,1)} %dense.1, ...), custom_call_target="tpu_custom_call" | custom-call | tf_op jit(solution)/shard_map/gather_all/pallas_call | solution.py:760
  136.1 0.9 copy.50
  137.0 0.1 fusion.3
  137.1 0.1 pad.15.clone
  137.2 0.1 pad.12.clone
  137.3 2.0 fusion.2
  139.2 0.1 reshape.225
  139.3 0.6 dynamic-slice_convert_fusion
  139.9 0.6 constant_dynamic-slice_fusion
  140.5 0.1 convert_element_type.87
  140.6 0.1 convert_element_type.90
  140.7 0.1 convert_element_type.89
  140.8 0.1 convert_element_type.88
  140.9 0.7 maximum_convert_fusion.gains
  141.5 1.3 maximum_maximum_fusion
  142.8 91.6 %forward_part.1 = (bf16[2048,2048]{1,0:T(8,128)(2,1)}, bf16[2048,2048]{1,0:T(8,128)(2,1)}, bf16[3,2048,256]{2,1,0:T(8,128)(2,1)}, bf16[2,1024,1024]{2,1,0:T(8,12...) custom-call(s32[2]{0:T(128)} %bitcast.61, ...), custom_call_target="tpu_custom_call" | custom-call | flops 27917287424 | bytes 67108864 | tf_op jit(solution)/shard_map/forward_part/pallas_call | solution.py:1018
  234.4 0.0 copy-start
  234.4 0.0 reduce-scatter.2.cloned.1.call-update
  234.4 1.2 copy-done
  235.6 0.2 convert_reduce_fusion
  235.8 0.1 reshape.212
  235.9 0.1 convert_add_fusion
  235.9 0.7 add.32.out_shift
  236.6 99.5 %backward_part.1 = (bf16[2048,1024]{1,0:T(8,128)(2,1)}, bf16[2048,768]{1,0:T(8,128)(2,1)}, bf16[1024,2048]{1,0:T(8,128)(2,1)}, f32[8,2048]{1,0:T(8,128)}, f32[1,...) custom-call(bf16[2048,2048]{1,0:T(8,128)(2,1)} %bitcast.39, ...), custom_call_target="tpu_custom_call" | custom-call | tf_op jit(solution)/shard_map/backward_part/pallas_call | solution.py:1605
  336.1 0.7 slice.59
  336.8 0.6 slice_bitcast_fusion.1
  337.5 0.1 reshape.211
  337.5 1.1 slice_reduce_fusion
  338.6 0.1 reshape_squeeze.19
  338.7 0.1 reshape_squeeze.18
  338.8 0.1 reshape_squeeze.17
  338.8 0.1 reshape_squeeze.16
  338.9 0.7 dynamic_update_slice.11
  339.6 0.1 concatenate.15
  339.7 0.7 copy.48
  340.4 107.9 %reduce_all.1 = (bf16[128,2048]{1,0:T(8,128)(2,1)}, bf16[8,64,768]{2,1,0:T(8,128)(2,1)}, bf16[8,64,1024]{2,1,0:T(8,128)(2,1)}, f32[8,128]{1,0:T(8,128)}) custom-call(bf16[1024,2048]{1,0:T(8,128)(2,1)} %get-tuple-element.64.back, bf16[2048,2048]{1,0:T(8,128)(2,1)} %get-tuple-element.65.hidden_attn, bf16[2048,2048]{1,0:T(8,128)(2,1)} %get-tuple-element.66.hidden_mlp, ...), custom_call_target="tpu_custom_call" | custom-call | tf_op jit(solution)/shard_map/reduce_all/pallas_call | solution.py:1950
  448.3 0.0 reduce-scatter.2.cloned.1.call-done.out_last
  448.4 7.5 %finish_part.1 = (f32[64,6144]{1,0:T(8,128)}, f32[64,8192]{1,0:T(8,128)}, f32[256,2048]{1,0:T(8,128)}, f32[64,2048]{1,0:T(8,128)}, bf16[2,128,2048]{2,1,0:T(8,12...) custom-call(bf16[8,64,768]{2,1,0:T(8,128)(2,1)} %get-tuple-element.7, ...), custom_call_target="tpu_custom_call" | custom-call | tf_op jit(solution)/shard_map/finish_part/pallas_call | solution.py:2064
  455.8 1.2 copy.55
  (12 shorter events, 0.1 us)
Async XLA Ops:
  7.2 441.2 %reduce-scatter.2.cloned.1.call-start = ((), (), s32[]{:S(2)}) async-start(), calls=%async_computation.1 | async-start | bytes 4718592 | tf_op jit(solution)/shard_map/reduce_scatter | solution.py:2143
  234.4 1.2 copy-start
Sparse Core Ops, SparseCore 0:
  234.6 49.4 reduce-scatter.1

commit v7 on v6

--- a/solution.py
+++ b/solution.py
@@ -3,6 +3,7 @@
 
 import jax
 import jax.numpy as jnp
+import numpy as np
 from jax import lax
 from jax.experimental import pallas as pl
 from jax.experimental.pallas import tpu as pltpu
@@ -796,13 +797,13 @@
 
 
 def turn_tables(length):
-    freqs = jnp.exp(jnp.arange(ROT // 2, dtype=jnp.float32) * (-2.0 * math.log(10000.0) / ROT))
-    angles = jnp.arange(length, dtype=jnp.float32)[:, None] * freqs[None, :]
-    cos, sin = jnp.cos(angles), jnp.sin(angles)
-    rest = jnp.zeros((length, 128 - ROT), jnp.float32)
+    freqs = np.exp(np.arange(ROT // 2) * (-2.0 * math.log(10000.0) / ROT))
+    angles = np.arange(length)[:, None] * freqs[None, :]
+    cos, sin = np.cos(angles), np.sin(angles)
+    rest = np.zeros((length, 128 - ROT))
     return (
-        jnp.concatenate([cos, cos, rest + 1.0], axis=1),
-        jnp.concatenate([-sin, sin, rest], axis=1),
+        jnp.asarray(np.concatenate([cos, cos, rest + 1.0], axis=1), jnp.float32),
+        jnp.asarray(np.concatenate([-sin, sin, rest], axis=1), jnp.float32),
     )
 
 
@@ -2102,29 +2103,25 @@
     scale = 1.0 / math.sqrt(HEAD)
     ff = expand_weight.shape[1]
     unit = shrink_weight.shape[0]
-    lengths = tuple(
-        member.shape[0]
-        for member in (attn_gain, attn_shift, mlp_gain, mlp_shift, qkv_bias, dense_bias, expand_bias, shrink_bias)
-    )
-    packed = jnp.concatenate(
-        [attn_gain, attn_shift, mlp_gain, mlp_shift, qkv_bias, dense_bias, expand_bias, shrink_bias]
+    members = (attn_gain, attn_shift, mlp_gain, mlp_shift, qkv_bias, dense_bias, expand_bias, shrink_bias)
+    columns = max(member.shape[0] for member in members)
+    packed = sum(
+        jnp.pad(member[None], ((row, 15 - row), (0, columns - member.shape[0])))
+        for row, member in enumerate(members)
     )
     own_x = layer_input.reshape(sequences, span, width)
     own_g = out_grad.reshape(sequences, span, width)
-    count = packed.shape[0]
-    packed = jnp.pad(packed, (0, -count % 2048)).reshape(-1, 128)
     x_all, panels, out_part, small = gather_call(
         dp_size, ctx_size, own_x, qkv_weight, expand_weight, dense_weight, shrink_weight, packed
     )
     x_all = x_all.reshape(tokens, width)
-    small = unpack_small(small.reshape(devices, -1)[:, :count], lengths, devices)
-    gain_attn, shift_attn, gain_mlp, shift_mlp, qkv_shift, dense_shift, expand_shift, shrink_shift = small
-    qkv_shift = lax.dynamic_slice_in_dim(qkv_shift.reshape(3, ctx_size, HEAD), me, 1, 1).reshape(-1)
-    expand_shift = lax.dynamic_slice_in_dim(
-        expand_shift.reshape(dp_size, ctx_size, unit), me, 1, 1
-    ).reshape(-1)
-
-    gains = jnp.stack([gain_attn, shift_attn, gain_mlp, shift_mlp])
+    small = small.astype(jnp.float32)
+    gains = jnp.transpose(small[:, :4, : attn_gain.shape[0]], (1, 0, 2)).reshape(4, width)
+    qkv_shift = small[:, 4, : qkv_bias.shape[0]].reshape(3, ctx_size, HEAD)
+    qkv_shift = lax.dynamic_slice_in_dim(qkv_shift, me, 1, 1).reshape(-1)
+    expand_shift = small.reshape(dp_size, ctx_size, 16, columns)[:, :, 6, :unit]
+    expand_shift = lax.dynamic_slice_in_dim(expand_shift, me, 1, 1).reshape(-1)
+    out_shift = (small[:, 5, : dense_bias.shape[0]] + small[:, 7, : shrink_bias.shape[0]]).reshape(1, width)
     cos, sin = turn_tables(SEQ)
     hidden_attn, hidden_mlp, heads, probs, features, slopes, partial, g_all, out_first = forward_call(
         ctx_size // 2,
@@ -2194,7 +2191,7 @@
         own_g,
         out_first,
         out_last,
-        (dense_shift + shrink_shift)[None],
+        out_shift,
         tail,
         small_lengths,
     )

time: 472 us -> 466 us (0.987)
  local copies, waits for them, and re-layouts: 15.6 us -> 10.8 us
    concatenate x3 -> x0, local copies, waits for them, and re-layouts: 5.57 us -> none  [the longest x1 5.42 us: tensor_shards(): jnp.concatenate([attn_gain, attn_shift, mlp_gain, mlp_shift, qkv_bias, de...]
where the time goes in v7:
time: 466 us; the launch traced here: 459 us
  Pallas kernels  431 us (92%)
  between operations  14.6 us (3%)
  local copies, waits for them, and re-layouts  10.8 us (2%)
    pallas_call x1, Pallas kernels, gather_call(): pl.pallas_call(functools.partial(gather_kernel, dp_size, ctx_size), out_s...  125 us
    pallas_call x1, Pallas kernels, reduce_call(): pl.pallas_call(functools.partial(reduce_kernel, dp_size, ctx_size), out_s...  108 us
    pallas_call x1, Pallas kernels, backward_call(): pl.pallas_call(functools.partial(backward_kernel, tiles, dp_size, ctx_siz...  99.5 us
    pallas_call x1, Pallas kernels, forward_call(): pl.pallas_call(functools.partial(forward_kernel, tiles, levels), grid=(st...  91.6 us
  transfers between devices with their start and end apart: 1, of which 0 were waited for; matrix products, arithmetic and copies ran while one was open for 1% of the time, Pallas kernels for 45%

profile of v7, /device:TPU:9, one launch (start us, length us, event | category | flops | bytes accessed | tf_op | source)
XLA Modules:
  0.0 459.4 jit_solution(17740150148068939376)
XLA Ops:
  7.2 0.0 reduce-scatter.2.cloned.1.call-start
  7.2 0.7 broadcast_in_dim.37
  7.9 0.7 broadcast_in_dim.39
  8.5 1.4 pad_add_fusion.packed
  9.9 124.9 %gather_all.1 = (bf16[2,1024,2048]{2,1,0:T(8,128)(2,1)}, bf16[7,2048,256]{2,1,0:T(8,128)(2,1)}, bf16[1280,2048]{1,0:T(8,128)(2,1)}, bf16[32,16,256]{2,1,0:T(8,128)(2,1)}) custom-call(bf16[2,128,2048]{2,1,0:T(8,128)(2,1)} %bitcast.45, bf16[64,6144]{1,0:T(8,128)(2,1)} %qkv.1, bf16[64,8192]{1,0:T(8,128)(2,1)} %expand.1, bf16[64,2048]{1,0:T(8,128)(2,1)} %dense.1, ...), custom_call_target="tpu_custom_call" | custom-call | tf_op jit(solution)/shard_map/gather_all/pallas_call | solution.py:761
  134.8 1.0 convert_element_type.24
  135.8 0.1 slice_reduce_fusion
  136.0 0.1 reshape_squeeze.18
  136.1 0.6 constant_dynamic-slice_fusion
  136.7 0.6 constant_dynamic-slice_fusion.1
  137.3 0.7 reshape.131.gains
  138.0 91.6 %forward_part.1 = (bf16[2048,2048]{1,0:T(8,128)(2,1)}, bf16[2048,2048]{1,0:T(8,128)(2,1)}, bf16[3,2048,256]{2,1,0:T(8,128)(2,1)}, bf16[2,1024,1024]{2,1,0:T(8,12...) custom-call(s32[2]{0:T(128)} %bitcast.63, ...), custom_call_target="tpu_custom_call" | custom-call | flops 27917287424 | bytes 67108864 | tf_op jit(solution)/shard_map/forward_part/pallas_call | solution.py:1019
  229.6 0.0 copy-start
  229.6 0.0 reduce-scatter.2.cloned.1.call-update
  229.6 1.2 copy-done
  230.8 0.2 convert_reduce_fusion
  231.0 0.1 reshape.138
  231.0 0.1 fusion
  231.1 0.7 add.70.out_shift
  231.8 99.5 %backward_part.1 = (bf16[2048,1024]{1,0:T(8,128)(2,1)}, bf16[2048,768]{1,0:T(8,128)(2,1)}, bf16[1024,2048]{1,0:T(8,128)(2,1)}, f32[8,2048]{1,0:T(8,128)}, f32[1,...) custom-call(bf16[2048,2048]{1,0:T(8,128)(2,1)} %bitcast.39, ...), custom_call_target="tpu_custom_call" | custom-call | tf_op jit(solution)/shard_map/backward_part/pallas_call | solution.py:1606
  331.3 0.7 slice.38
  332.0 0.6 slice_bitcast_fusion.1
  332.6 0.1 reshape.137
  332.7 1.1 slice_reduce_fusion.1
  333.8 0.1 reshape_squeeze.23
  333.9 0.1 reshape_squeeze.22
  333.9 0.1 reshape_squeeze.21
  334.0 0.1 reshape_squeeze.20
  334.1 0.7 dynamic_update_slice.11
  334.8 0.1 concatenate.3
  334.9 0.7 copy.49
  335.6 107.9 %reduce_all.1 = (bf16[128,2048]{1,0:T(8,128)(2,1)}, bf16[8,64,768]{2,1,0:T(8,128)(2,1)}, bf16[8,64,1024]{2,1,0:T(8,128)(2,1)}, f32[8,128]{1,0:T(8,128)}) custom-call(bf16[1024,2048]{1,0:T(8,128)(2,1)} %get-tuple-element.64.back, bf16[2048,2048]{1,0:T(8,128)(2,1)} %get-tuple-element.65.hidden_attn, bf16[2048,2048]{1,0:T(8,128)(2,1)} %get-tuple-element.66.hidden_mlp, ...), custom_call_target="tpu_custom_call" | custom-call | tf_op jit(solution)/shard_map/reduce_all/pallas_call | solution.py:1951
  443.5 0.0 reduce-scatter.2.cloned.1.call-done.out_last
  443.5 7.5 %finish_part.1 = (f32[64,6144]{1,0:T(8,128)}, f32[64,8192]{1,0:T(8,128)}, f32[256,2048]{1,0:T(8,128)}, f32[64,2048]{1,0:T(8,128)}, bf16[2,128,2048]{2,1,0:T(8,12...) custom-call(bf16[8,64,768]{2,1,0:T(8,128)(2,1)} %get-tuple-element.7, ...), custom_call_target="tpu_custom_call" | custom-call | tf_op jit(solution)/shard_map/finish_part/pallas_call | solution.py:2065
  451.0 1.2 copy.54
  (10 shorter events, 0.1 us)
Async XLA Ops:
  7.2 436.3 %reduce-scatter.2.cloned.1.call-start = ((), (), s32[]{:S(2)}) async-start(), calls=%async_computation.1 | async-start | bytes 4718592 | tf_op jit(solution)/shard_map/reduce_scatter | solution.py:2140
  229.6 1.2 copy-start
Sparse Core Ops, SparseCore 0:
  229.7 49.4 reduce-scatter.1

commit v8 on v7

--- a/solution.py
+++ b/solution.py
@@ -832,8 +832,8 @@
     prefix,
     x,
     own_g,
-    panels,
-    out_w,
+    panels_in,
+    out_w_in,
     gains,
     qkv_shift,
     expand_shift,
@@ -848,6 +848,9 @@
     partial,
     g_all,
     first_out,
+    panels,
+    out_w,
+    weight_sem,
     head_rows,
     acts,
     board,
@@ -889,11 +892,21 @@
     def out_store(level):
         return pltpu.make_async_copy(own_block(level), first_out, store_sem.at[0])
 
+    panels_copy = pltpu.make_async_copy(panels_in, panels, weight_sem.at[0])
+    out_w_copy = pltpu.make_async_copy(out_w_in, out_w, weight_sem.at[1])
+
     @pl.when(step == 0)
     def _():
         greet_line(d, c, levels)
         for m in range(micro):
             g_start(m)
+        panels_copy.start()
+        out_w_copy.start()
+        panels_copy.wait()
+
+    @pl.when(step == tiles)
+    def _():
+        out_w_copy.wait()
 
     for place, level in enumerate(outside_in(levels)):
         @pl.when(step == tiles + 1 + place)
@@ -1034,8 +1047,8 @@
             pl.BlockSpec(memory_space=pltpu.SMEM),
             pl.BlockSpec((TILE, width), lambda step: (early(step), 0)),
             pl.BlockSpec(memory_space=pl.ANY),
-            whole_spec(panels),
-            whole_spec(out_w),
+            pl.BlockSpec(memory_space=pl.ANY),
+            pl.BlockSpec(memory_space=pl.ANY),
             whole_spec(gains),
             whole_spec(qkv_shift),
             whole_spec(expand_shift),
@@ -1054,6 +1067,9 @@
             pl.BlockSpec(memory_space=pl.ANY),
         ),
         scratch_shapes=[
+            pltpu.VMEM(panels.shape, kind),
+            pltpu.VMEM(out_w.shape, kind),
+            dma((2,)),
             pltpu.VMEM((3, length, HEAD), kind),
             pltpu.VMEM((length, hidden), kind),
             pltpu.VMEM((levels, 2, span, width), kind),
@@ -1200,8 +1216,8 @@
     ctx_size,
     g,
     x,
-    panels,
-    out_w,
+    panels_in,
+    out_w_in,
     gains,
     cos,
     sin,
@@ -1219,6 +1235,9 @@
     back_out,
     shrink_out,
     dense_out,
+    panels,
+    out_w,
+    weight_sem,
     grad_queries,
     grad_keys,
     grad_values,
@@ -1426,11 +1445,17 @@
     def at(when):
         return pl.when(step == when)
 
+    panels_copy = pltpu.make_async_copy(panels_in, panels, weight_sem.at[0])
+    out_w_copy = pltpu.make_async_copy(out_w_in, out_w, weight_sem.at[1])
+
     @at(0)
     def _():
+        out_w_copy.start()
         greet_all(d, c, dp_size, ctx_size)
         left_copy(0).start()
         right_copy.start()
+        panels_copy.start()
+        out_w_copy.wait()
         norm_sums[...] = jnp.zeros_like(norm_sums)
         joined_sums[...] = jnp.zeros_like(joined_sums)
         expand_sums[...] = jnp.zeros_like(expand_sums)
@@ -1456,6 +1481,7 @@
 
     @at(4)
     def _():
+        panels_copy.wait()
         compute(4)
 
     for place, level in enumerate(outside_in(levels)):
@@ -1620,8 +1646,8 @@
         in_specs=[
             pl.BlockSpec((TILE, width), lambda step: (both(step), 0)),
             pl.BlockSpec((TILE, width), lambda step: (second(step), 0)),
-            whole_spec(panels),
-            whole_spec(out_w),
+            pl.BlockSpec(memory_space=pl.ANY),
+            pl.BlockSpec(memory_space=pl.ANY),
             whole_spec(gains),
             whole_spec(cos),
             whole_spec(sin),
@@ -1643,6 +1669,9 @@
             anywhere,
         ),
         scratch_shapes=[
+            vmem(panels.shape, kind),
+            vmem(out_w.shape, kind),
+            dma((2,)),
             vmem((length, HEAD), jnp.float32),
             vmem((length, HEAD), jnp.float32),
             vmem((length, HEAD), jnp.float32),

time: 466 us -> 458 us (0.983)
  Pallas kernels: 431 us -> 424 us
where the time goes in v8:
time: 458 us; the launch traced here: 452 us
  Pallas kernels  424 us (93%)
  between operations  14.6 us (3%)
  local copies, waits for them, and re-layouts  10.8 us (2%)
    pallas_call x1, Pallas kernels, gather_call(): pl.pallas_call(functools.partial(gather_kernel, dp_size, ctx_size), out_s...  125 us
    pallas_call x1, Pallas kernels, reduce_call(): pl.pallas_call(functools.partial(reduce_kernel, dp_size, ctx_size), out_s...  108 us
    pallas_call x1, Pallas kernels, backward_call(): pl.pallas_call(functools.partial(backward_kernel, tiles, dp_size, ctx_siz...  96 us
    pallas_call x1, Pallas kernels, forward_call(): pl.pallas_call(functools.partial(forward_kernel, tiles, levels), grid=(st...  87.9 us
  transfers between devices with their start and end apart: 1, of which 0 were waited for; matrix products, arithmetic and copies ran while one was open for 1% of the time, Pallas kernels for 45%

profile of v8, /device:TPU:9, one launch (start us, length us, event | category | flops | bytes accessed | tf_op | source)
XLA Modules:
  0.0 452.0 jit_solution(9302095033067643614)
XLA Ops:
  7.2 0.0 reduce-scatter.2.cloned.1.call-start
  7.2 0.7 broadcast_in_dim.37
  7.9 0.7 broadcast_in_dim.39
  8.5 1.4 pad_add_fusion.packed
  9.9 124.9 %gather_all.1 = (bf16[2,1024,2048]{2,1,0:T(8,128)(2,1)}, bf16[7,2048,256]{2,1,0:T(8,128)(2,1)}, bf16[1280,2048]{1,0:T(8,128)(2,1)}, bf16[32,16,256]{2,1,0:T(8,128)(2,1)}) custom-call(bf16[2,128,2048]{2,1,0:T(8,128)(2,1)} %bitcast.45, bf16[64,6144]{1,0:T(8,128)(2,1)} %qkv.1, bf16[64,8192]{1,0:T(8,128)(2,1)} %expand.1, bf16[64,2048]{1,0:T(8,128)(2,1)} %dense.1, ...), custom_call_target="tpu_custom_call" | custom-call | tf_op jit(solution)/shard_map/gather_all/pallas_call | solution.py:761
  134.8 1.0 convert_element_type.24
  135.8 0.1 slice_reduce_fusion
  136.0 0.1 reshape_squeeze.18
  136.1 0.6 constant_dynamic-slice_fusion
  136.7 0.6 constant_dynamic-slice_fusion.1
  137.3 0.7 reshape.131.gains
  138.0 87.9 %forward_part.1 = (bf16[2048,2048]{1,0:T(8,128)(2,1)}, bf16[2048,2048]{1,0:T(8,128)(2,1)}, bf16[3,2048,256]{2,1,0:T(8,128)(2,1)}, bf16[2,1024,1024]{2,1,0:T(8,12...) custom-call(s32[2]{0:T(128)} %bitcast.63, ...), custom_call_target="tpu_custom_call" | custom-call | flops 27917287424 | bytes 67108864 | tf_op jit(solution)/shard_map/forward_part/pallas_call | solution.py:1032
  225.9 0.0 copy-start
  225.9 0.0 reduce-scatter.2.cloned.1.call-update
  225.9 1.2 copy-done
  227.1 0.2 convert_reduce_fusion
  227.3 0.1 reshape.138
  227.4 0.1 fusion
  227.4 0.7 add.70.out_shift
  228.1 96.0 %backward_part.1 = (bf16[2048,1024]{1,0:T(8,128)(2,1)}, bf16[2048,768]{1,0:T(8,128)(2,1)}, bf16[1024,2048]{1,0:T(8,128)(2,1)}, f32[8,2048]{1,0:T(8,128)}, f32[1,...) custom-call(bf16[2048,2048]{1,0:T(8,128)(2,1)} %bitcast.39, ...), custom_call_target="tpu_custom_call" | custom-call | tf_op jit(solution)/shard_map/backward_part/pallas_call | solution.py:1632
  324.1 0.7 slice.38
  324.8 0.6 slice_bitcast_fusion.1
  325.5 0.1 reshape.137
  325.5 1.1 slice_reduce_fusion.1
  326.6 0.1 reshape_squeeze.23
  326.7 0.1 reshape_squeeze.22
  326.7 0.1 reshape_squeeze.21
  326.8 0.1 reshape_squeeze.20
  326.9 0.7 dynamic_update_slice.11
  327.6 0.1 concatenate.3
  327.7 0.7 copy.49
  328.4 107.6 %reduce_all.1 = (bf16[128,2048]{1,0:T(8,128)(2,1)}, bf16[8,64,768]{2,1,0:T(8,128)(2,1)}, bf16[8,64,1024]{2,1,0:T(8,128)(2,1)}, f32[8,128]{1,0:T(8,128)}) custom-call(bf16[1024,2048]{1,0:T(8,128)(2,1)} %get-tuple-element.64.back, bf16[2048,2048]{1,0:T(8,128)(2,1)} %get-tuple-element.65.hidden_attn, bf16[2048,2048]{1,0:T(8,128)(2,1)} %get-tuple-element.66.hidden_mlp, ...), custom_call_target="tpu_custom_call" | custom-call | tf_op jit(solution)/shard_map/reduce_all/pallas_call | solution.py:1980
  436.0 0.0 reduce-scatter.2.cloned.1.call-done.out_last
  436.1 7.5 %finish_part.1 = (f32[64,6144]{1,0:T(8,128)}, f32[64,8192]{1,0:T(8,128)}, f32[256,2048]{1,0:T(8,128)}, f32[64,2048]{1,0:T(8,128)}, bf16[2,128,2048]{2,1,0:T(8,12...) custom-call(bf16[8,64,768]{2,1,0:T(8,128)(2,1)} %get-tuple-element.7, ...), custom_call_target="tpu_custom_call" | custom-call | tf_op jit(solution)/shard_map/finish_part/pallas_call | solution.py:2094
  443.5 1.2 copy.54
  (10 shorter events, 0.1 us)
Async XLA Ops:
  7.2 428.9 %reduce-scatter.2.cloned.1.call-start = ((), (), s32[]{:S(2)}) async-start(), calls=%async_computation.1 | async-start | bytes 4718592 | tf_op jit(solution)/shard_map/reduce_scatter | solution.py:2169
  225.9 1.2 copy-start
Sparse Core Ops, SparseCore 0:
  226.1 49.4 reduce-scatter.1

commit v9 on v8

--- a/solution.py
+++ b/solution.py
@@ -1794,7 +1794,7 @@
         owner, way = tile_of[index]
         columns = pl.ds(pl.multiple_of(owner * group_rows + way * half, half), half)
         source = (hidden_attn, hidden_mlp)[kind]
-        return pltpu.make_async_copy(source.at[:, columns], left.at[place % 2], left_sem.at[place % 2])
+        return pltpu.make_async_copy(source.at[:, columns], left.at[place % 4], left_sem.at[place % 4])
 
     right_copies = (
         pltpu.make_async_copy(grad_joined, right_attn, right_sem.at[0]),
@@ -1803,13 +1803,13 @@
 
     def compute(kind, index):
         place = sequence.index((kind, index))
-        if place + 1 < len(sequence):
-            left_copy(place + 1).start()
+        if place + 3 < len(sequence):
+            left_copy(place + 3).start()
         left_copy(place).wait()
         if index == 0:
             right_copies[kind].wait()
         target, right = ((attn_own, right_attn), (mlp_own, right_mlp))[kind]
-        target[index] = dot_tn(left[place % 2], right[...]).astype(jnp.bfloat16)
+        target[index] = dot_tn(left[place % 4], right[...]).astype(jnp.bfloat16)
 
     def square(own, recv, last, sems):
         return square_sum(
@@ -1894,7 +1894,8 @@
         return pltpu.make_async_copy(back_own.at[level], back_out, store_sem.at[2])
 
     right_copies[0].start()
-    left_copy(0).start()
+    for place in range(3):
+        left_copy(place).start()
     for level in order:
         core_copy(level).start()
         back_load(level).start()
@@ -1986,7 +1987,7 @@
             vmem((levels, span, width), kind),
             vmem((levels, span, width), kind),
             vmem((2, levels - 1, span, width), kind),
-            vmem((2, tokens, HEAD), kind),
+            vmem((4, tokens, HEAD), kind),
             vmem((tokens, joined), kind),
             vmem((tokens, hidden), kind),
             vmem((8, half, joined), kind),
@@ -1997,7 +1998,7 @@
             vmem((2, half, hidden), kind),
             vmem((devices,) + board.shape[1:], jnp.float32),
             dma((levels + 1,)),
-            dma((2,)),
+            dma((4,)),
             dma((2,)),
             dma((levels,)),
             dma((levels,)),

time: 458 us -> 458 us (level)
  no operation moved by 1% of the time
where the time goes in v9:
time: 458 us; the launch traced here: 452 us
  Pallas kernels  423 us (92%)
  between operations  14.6 us (3%)
  local copies, waits for them, and re-layouts  10.8 us (2%)
    pallas_call x1, Pallas kernels, gather_call(): pl.pallas_call(functools.partial(gather_kernel, dp_size, ctx_size), out_s...  125 us
    pallas_call x1, Pallas kernels, reduce_call(): pl.pallas_call(functools.partial(reduce_kernel, dp_size, ctx_size), out_s...  107 us
    pallas_call x1, Pallas kernels, backward_call(): pl.pallas_call(functools.partial(backward_kernel, tiles, dp_size, ctx_siz...  96 us
    pallas_call x1, Pallas kernels, forward_call(): pl.pallas_call(functools.partial(forward_kernel, tiles, levels), grid=(st...  87.9 us
  transfers between devices with their start and end apart: 1, of which 0 were waited for; matrix products, arithmetic and copies ran while one was open for 1% of the time, Pallas kernels for 45%

profile of v9, /device:TPU:9, one launch (start us, length us, event | category | flops | bytes accessed | tf_op | source)
XLA Modules:
  0.0 451.5 jit_solution(1199822490369131799)
XLA Ops:
  7.2 0.0 reduce-scatter.2.cloned.1.call-start
  7.2 0.7 broadcast_in_dim.37
  7.9 0.7 broadcast_in_dim.39
  8.5 1.4 pad_add_fusion.packed
  9.9 124.9 %gather_all.1 = (bf16[2,1024,2048]{2,1,0:T(8,128)(2,1)}, bf16[7,2048,256]{2,1,0:T(8,128)(2,1)}, bf16[1280,2048]{1,0:T(8,128)(2,1)}, bf16[32,16,256]{2,1,0:T(8,128)(2,1)}) custom-call(bf16[2,128,2048]{2,1,0:T(8,128)(2,1)} %bitcast.45, bf16[64,6144]{1,0:T(8,128)(2,1)} %qkv.1, bf16[64,8192]{1,0:T(8,128)(2,1)} %expand.1, bf16[64,2048]{1,0:T(8,128)(2,1)} %dense.1, ...), custom_call_target="tpu_custom_call" | custom-call | tf_op jit(solution)/shard_map/gather_all/pallas_call | solution.py:761
  134.8 1.0 convert_element_type.24
  135.8 0.1 slice_reduce_fusion
  136.0 0.1 reshape_squeeze.18
  136.1 0.6 constant_dynamic-slice_fusion
  136.7 0.6 constant_dynamic-slice_fusion.1
  137.3 0.7 reshape.131.gains
  138.0 87.9 %forward_part.1 = (bf16[2048,2048]{1,0:T(8,128)(2,1)}, bf16[2048,2048]{1,0:T(8,128)(2,1)}, bf16[3,2048,256]{2,1,0:T(8,128)(2,1)}, bf16[2,1024,1024]{2,1,0:T(8,12...) custom-call(s32[2]{0:T(128)} %bitcast.63, ...), custom_call_target="tpu_custom_call" | custom-call | flops 27917287424 | bytes 67108864 | tf_op jit(solution)/shard_map/forward_part/pallas_call | solution.py:1032
  225.9 0.0 copy-start
  225.9 0.0 reduce-scatter.2.cloned.1.call-update
  225.9 1.2 copy-done
  227.1 0.2 convert_reduce_fusion
  227.3 0.1 reshape.138
  227.4 0.1 fusion
  227.4 0.7 add.70.out_shift
  228.1 96.0 %backward_part.1 = (bf16[2048,1024]{1,0:T(8,128)(2,1)}, bf16[2048,768]{1,0:T(8,128)(2,1)}, bf16[1024,2048]{1,0:T(8,128)(2,1)}, f32[8,2048]{1,0:T(8,128)}, f32[1,...) custom-call(bf16[2048,2048]{1,0:T(8,128)(2,1)} %bitcast.39, ...), custom_call_target="tpu_custom_call" | custom-call | tf_op jit(solution)/shard_map/backward_part/pallas_call | solution.py:1632
  324.1 0.7 slice.38
  324.8 0.6 slice_bitcast_fusion.1
  325.5 0.1 reshape.137
  325.5 1.1 slice_reduce_fusion.1
  326.6 0.1 reshape_squeeze.23
  326.7 0.1 reshape_squeeze.22
  326.7 0.1 reshape_squeeze.21
  326.8 0.1 reshape_squeeze.20
  326.9 0.7 dynamic_update_slice.11
  327.6 0.1 concatenate.3
  327.7 0.7 copy.49
  328.4 107.2 %reduce_all.1 = (bf16[128,2048]{1,0:T(8,128)(2,1)}, bf16[8,64,768]{2,1,0:T(8,128)(2,1)}, bf16[8,64,1024]{2,1,0:T(8,128)(2,1)}, f32[8,128]{1,0:T(8,128)}) custom-call(bf16[1024,2048]{1,0:T(8,128)(2,1)} %get-tuple-element.64.back, bf16[2048,2048]{1,0:T(8,128)(2,1)} %get-tuple-element.65.hidden_attn, bf16[2048,2048]{1,0:T(8,128)(2,1)} %get-tuple-element.66.hidden_mlp, ...), custom_call_target="tpu_custom_call" | custom-call | tf_op jit(solution)/shard_map/reduce_all/pallas_call | solution.py:1981
  435.6 0.0 reduce-scatter.2.cloned.1.call-done.out_last
  435.6 7.5 %finish_part.1 = (f32[64,6144]{1,0:T(8,128)}, f32[64,8192]{1,0:T(8,128)}, f32[256,2048]{1,0:T(8,128)}, f32[64,2048]{1,0:T(8,128)}, bf16[2,128,2048]{2,1,0:T(8,12...) custom-call(bf16[8,64,768]{2,1,0:T(8,128)(2,1)} %get-tuple-element.7, ...), custom_call_target="tpu_custom_call" | custom-call | tf_op jit(solution)/shard_map/finish_part/pallas_call | solution.py:2095
  443.1 1.2 copy.54
  (10 shorter events, 0.1 us)
Async XLA Ops:
  7.2 428.4 %reduce-scatter.2.cloned.1.call-start = ((), (), s32[]{:S(2)}) async-start(), calls=%async_computation.1 | async-start | bytes 4718592 | tf_op jit(solution)/shard_map/reduce_scatter | solution.py:2170
  225.9 1.2 copy-start
Sparse Core Ops, SparseCore 0:
  226.1 49.4 reduce-scatter.1
